TPU v7x, 32 devices: a whole 2x2x4 slice. The times are simulated.
32 devices in a mesh: seq: 16 (over z, y, x), head: 2 (over core).
Axes of the slice: x: 2, y: 2, z: 4, core: 2. Of those that a mesh axis runs over, the one named last changes fastest.
Arguments:
- block_input: bfloat16 [4, 2048, 2560], P(None, 'seq'), may hold values from -6 to 6
- norm_gain: float32 [2560], replicated, may hold values from 0.1 to 1.9
- conv_weight: float32 [4, 2560], P(None, 'head'), may hold values from -3 to 3
- conv_bias: float32 [2560], P('head'), may hold values from -3 to 3
- recur_weight: bfloat16 [10, 256, 256], P('head'), may hold values from -0.375 to 0.375
- recur_bias: float32 [2560], P('head'), may hold values from -4 to 4
- input_weight: bfloat16 [10, 256, 256], P('head'), may hold values from -0.375 to 0.375
- input_bias: float32 [2560], P('head'), may hold values from -4 to 4
- decay_param: float32 [2560], P('head'), may hold values from 5 to 12, as said below
- mlp_gain: float32 [2560], replicated, may hold values from 0.1 to 1.9
- w_gate: bfloat16 [2560, 7680], P('seq', 'head'), may hold values from -0.125 to 0.125
- w_up: bfloat16 [2560, 7680], P('seq', 'head'), may hold values from -0.125 to 0.125
- w_down: bfloat16 [2560, 7680], P('seq', 'head'), may hold values from -0.0625 to 0.0625
- out_grad: bfloat16 [4, 2048, 2560], P(None, 'seq'), may hold values from -6 to 6
Outputs:
- block_output: bfloat16 [4, 2048, 2560], P(None, 'seq')
- input_grad: float32 [4, 2048, 2560], P(None, 'seq')
- norm_gain_grad: float32 [2560], replicated
- conv_weight_grad: float32 [4, 2560], P(None, 'head')
- conv_bias_grad: float32 [2560], P('head')
- recur_weight_grad: float32 [10, 256, 256], P('head')
- recur_bias_grad: float32 [2560], P('head')
- input_weight_grad: float32 [10, 256, 256], P('head')
- input_bias_grad: float32 [2560], P('head')
- decay_param_grad: float32 [2560], P('head')
- mlp_gain_grad: float32 [2560], replicated
- w_gate_grad: float32 [2560, 7680], P('seq', 'head')
- w_up_grad: float32 [2560, 7680], P('seq', 'head')
- w_down_grad: float32 [2560, 7680], P('seq', 'head')
Inputs may be any that keep to these rules, and one draw needn't show every extreme that they name: softplus(-decay_param) lies between 0.1 / 2048 and 0.006 for every channel.
All inputs are finite; a program needn't handle non-finite values.
Results may differ from a plain program's by a relative error of at most 0.0081.
Values may be sent and summed in bfloat16 or wider, within the bound.
A program may use at most 256 MiB of HBM per device.

v0:
```python
import math

import jax
import jax.numpy as jnp
from jax import lax
from jax.sharding import PartitionSpec as P

EPS = 1e-06


def from_behind(value, axis, steps):
    count = lax.axis_size(axis)
    initial, last = (max(0, -steps), min(count, count - steps))
    return lax.ppermute(value, axis, [(source, source + steps) for source in range(initial, last)])


def prefix(part, axis, combine, identity, reverse):
    count = lax.axis_size(axis)
    place = lax.axis_index(axis)
    ahead = count - 1 - place if reverse else place
    gathered = jax.tree.map(lambda a: lax.all_gather(a, axis), part)
    state = jax.tree.map(lambda a, e: jnp.zeros_like(a) + jnp.asarray(e, a.dtype), part, identity)

    def one(lap, state):
        source = count - 1 - lap if reverse else lap
        return combine(
            state, jax.tree.map(lambda a: lax.dynamic_index_in_dim(a, source, 0, False), gathered)
        )

    return lax.fori_loop(0, ahead, one, state)


def norm_rows(values):
    scale = lax.rsqrt(jnp.mean(values * values, axis=-1, keepdims=True) + EPS)
    return (scale, values * scale)


def link_forward(earlier, latter):
    return (earlier[0] * latter[0], latter[0] * earlier[1] + latter[1])


def link_backward(earlier, latter):
    return (earlier[0] * latter[0], latter[1] + latter[0] * earlier[1])


def contract_last(left_side, right_side):
    return lax.dot_general(
        left_side, right_side, (((1,), (1,)), ((), ())), preferred_element_type=jnp.float32
    )


def contract_first(left_side, right_side):
    return lax.dot_general(
        left_side, right_side, (((0,), (0,)), ((), ())), preferred_element_type=jnp.float32
    )


def shards(
    block_input,
    norm_gain,
    conv_weight,
    conv_bias,
    recur_weight,
    recur_bias,
    input_weight,
    input_bias,
    decay_param,
    mlp_gain,
    w_gate,
    w_up,
    w_down,
    out_grad,
):
    sequences, span_len, model_width = block_input.shape
    lru_width = conv_bias.shape[0]
    heads_here = recur_weight.shape[0]
    block_width = recur_weight.shape[1]
    token_rows = sequences * span_len
    head_at = lax.axis_index("head")
    stream = block_input.astype(jnp.float32)
    first_scale, first_hat = norm_rows(stream)
    xn_first = (first_hat * norm_gain).astype(jnp.bfloat16)
    own_input = lax.dynamic_slice_in_dim(xn_first, head_at * lru_width, lru_width, 2)
    edge_rows = from_behind(own_input[:, span_len - 3 :, :], "seq", 1)
    padded = jnp.concatenate([edge_rows, own_input], axis=1).astype(jnp.float32)
    conv_sum = conv_bias + conv_weight[0] * padded[:, 3 : 3 + span_len]
    for offset in range(1, 4):
        conv_sum = conv_sum + conv_weight[offset] * padded[:, 3 - offset : 3 - offset + span_len]
    conv_out = conv_sum.astype(jnp.bfloat16)
    conv_blocks = conv_out.reshape(token_rows, heads_here, block_width)
    recur_pre = (
        jnp.einsum(
            "tnh,nhk->tnk", conv_blocks, recur_weight, preferred_element_type=jnp.float32
        ).reshape(sequences, span_len, lru_width)
        + recur_bias
    )
    input_pre = (
        jnp.einsum(
            "tnh,nhk->tnk", conv_blocks, input_weight, preferred_element_type=jnp.float32
        ).reshape(sequences, span_len, lru_width)
        + input_bias
    )
    recur_gate = jax.nn.sigmoid(recur_pre)
    input_gate = jax.nn.sigmoid(input_pre)
    rate = jax.nn.softplus(-decay_param)
    log_decay = -8.0 * rate * recur_gate
    decay = jnp.exp(log_decay)
    multiplier = jnp.sqrt(-jnp.expm1(2.0 * log_decay))
    conv_float = conv_out.astype(jnp.float32)
    pushed = multiplier * input_gate * conv_float
    decay_prod, local_state = lax.associative_scan(link_forward, (decay, pushed), axis=1)
    ones_edge = jnp.ones((sequences, lru_width), jnp.float32)
    zeros_edge = jnp.zeros((sequences, lru_width), jnp.float32)
    entering = prefix(
        (decay_prod[:, -1], local_state[:, -1]), "seq", link_forward, (ones_edge, zeros_edge), False
    )
    state = local_state + decay_prod * entering[1][:, None, :]
    state_full = lax.all_gather(state.astype(jnp.bfloat16), "head", axis=2, tiled=True)
    residual = stream + state_full.astype(jnp.float32)
    second_scale, second_hat = norm_rows(residual)
    xn_second = (second_hat * mlp_gain).astype(jnp.bfloat16).reshape(token_rows, model_width)
    hidden_width = w_gate.shape[1]
    pieces = (
        lax.all_gather(w_gate, "seq", axis=0, tiled=True),
        lax.all_gather(w_up, "seq", axis=0, tiled=True),
    )
    columns = xn_second
    gate = jnp.dot(columns, pieces[0], preferred_element_type=jnp.float32)
    up_value = jnp.dot(columns, pieces[1], preferred_element_type=jnp.float32)
    activated, gelu_back = jax.vjp(jax.nn.gelu, gate)
    hidden = (activated * up_value).astype(jnp.bfloat16)
    partial_mix = contract_last(hidden, lax.all_gather(w_down, "seq", axis=0, tiled=True))
    mixed = lax.psum(partial_mix, "head")
    block_output = (
        (residual.reshape(token_rows, model_width) + mixed)
        .astype(jnp.bfloat16)
        .reshape(block_input.shape)
    )
    cotangent = out_grad.reshape(token_rows, model_width)
    columns = cotangent
    grad_hidden = jnp.dot(
        columns,
        lax.all_gather(w_down, "seq", axis=0, tiled=True),
        preferred_element_type=jnp.float32,
    )
    grad_gate = gelu_back(grad_hidden * up_value)[0].astype(jnp.bfloat16)
    grad_up = (grad_hidden * activated).astype(jnp.bfloat16)
    pieces = (
        lax.all_gather(w_gate, "seq", axis=0, tiled=True),
        lax.all_gather(w_up, "seq", axis=0, tiled=True),
    )
    block_value = contract_last(grad_gate, pieces[0]) + contract_last(grad_up, pieces[1])
    grad_xn_second = lax.psum(block_value, "head").reshape(block_input.shape)
    stacked = jnp.concatenate([grad_gate, grad_up], axis=1)
    local_rows = w_gate.shape[0]
    seq_count = lax.axis_size("seq")
    turns = math.gcd(local_rows, 8)
    per_turn = local_rows // turns
    input_view = xn_second.reshape(token_rows, seq_count, local_rows)
    grad_view = cotangent.reshape(token_rows, seq_count, local_rows)

    def grad_turn(turn, collected):
        first_row = turn * per_turn
        input_cols = lax.dynamic_slice_in_dim(input_view, first_row, per_turn, 2).reshape(
            token_rows, seq_count * per_turn
        )
        grad_cols = lax.dynamic_slice_in_dim(grad_view, first_row, per_turn, 2).reshape(
            token_rows, seq_count * per_turn
        )
        term = jnp.concatenate(
            [contract_first(input_cols, stacked), contract_first(grad_cols, hidden)], axis=1
        )
        share = lax.psum_scatter(term, "seq", scatter_dimension=0, tiled=True)
        return lax.dynamic_update_slice_in_dim(collected, share, first_row, 0)

    weight_grads = lax.fori_loop(
        0, turns, grad_turn, jnp.zeros((local_rows, 3 * hidden_width), jnp.float32)
    )
    w_gate_grad = weight_grads[:, :hidden_width]
    w_up_grad = weight_grads[:, hidden_width : 2 * hidden_width]
    w_down_grad = weight_grads[:, 2 * hidden_width :]
    weighted_second = grad_xn_second * mlp_gain
    mlp_gain_local = jnp.sum(grad_xn_second * second_hat, axis=(0, 1))
    grad_residual = out_grad.astype(jnp.float32) + second_scale * (
        weighted_second
        - second_hat * jnp.mean(weighted_second * second_hat, axis=-1, keepdims=True)
    )
    grad_state = lax.dynamic_slice_in_dim(grad_residual, head_at * lru_width, lru_width, 2)
    next_decay = jnp.concatenate([decay[:, 1:], jnp.ones_like(decay[:, :1])], axis=1)
    flipped = lax.associative_scan(
        link_forward, (jnp.flip(next_decay, 1), jnp.flip(grad_state, 1)), axis=1
    )
    after_prod = jnp.flip(flipped[0], 1)
    local_adjoint = jnp.flip(flipped[1], 1)
    leaving = (decay_prod[:, -1], decay[:, 0] * local_adjoint[:, 0])
    arriving = prefix(leaving, "seq", link_backward, (ones_edge, zeros_edge), True)
    adjoint = local_adjoint + after_prod * arriving[1][:, None, :]
    previous = jnp.concatenate([entering[1][:, None, :], state[:, :-1]], axis=1)
    grad_mult = adjoint * input_gate * conv_float
    grad_log = adjoint * previous * decay - grad_mult * decay * decay / multiplier
    grad_recur_pre = (grad_log * (-8.0 * rate) * recur_gate * (1.0 - recur_gate)).astype(
        jnp.bfloat16
    )
    grad_input_pre = (adjoint * multiplier * conv_float * input_gate * (1.0 - input_gate)).astype(
        jnp.bfloat16
    )
    decay_local = jnp.sum(grad_log * 8.0 * recur_gate, axis=(0, 1)) * jax.nn.sigmoid(-decay_param)
    recur_blocks = grad_recur_pre.reshape(token_rows, heads_here, block_width)
    input_blocks = grad_input_pre.reshape(token_rows, heads_here, block_width)
    back_gates = jnp.einsum(
        "tnk,nhk->tnh", recur_blocks, recur_weight, preferred_element_type=jnp.float32
    )
    back_gates = back_gates + jnp.einsum(
        "tnk,nhk->tnh", input_blocks, input_weight, preferred_element_type=jnp.float32
    )
    grad_conv = (
        adjoint * multiplier * input_gate + back_gates.reshape(sequences, span_len, lru_width)
    ).astype(jnp.bfloat16)
    recur_weight_local = jnp.einsum(
        "tnh,tnk->nhk", conv_blocks, recur_blocks, preferred_element_type=jnp.float32
    )
    input_weight_local = jnp.einsum(
        "tnh,tnk->nhk", conv_blocks, input_blocks, preferred_element_type=jnp.float32
    )
    recur_bias_local = jnp.sum(grad_recur_pre.astype(jnp.float32), axis=(0, 1))
    input_bias_local = jnp.sum(grad_input_pre.astype(jnp.float32), axis=(0, 1))
    later_rows = from_behind(grad_conv[:, :3, :], "seq", -1)
    grad_padded = jnp.concatenate([grad_conv, later_rows], axis=1).astype(jnp.float32)
    grad_conv_float = grad_conv.astype(jnp.float32)
    grad_own_input = conv_weight[0] * grad_padded[:, 0:span_len]
    for offset in range(1, 4):
        grad_own_input = (
            grad_own_input + conv_weight[offset] * grad_padded[:, offset : offset + span_len]
        )
    conv_weight_local = jnp.stack(
        [
            jnp.sum(grad_conv_float * padded[:, 3 - offset : 3 - offset + span_len], axis=(0, 1))
            for offset in range(4)
        ]
    )
    conv_bias_local = jnp.sum(grad_conv_float, axis=(0, 1))
    grad_xn_first = lax.all_gather(
        grad_own_input.astype(jnp.bfloat16), "head", axis=2, tiled=True
    ).astype(grad_own_input.dtype)
    weighted_first = grad_xn_first * norm_gain
    norm_gain_local = jnp.sum(grad_xn_first * first_hat, axis=(0, 1))
    input_grad = grad_residual + first_scale * (
        weighted_first - first_hat * jnp.mean(weighted_first * first_hat, axis=-1, keepdims=True)
    )
    summed = lax.psum(
        (
            norm_gain_local,
            conv_weight_local,
            conv_bias_local,
            recur_weight_local,
            recur_bias_local,
            input_weight_local,
            input_bias_local,
            decay_local,
            mlp_gain_local,
        ),
        "seq",
    )
    return (
        block_output,
        input_grad,
        summed[0],
        summed[1],
        summed[2],
        summed[3],
        summed[4],
        summed[5],
        summed[6],
        summed[7],
        summed[8],
        w_gate_grad,
        w_up_grad,
        w_down_grad,
    )


def solution(mesh):
    placed = (
        P(None, "seq", None),
        P(),
        P(None, "head"),
        P("head"),
        P("head", None, None),
        P("head"),
        P("head", None, None),
        P("head"),
        P("head"),
        P(),
        P("seq", "head"),
        P("seq", "head"),
        P("seq", "head"),
        P(None, "seq", None),
    )
    return jax.shard_map(
        shards,
        mesh=mesh,
        in_specs=placed,
        out_specs=(
            P(None, "seq", None),
            P(None, "seq", None),
            P(),
            P(None, "head"),
            P("head"),
            P("head", None, None),
            P("head"),
            P("head", None, None),
            P("head"),
            P("head"),
            P(),
            P("seq", "head"),
            P("seq", "head"),
            P("seq", "head"),
        ),
        check_vma=False,
    )
```

profile of v0, /device:TPU:0, one launch (start us, length us, event | category | flops | bytes accessed | tf_op | source)
XLA Modules:
  0.0 5454.6 jit_solution(9209895214145130442)
XLA Ops:
  230.7 45.8 all-gather
  295.0 39.5 all-gather.1
  381.3 211.0 %all-gather.11.cloned.1.call-done = bf16[2560,3840]{1,0:T(8,128)(2,1)} async-done(((bf16[160,3840]{1,0:T(8,128)(2,1)}), bf16[2560,3840]{1,0:T(8,128)(2,1)}) %all-gather.11.cloned.1.call-update) | async-done | bytes 19660816 | tf_op jit(solution)/shard_map/all_gather | solution.py:124
  610.1 202.2 %all-gather.13.cloned.1.call-done = bf16[2560,3840]{1,0:T(8,128)(2,1)} async-done(((bf16[160,3840]{1,0:T(8,128)(2,1)}), bf16[2560,3840]{1,0:T(8,128)(2,1)}) %all-gather.13.cloned.1.call-update) | async-done | bytes 19660816 | tf_op jit(solution)/shard_map/all_gather | solution.py:125
  830.1 201.9 %all-gather.15.cloned.1.call-done = bf16[2560,3840]{1,0:T(8,128)(2,1)} async-done(((bf16[160,3840]{1,0:T(8,128)(2,1)}), bf16[2560,3840]{1,0:T(8,128)(2,1)}) %all-gather.15.cloned.1.call-update) | async-done | bytes 19660816 | tf_op jit(solution)/shard_map/all_gather | solution.py:132
  1032.1 25.7 multiply_convert_fusion
  1399.8 41.5 all-gather.2
  1525.3 3752.9 %while.41 = (s32[]{:T(128)}, f32[160,11520]{1,0:T(8,128)}, bf16[512,16,160]{0,2,1:T(8,128)(2,1)}, bf16[512,7680]{1,0:T(8,128)(2,1)}, bf16[512,16,160]{0,2,1:T(8,...) while((s32[]{:T(128)}, f32[160,11520]{1,0:T(8,128)}, ...), condition=%wide.region_31.32_spmd, body=%wide.region_29.31_spmd.sunk | while | flops 3782983680 | bytes 130212720 | solution.py:176
  1540.6 350.3 %fusion.116 = f32[24,11520]{1,0:T(8,128)S(1)} fusion(f32[320,11520]{1,0:T(8,128)} %pad_maximum_fusion.27), kind=kCustom, calls=%all-reduce-scatter.clone.1 | all-reduce-scatter fusion | flops 4423681 | bytes 15852032 | tf_op jit(solution)/shard_map/while
  1918.3 27.2 collective-permute-done
  1993.1 359.2 %fusion.116 = f32[24,11520]{1,0:T(8,128)S(1)} fusion(f32[320,11520]{1,0:T(8,128)} %pad_maximum_fusion.27), kind=kCustom, calls=%all-reduce-scatter.clone.1 | all-reduce-scatter fusion | flops 4423681 | bytes 15852032 | tf_op jit(solution)/shard_map/while
  2457.2 378.6 %fusion.116 = f32[24,11520]{1,0:T(8,128)S(1)} fusion(f32[320,11520]{1,0:T(8,128)} %pad_maximum_fusion.27), kind=kCustom, calls=%all-reduce-scatter.clone.1 | all-reduce-scatter fusion | flops 4423681 | bytes 15852032 | tf_op jit(solution)/shard_map/while
  2918.2 391.5 %fusion.116 = f32[24,11520]{1,0:T(8,128)S(1)} fusion(f32[320,11520]{1,0:T(8,128)} %pad_maximum_fusion.27), kind=kCustom, calls=%all-reduce-scatter.clone.1 | all-reduce-scatter fusion | flops 4423681 | bytes 15852032 | tf_op jit(solution)/shard_map/while
  3320.4 29.1 collective-permute-done
  3393.5 407.3 %fusion.116 = f32[24,11520]{1,0:T(8,128)S(1)} fusion(f32[320,11520]{1,0:T(8,128)} %pad_maximum_fusion.27), kind=kCustom, calls=%all-reduce-scatter.clone.1 | all-reduce-scatter fusion | flops 4423681 | bytes 15852032 | tf_op jit(solution)/shard_map/while
  3808.8 31.7 collective-permute-done
  3884.4 385.0 %fusion.116 = f32[24,11520]{1,0:T(8,128)S(1)} fusion(f32[320,11520]{1,0:T(8,128)} %pad_maximum_fusion.27), kind=kCustom, calls=%all-reduce-scatter.clone.1 | all-reduce-scatter fusion | flops 4423681 | bytes 15852032 | tf_op jit(solution)/shard_map/while
  4277.4 31.7 collective-permute-done
  4353.2 384.0 %fusion.116 = f32[24,11520]{1,0:T(8,128)S(1)} fusion(f32[320,11520]{1,0:T(8,128)} %pad_maximum_fusion.27), kind=kCustom, calls=%all-reduce-scatter.clone.1 | all-reduce-scatter fusion | flops 4423681 | bytes 15852032 | tf_op jit(solution)/shard_map/while
  4745.2 31.7 collective-permute-done
  4820.8 364.4 %fusion.116 = f32[24,11520]{1,0:T(8,128)S(1)} fusion(f32[320,11520]{1,0:T(8,128)} %pad_maximum_fusion.27), kind=kCustom, calls=%all-reduce-scatter.clone.1 | all-reduce-scatter fusion | flops 4423681 | bytes 15852032 | tf_op jit(solution)/shard_map/while
  5212.8 33.1 collective-permute-done
  5303.8 92.5 %all-reduce.60 = (f32[2560]{0:T(1024)}, f32[4,1280]{1,0:T(4,128)}, f32[1280]{0:T(1024)}, f32[1280]{0:T(1024)}, f32[1280]{0:T(1024)}, /*index=5*/f32[1280]{0:T(1024)}, f32[2560]{0:T(1024)}) all-reduce(f32[2560]{0:T(1024)S(1)} %get-tuple-element.298, ...), channel_id=1, replica_groups=mesh['seq'=16,'head'=2] {'seq'}, use_global_device_ids=true, to_apply=%region_11.12 | all-reduce | flops 15360 | bytes 122880 | tf_op jit(solution)/shard_map/psum | solution.py:250
  5403.7 40.2 all-reduce.68.cloned.1.call-done
  (698 shorter events, 1339.1 us)
Async XLA Ops:
  7.2 362.2 %all-gather.9.cloned.1.call-start = ((), (), s32[]{:S(2)}) async-start(), calls=%async_computation | async-start | bytes 3932160 | tf_op jit(solution)/shard_map/all_gather | solution.py:118
  348.2 244.1 %all-gather.11.cloned.1.call-start = ((), (), s32[]{:S(2)}) async-start(), calls=%async_computation.1 | async-start | bytes 20889600 | tf_op jit(solution)/shard_map/all_gather | solution.py:124
  349.0 463.3 %all-gather.13.cloned.1.call-start = ((), (), s32[]{:S(2)}) async-start(), calls=%async_computation.2 | async-start | bytes 20889600 | tf_op jit(solution)/shard_map/all_gather | solution.py:125
  349.7 682.4 %all-gather.15.cloned.1.call-start = ((), (), s32[]{:S(2)}) async-start(), calls=%async_computation.3 | async-start | bytes 20889600 | tf_op jit(solution)/shard_map/all_gather | solution.py:132
  350.3 810.9 %all-reduce.70.cloned.1.call-start = ((), (), s32[]{:S(2)}) async-start(), calls=%async_computation.6 | async-start | bytes 20971520 | tf_op jit(solution)/shard_map/psum | solution.py:133
  1109.8 4184.7 %all-gather.17.cloned.1.call-start = ((), (), s32[]{:S(2)}) async-start(), calls=%async_computation.4 | async-start | bytes 3932160 | tf_op jit(solution)/shard_map/all_gather | solution.py:242
  1521.7 3922.1 %all-reduce.68.cloned.1.call-start = ((), (), s32[]{:S(2)}) async-start(), calls=%async_computation.5 | async-start | bytes 5242880 | tf_op jit(solution)/shard_map/psum | solution.py:250
  1890.9 58.2 %collective-permute-start.1 = (f32[24,11520]{1,0:T(8,128)S(1)}, f32[24,11520]{1,0:T(8,128)S(1)}, u32[]{:S(2)}, u32[]{:S(2)}) collective-permute-start(f32[24,11520]{1,0:T(8,128)S(1)} %fusion.116), channel_id=1, source_target_pairs={{0,4},{2,6},{4,8},{6,10},{8,12},{10,14},{12,16},{14,18},{16,20},{1... | collective-permute-start | bytes 3317768 | tf_op jit(solution)/shard_map/while
  1908.6 40.5 collective-permute-start.2
  2352.3 60.9 %collective-permute-start.1 = (f32[24,11520]{1,0:T(8,128)S(1)}, f32[24,11520]{1,0:T(8,128)S(1)}, u32[]{:S(2)}, u32[]{:S(2)}) collective-permute-start(f32[24,11520]{1,0:T(8,128)S(1)} %fusion.116), channel_id=1, source_target_pairs={{0,4},{2,6},{4,8},{6,10},{8,12},{10,14},{12,16},{14,18},{16,20},{1... | collective-permute-start | bytes 3317768 | tf_op jit(solution)/shard_map/while
  2366.4 46.8 collective-permute-start.2
  2372.7 36.9 collective-permute-start
  2835.8 38.5 collective-permute-start.1
  3309.8 39.7 collective-permute-start.1
  3311.1 38.4 collective-permute-start.2
  3800.8 39.7 collective-permute-start.1
  3802.1 38.4 collective-permute-start.2
  4269.4 39.7 collective-permute-start.1
  4270.8 38.4 collective-permute-start.2
  4737.2 39.7 collective-permute-start.1
  4738.5 38.4 collective-permute-start.2
  5185.2 64.3 %collective-permute-start.1 = (f32[24,11520]{1,0:T(8,128)S(1)}, f32[24,11520]{1,0:T(8,128)S(1)}, u32[]{:S(2)}, u32[]{:S(2)}) collective-permute-start(f32[24,11520]{1,0:T(8,128)S(1)} %fusion.116), channel_id=1, source_target_pairs={{0,4},{2,6},{4,8},{6,10},{8,12},{10,14},{12,16},{14,18},{16,20},{1... | collective-permute-start | bytes 3317768 | tf_op jit(solution)/shard_map/while
  5202.7 46.8 collective-permute-start.2
  5209.0 36.9 collective-permute-start
  (121 other events, 2137.0 us)
Sparse Core Ops, SparseCore 0:
  348.3 21.0 all-gather.8
  372.2 220.0 all-gather.10
  595.1 217.0 all-gather.12
  814.9 217.0 all-gather.14
  1109.9 40.8 all-reduce.69
  1521.8 9.7 all-gather.16
  5288.3 155.5 all-reduce.67
where the time goes:
time: 5480 us; the launch traced here: 5450 us
  blocking collectives  3240 us (59%)
  waiting for transfers between devices  920 us (17%)
  local copies, waits for them, and re-layouts  730 us (13%)
  other arithmetic  236 us (4%)
  matrix products  179 us (3%)
  starting transfers between devices  128 us (2%)
    while x8, blocking collectives  3020 us
    while x24, waiting for transfers between devices  242 us
    all_gather x1, waiting for transfers between devices, shards(): lax.all_gather(w_gate, 'seq', axis=0, tiled=True)  211 us
    while x48, local copies, waits for them, and re-layouts  210 us
    all_gather x1, waiting for transfers between devices, shards(): lax.all_gather(w_up, 'seq', axis=0, tiled=True)  202 us
    all_gather x1, waiting for transfers between devices, shards(): lax.all_gather(w_down, 'seq', axis=0, tiled=True)  202 us
    slice x49, local copies, waits for them, and re-layouts, shards(): lax.associative_scan(link_forward, (jnp.flip(next_decay, 1), jnp.flip(gra...  129 us
    all_gather x3, blocking collectives, prefix(): gathered = jax.tree.map(lambda a: lax.all_gather(a, axis), part)  127 us
  transfers between devices with their start and end apart: 33, of which 17 were waited for; matrix products, arithmetic and copies ran while one was open for 65% of the time, Pallas kernels for 0%

commit v1 on v0

--- a/solution.py
+++ b/solution.py
@@ -1,11 +1,17 @@
+import functools
 import math
 
 import jax
 import jax.numpy as jnp
 from jax import lax
+from jax.experimental import pallas as pl
+from jax.experimental.pallas import tpu as pltpu
 from jax.sharding import PartitionSpec as P
 
 EPS = 1e-06
+MESH = pl.DeviceIdType.MESH
+LANES = 128
+CHUNK = 256
 
 
 def from_behind(value, axis, steps):
@@ -53,6 +59,560 @@
     return lax.dot_general(
         left_side, right_side, (((0,), (0,)), ((), ())), preferred_element_type=jnp.float32
     )
+
+
+def dot_nn(left_side, right_side):
+    return jnp.dot(left_side, right_side, preferred_element_type=jnp.float32)
+
+
+def remote(src, dst, send, recv, seq, head):
+    return pltpu.make_async_remote_copy(
+        src_ref=src, dst_ref=dst, send_sem=send, recv_sem=recv,
+        device_id={"seq": seq, "head": head}, device_id_type=MESH,
+    )
+
+
+def ffn_kernel(
+    seq_count, xn_ref, g_ref, wg_ref, wu_ref, wd_ref,
+    mix_ref, gx_ref, dw_ref, dh_ref, r1_ref, e_ref, r2_ref, f_ref, sib_ref, peer_ref,
+    x_all, g_all, w_all, hid, gg, gu, dv, va, vb, acc, ld,
+    tok_s, tok_r, fwd_s, fwd_r, s1_s, s1_r, z_s, z_r, y_s, y_r, c1_s, c1_r, c2_s, c2_r, c3_s, c3_r,
+    sib_s, sib_r, peer_s, peer_r, loc,
+):
+    far = seq_count // 8
+    rows = wg_ref.shape[0]
+    pair = 2 * rows
+    tokens, half = xn_ref.shape
+    span = w_all.shape[2]
+    chunks = span // CHUNK
+    tiles = wg_ref.shape[1] // LANES
+    base, extra = tiles // 4, tiles % 4
+    s = lax.axis_index("seq")
+    h = lax.axis_index("head")
+    x = s % 2
+    y = (s // 2) % 2
+    zl = (s // 4) % 2
+    zh = s // 8
+    a = zl * 2 + x
+    weights = (wg_ref, wu_ref, wd_ref)
+
+    def seq_of(zh_, zl_, y_, x_):
+        return ((zh_ * 2 + zl_) * 2 + y_) * 2 + x_
+
+    def peer(d):
+        zl_, x_ = (zl + d // 2) % 2, (x + d % 2) % 2
+        return zl_ * 2 + x_, seq_of(zh, zl_, y, x_), zl_, x_
+
+    def first_tile(a_):
+        low = base * a_ + jnp.minimum(a_, extra)
+        high = base * a_ + jnp.maximum(a_ - (4 - extra), 0)
+        return jnp.where(h == 0, low, high)
+
+    def wide(zl_):
+        return zl_ == h
+
+    def block_rows(zh_, zl_, y_):
+        return pl.ds(pl.multiple_of(((zh_ * 2 + zl_) * 2 + y_) * pair, 32), pair)
+
+    def cols(c, width=CHUNK):
+        return pl.ds(pl.multiple_of(c * CHUNK, CHUNK), width)
+
+    def by_width(c, is_wide, run):
+        narrow = (c == chunks - 1) & jnp.logical_not(is_wide)
+        pl.when(narrow)(lambda: run(LANES))
+        pl.when(jnp.logical_not(narrow))(lambda: run(CHUNK))
+
+    y_seq = seq_of(zh, zl, 1 - y, x)
+
+    def z_seq(q):
+        return seq_of((zh + q) % far, zl, y, x)
+
+    barrier = pltpu.get_barrier_semaphore()
+    partners = [(peer(d)[1], h) for d in (1, 2, 3)] + [(s, 1 - h), (y_seq, h)]
+    partners += [(z_seq(q), h) for q in range(1, far)]
+    for seq, head in partners:
+        pl.semaphore_signal(barrier, inc=1, device_id={"seq": seq, "head": head}, device_id_type=MESH)
+    pl.semaphore_wait(barrier, len(partners))
+
+    def s1_send(c, d, w, width):
+        a_, seq, zl_, _ = peer(d)
+        col = pl.multiple_of((first_tile(a_) + 2 * c) * LANES, LANES)
+        return remote(
+            weights[w].at[:, pl.ds(col, width)],
+            w_all.at[w, pl.ds(pl.multiple_of(s * rows, 32), rows), cols(c, width)],
+            s1_s.at[c, d - 1, w], s1_r.at[c, d - 1, w], seq, h,
+        )
+
+    def s1_recv(c, d, w, width):
+        _, seq, _, _ = peer(d)
+        return remote(
+            weights[w].at[:, pl.ds(0, width)],
+            w_all.at[w, pl.ds(pl.multiple_of(seq * rows, 32), rows), cols(c, width)],
+            s1_s.at[c, d - 1, w], s1_r.at[c, d - 1, w], seq, h,
+        )
+
+    def s1_own(c, w, width):
+        col = pl.multiple_of((first_tile(a) + 2 * c) * LANES, LANES)
+        return pltpu.make_async_copy(
+            weights[w].at[:, pl.ds(col, width)],
+            w_all.at[w, pl.ds(pl.multiple_of(s * rows, 32), rows), cols(c, width)],
+            loc.at[c, w],
+        )
+
+    def s1_start(c):
+        for d in (1, 2, 3):
+            def go(width, d=d):
+                for w in range(3):
+                    s1_send(c, d, w, width).start()
+            by_width(c, wide(peer(d)[2]), go)
+
+        def own(width):
+            for w in range(3):
+                s1_own(c, w, width).start()
+        by_width(c, wide(zl), own)
+
+    def s1_wait(c):
+        def got(width):
+            for w in range(3):
+                s1_own(c, w, width).wait()
+                for d in (1, 2, 3):
+                    s1_recv(c, d, w, width).wait_recv()
+        by_width(c, wide(zl), got)
+
+    def s1_drain(c):
+        for d in (1, 2, 3):
+            def go(width, d=d):
+                for w in range(3):
+                    s1_send(c, d, w, width).wait_send()
+            by_width(c, wide(peer(d)[2]), go)
+
+    def z_copy(c, q, zl_, width, incoming):
+        zh_ = (zh - q + far) % far if incoming else zh
+        part = w_all.at[:, block_rows(zh_, zl_, y), cols(c, width)]
+        return remote(part, part, z_s.at[c, q - 1, zl_], z_r.at[c, q - 1, zl_], z_seq(q), h)
+
+    def y_copy(c, q, zl_, width, incoming):
+        part = w_all.at[:, block_rows((zh - q + far) % far, zl_, 1 - y if incoming else y), cols(c, width)]
+        return remote(part, part, y_s.at[c, q, zl_], y_r.at[c, q, zl_], y_seq, h)
+
+    def z_start(c):
+        def go(width):
+            for q in range(1, far):
+                for zl_ in range(2):
+                    z_copy(c, q, zl_, width, False).start()
+            for zl_ in range(2):
+                y_copy(c, 0, zl_, width, False).start()
+        by_width(c, wide(zl), go)
+
+    def z_forward(c):
+        def go(width):
+            for q in range(1, far):
+                for zl_ in range(2):
+                    z_copy(c, q, zl_, width, True).wait_recv()
+                    y_copy(c, q, zl_, width, False).start()
+        by_width(c, wide(zl), go)
+
+    def y_wait(c):
+        def go(width):
+            for q in range(far):
+                for zl_ in range(2):
+                    y_copy(c, q, zl_, width, True).wait_recv()
+        by_width(c, wide(zl), go)
+
+    def zy_drain(c):
+        def go(width):
+            for zl_ in range(2):
+                for q in range(1, far):
+                    z_copy(c, q, zl_, width, False).wait_send()
+                for q in range(far):
+                    y_copy(c, q, zl_, width, False).wait_send()
+        by_width(c, wide(zl), go)
+
+    half_cols = pl.ds(pl.multiple_of(h * half, LANES), half)
+
+    def tok_rows(a_):
+        return pl.ds(pl.multiple_of(a_ * tokens, 32), tokens)
+
+    def tok_copy(k, d, incoming):
+        src = xn_ref if k == 0 else g_ref.at[:, half_cols]
+        dst = (x_all, g_all)[k]
+        a_, seq, _, _ = peer(d)
+        return remote(
+            src, dst.at[tok_rows(a_ if incoming else a), half_cols],
+            tok_s.at[k, d - 1], tok_r.at[k, d - 1], seq, h,
+        )
+
+    def fwd_copy(k, d, incoming):
+        dst = (x_all, g_all)[k]
+        side = pl.ds(pl.multiple_of((1 - h if incoming else h) * half, LANES), half)
+        part = dst.at[tok_rows(peer(d)[0]), side]
+        return remote(part, part, fwd_s.at[k, d], fwd_r.at[k, d], s, 1 - h)
+
+    own_x = pltpu.make_async_copy(xn_ref, x_all.at[tok_rows(a), half_cols], loc.at[chunks, 0])
+    own_g = pltpu.make_async_copy(g_ref, g_all.at[tok_rows(a), :], loc.at[chunks, 1])
+
+    s1_start(0)
+    for d in (1, 2, 3):
+        tok_copy(1, d, False).start()
+        tok_copy(0, d, False).start()
+    own_x.start()
+    own_g.start()
+    pl.loop(1, chunks)(s1_start)
+
+    @pl.when(jnp.logical_not(wide(zl)))
+    def _():
+        w_all[:, :, pl.ds(span - LANES, LANES)] = jnp.zeros((3, w_all.shape[1], LANES), jnp.bfloat16)
+
+    @pl.loop(0, chunks)
+    def _(c):
+        s1_wait(c)
+        z_start(c)
+
+    z_forward(0)
+    z_forward(1)
+    own_x.wait()
+    fwd_copy(0, 0, False).start()
+    own_g.wait()
+    for d in (1, 2, 3):
+        for k in (1, 0):
+            tok_copy(k, d, True).wait_recv()
+            fwd_copy(k, d, False).start()
+    fwd_copy(0, 0, True).wait_recv()
+    for d in (1, 2, 3):
+        for k in (1, 0):
+            fwd_copy(k, d, True).wait_recv()
+
+    def r1_copy(c, zh_, zl_, incoming):
+        return remote(
+            dh_ref.at[c, :, block_rows(zh_, zl_, 1 - y), :], r1_ref.at[c, :, zh_ * 2 + zl_],
+            c1_s.at[c, zh_, zl_], c1_r.at[c, zh_, zl_], y_seq, h,
+        )
+
+    def r1_start(c):
+        for zh_ in range(far):
+            for zl_ in range(2):
+                r1_copy(c, zh_, zl_, False).start()
+
+    def r2_copy(c, q, zl_):
+        return remote(
+            e_ref.at[c, :, ((zh + q) % far) * 2 + zl_], r2_ref.at[c, q - 1, :, zl_],
+            c2_s.at[c, q - 1, zl_], c2_r.at[c, q - 1, zl_], z_seq(q), h,
+        )
+
+    def add_into(first, second, blocks):
+        @pl.loop(0, 3)
+        def _(w):
+            @pl.loop(0, blocks)
+            def _(b):
+                total = first[w, b].astype(jnp.float32) + second[w, b].astype(jnp.float32)
+                first[w, b] = total.astype(jnp.bfloat16)
+
+    def sum_near(c):
+        loads = []
+        for zh_ in range(far):
+            for zl_ in range(2):
+                loads.append(pltpu.make_async_copy(
+                    dh_ref.at[c, :, block_rows(zh_, zl_, y), :], va.at[:, zh_ * 2 + zl_], loc.at[chunks + 1 + zh_, zl_]
+                ))
+        for load in loads:
+            load.start()
+        for zh_ in range(far):
+            for zl_ in range(2):
+                r1_copy(c, zh_, zl_, True).wait_recv()
+        other = pltpu.make_async_copy(r1_ref.at[c], vb, loc.at[chunks, 2])
+        other.start()
+        for load in loads:
+            load.wait()
+        other.wait()
+        add_into(va, vb, 2 * far)
+        back = pltpu.make_async_copy(va, e_ref.at[c], loc.at[chunks, 2])
+        back.start()
+        back.wait()
+        for q in range(1, far):
+            for zl_ in range(2):
+                r2_copy(c, q, zl_).start()
+
+    def c3_copy(c, d, width, incoming):
+        a_, seq, zl_, x_ = peer(d)
+        col = pl.multiple_of((first_tile(a_ if incoming else a) + 2 * c) * LANES, LANES)
+        return remote(
+            f_ref.at[c, :, zl_, pl.ds(pl.multiple_of(x_ * rows, 32), rows), pl.ds(0, width)],
+            dw_ref.at[:, :, pl.ds(col, width)],
+            c3_s.at[c, d - 1], c3_r.at[c, d - 1], seq, h,
+        )
+
+    def c3_own(c, width):
+        col = pl.multiple_of((first_tile(a) + 2 * c) * LANES, LANES)
+        return pltpu.make_async_copy(
+            f_ref.at[c, :, zl, pl.ds(pl.multiple_of(x * rows, 32), rows), pl.ds(0, width)],
+            dw_ref.at[:, :, pl.ds(col, width)], loc.at[c, 0],
+        )
+
+    def sum_far(c):
+        mine = pltpu.make_async_copy(e_ref.at[c, :, pl.ds(zh * 2, 2)], va.at[:, pl.ds(0, 2)], loc.at[chunks, 0])
+        mine.start()
+        mine.wait()
+        for q in range(1, far):
+            for zl_ in range(2):
+                r2_copy(c, q, zl_).wait_recv()
+            other = pltpu.make_async_copy(r2_ref.at[c, q - 1], vb.at[:, pl.ds(0, 2)], loc.at[chunks, 0])
+            other.start()
+            other.wait()
+            add_into(va, vb, 2)
+        back = pltpu.make_async_copy(va.at[:, pl.ds(0, 2)], f_ref.at[c], loc.at[chunks, 0])
+        back.start()
+        back.wait()
+
+        def go(width):
+            for d in (1, 2, 3):
+                c3_copy(c, d, width, False).start()
+            c3_own(c, width).start()
+        by_width(c, wide(zl), go)
+
+    def forward_chunk(c):
+        @pl.loop(0, 4)
+        def _(i):
+            r = tok_rows(i)
+            xb = x_all[r, :]
+            gate = dot_nn(xb, w_all[0, :, cols(c)])
+            up = dot_nn(xb, w_all[1, :, cols(c)])
+            gh = dot_nn(g_all[r, :], w_all[2, :, cols(c)])
+            k0, k1 = 0.7978845608028654, 0.044715
+            th = jnp.tanh(k0 * (gate + k1 * gate * gate * gate))
+            cdf = 0.5 * (1.0 + th)
+            act = gate * cdf
+            slope = cdf + 0.5 * gate * (1.0 - th * th) * k0 * (1.0 + 3.0 * k1 * gate * gate)
+            hid[r, cols(c)] = (act * up).astype(jnp.bfloat16)
+            gu[r, cols(c)] = (gh * act).astype(jnp.bfloat16)
+            gg[r, cols(c)] = (gh * up * slope).astype(jnp.bfloat16)
+
+    def weight_chunk(c):
+        for w, (left, right) in enumerate(((x_all, gg), (x_all, gu), (g_all, hid))):
+            @pl.loop(0, x_all.shape[1] // 512)
+            def _(j):
+                r = pl.ds(pl.multiple_of(j * 512, 512), 512)
+                dv[w, r, :] = contract_first(left[:, r], right[:, cols(c)]).astype(jnp.bfloat16)
+            pltpu.make_async_copy(dv.at[w], dh_ref.at[c, w], loc.at[chunks, w]).start()
+        for w in range(3):
+            pltpu.make_async_copy(dv.at[w], dh_ref.at[c, w], loc.at[chunks, w]).wait()
+        r1_start(c)
+
+    @pl.loop(0, chunks)
+    def _(c):
+        y_wait(c)
+        forward_chunk(c)
+        weight_chunk(c)
+        pl.when(c + 2 < chunks)(lambda: z_forward(c + 2))
+        pl.when(c >= 1)(lambda: sum_near(c - 1))
+        pl.when(c >= 2)(lambda: sum_far(c - 2))
+
+    def product(which, r, d_rows):
+        if which == 0:
+            return contract_last(gg[r, :], w_all[0, d_rows, :]) + contract_last(gu[r, :], w_all[1, d_rows, :])
+        return contract_last(hid[r, :], w_all[2, d_rows, :])
+
+    stage = (x_all, g_all)
+    outs = (gx_ref, mix_ref)
+
+    def sib_copy(which, k):
+        r = pl.ds(pl.multiple_of(k * tokens, 32), tokens)
+        return remote(
+            stage[which].at[r, pl.ds(0, half)], sib_ref.at[which, k], sib_s.at[which, k], sib_r.at[which, k], s, 1 - h
+        )
+
+    def peer_copy(which, k, d):
+        r = pl.ds(pl.multiple_of(k * tokens, 32), tokens)
+        return remote(
+            stage[which].at[r, pl.ds(half, half)], peer_ref.at[which, k], peer_s.at[which, k], peer_r.at[which, k],
+            peer(d)[1], h,
+        )
+
+    steps = half // 256
+
+    def token_sums(which):
+        @pl.loop(0, 4)
+        def _(k):
+            d = 3 - k
+            r = tok_rows(peer(d)[0])
+            kr = pl.ds(pl.multiple_of(k * tokens, 32), tokens)
+
+            @pl.loop(0, steps)
+            def _(j):
+                dr = pl.ds(pl.multiple_of((1 - h) * half + j * 256, 256), 256)
+                stage[which][kr, pl.ds(pl.multiple_of(j * 256, 256), 256)] = product(which, r, dr).astype(jnp.bfloat16)
+            sib_copy(which, k).start()
+
+            @pl.loop(0, steps)
+            def _(j):
+                dr = pl.ds(pl.multiple_of(h * half + j * 256, 256), 256)
+                acc[:, pl.ds(pl.multiple_of(j * 256, 256), 256)] = product(which, r, dr)
+            sib_copy(which, k).wait_recv()
+            load = pltpu.make_async_copy(sib_ref.at[which, k], ld, loc.at[chunks, 0])
+            load.start()
+            load.wait()
+            acc[...] += ld[...].astype(jnp.float32)
+
+            @pl.when(d != 0)
+            def _():
+                stage[which][kr, pl.ds(half, half)] = acc[...].astype(jnp.bfloat16)
+                peer_copy(which, k, d).start()
+
+    def token_finish(which):
+        for k in range(3):
+            peer_copy(which, k, 3 - k).wait_recv()
+            load = pltpu.make_async_copy(peer_ref.at[which, k], ld, loc.at[chunks, 0])
+            load.start()
+            load.wait()
+            acc[...] += ld[...].astype(jnp.float32)
+        store = pltpu.make_async_copy(acc, outs[which], loc.at[chunks, 0])
+        store.start()
+        store.wait()
+        for k in range(4):
+            sib_copy(which, k).wait_send()
+        for k in range(3):
+            peer_copy(which, k, 3 - k).wait_send()
+
+    for d in (1, 2, 3):
+        for k in (0, 1):
+            tok_copy(k, d, False).wait_send()
+            fwd_copy(k, d, False).wait_send()
+    fwd_copy(0, 0, False).wait_send()
+    token_sums(0)
+    token_finish(0)
+    sum_near(chunks - 1)
+    sum_far(chunks - 2)
+    token_sums(1)
+    token_finish(1)
+    sum_far(chunks - 1)
+
+    @pl.loop(0, chunks)
+    def _(c):
+        s1_drain(c)
+        zy_drain(c)
+        for zh_ in range(far):
+            for zl_ in range(2):
+                r1_copy(c, zh_, zl_, False).wait_send()
+        for q in range(1, far):
+            for zl_ in range(2):
+                r2_copy(c, q, zl_).wait_send()
+
+        def sent(width):
+            for d in (1, 2, 3):
+                c3_copy(c, d, width, False).wait_send()
+            c3_own(c, width).wait()
+        by_width(c, wide(zl), sent)
+        for d in (1, 2, 3):
+            by_width(c, wide(peer(d)[2]), lambda width, d=d: c3_copy(c, d, width, True).wait_recv())
+
+
+def feed_forward(seq_count, xn_half, cotangent, w_gate, w_up, w_down):
+    tokens, half = xn_half.shape
+    width = cotangent.shape[1]
+    rows, units = w_gate.shape
+    pair, far = 2 * rows, seq_count // 8
+    chunks = -(-units // (4 * CHUNK))
+    span = chunks * CHUNK
+    bf, f32 = jnp.bfloat16, jnp.float32
+    any_space = pl.BlockSpec(memory_space=pl.ANY)
+    outs = [
+        ((tokens, half), f32), ((tokens, half), f32), ((3, rows, units), bf),
+        ((chunks, 3, width, CHUNK), bf), ((chunks, 3, 2 * far, pair, CHUNK), bf), ((chunks, 3, 2 * far, pair, CHUNK), bf),
+        ((chunks, far - 1, 3, 2, pair, CHUNK), bf), ((chunks, 3, 2, pair, CHUNK), bf),
+        ((2, 4, tokens, half), bf), ((2, 3, tokens, half), bf),
+    ]
+    sem = pltpu.SemaphoreType.DMA
+    scratch = [
+        pltpu.VMEM((4 * tokens, width), bf), pltpu.VMEM((4 * tokens, width), bf), pltpu.VMEM((3, width, span), bf),
+        pltpu.VMEM((4 * tokens, span), bf), pltpu.VMEM((4 * tokens, span), bf), pltpu.VMEM((4 * tokens, span), bf),
+        pltpu.VMEM((3, width, CHUNK), bf), pltpu.VMEM((3, 2 * far, pair, CHUNK), bf), pltpu.VMEM((3, 2 * far, pair, CHUNK), bf),
+        pltpu.VMEM((tokens, half), f32), pltpu.VMEM((tokens, half), bf),
+    ]
+    for shape in (
+        (2, 3), (2, 4), (chunks, 3, 3), (chunks, far - 1, 2), (chunks, far, 2), (chunks, far, 2),
+        (chunks, far - 1, 2), (chunks, 3), (2, 4), (2, 3),
+    ):
+        scratch += [sem(shape), sem(shape)]
+    scratch.append(sem((chunks + 1 + far, 3)))
+    flops = 18 * 4 * tokens * width * span
+    results = pl.pallas_call(
+        functools.partial(ffn_kernel, seq_count),
+        out_shape=[jax.ShapeDtypeStruct(shape, kind) for shape, kind in outs],
+        in_specs=[any_space] * 5,
+        out_specs=[any_space] * len(outs),
+        scratch_shapes=scratch,
+        compiler_params=pltpu.CompilerParams(
+            collective_id=0, has_side_effects=True, vmem_limit_bytes=63 * 2**20
+        ),
+        cost_estimate=pl.CostEstimate(flops=flops, bytes_accessed=100 * 2**20, transcendentals=4 * tokens * span),
+        name="feed_forward",
+    )(xn_half, cotangent, w_gate, w_up, w_down)
+    return results[0], results[1], results[2]
+
+
+def gathered_feed_forward(block_input, residual, xn_second, out_grad, w_gate, w_up, w_down):
+    model_width = block_input.shape[2]
+    token_rows = xn_second.shape[0]
+    hidden_width = w_gate.shape[1]
+    pieces = (
+        lax.all_gather(w_gate, "seq", axis=0, tiled=True),
+        lax.all_gather(w_up, "seq", axis=0, tiled=True),
+    )
+    columns = xn_second
+    gate = jnp.dot(columns, pieces[0], preferred_element_type=jnp.float32)
+    up_value = jnp.dot(columns, pieces[1], preferred_element_type=jnp.float32)
+    activated, gelu_back = jax.vjp(jax.nn.gelu, gate)
+    hidden = (activated * up_value).astype(jnp.bfloat16)
+    partial_mix = contract_last(hidden, lax.all_gather(w_down, "seq", axis=0, tiled=True))
+    mixed = lax.psum(partial_mix, "head")
+    block_output = (
+        (residual.reshape(token_rows, model_width) + mixed)
+        .astype(jnp.bfloat16)
+        .reshape(block_input.shape)
+    )
+    cotangent = out_grad.reshape(token_rows, model_width)
+    columns = cotangent
+    grad_hidden = jnp.dot(
+        columns,
+        lax.all_gather(w_down, "seq", axis=0, tiled=True),
+        preferred_element_type=jnp.float32,
+    )
+    grad_gate = gelu_back(grad_hidden * up_value)[0].astype(jnp.bfloat16)
+    grad_up = (grad_hidden * activated).astype(jnp.bfloat16)
+    pieces = (
+        lax.all_gather(w_gate, "seq", axis=0, tiled=True),
+        lax.all_gather(w_up, "seq", axis=0, tiled=True),
+    )
+    block_value = contract_last(grad_gate, pieces[0]) + contract_last(grad_up, pieces[1])
+    grad_xn_second = lax.psum(block_value, "head").reshape(block_input.shape)
+    stacked = jnp.concatenate([grad_gate, grad_up], axis=1)
+    local_rows = w_gate.shape[0]
+    seq_count = lax.axis_size("seq")
+    turns = math.gcd(local_rows, 8)
+    per_turn = local_rows // turns
+    input_view = xn_second.reshape(token_rows, seq_count, local_rows)
+    grad_view = cotangent.reshape(token_rows, seq_count, local_rows)
+
+    def grad_turn(turn, collected):
+        first_row = turn * per_turn
+        input_cols = lax.dynamic_slice_in_dim(input_view, first_row, per_turn, 2).reshape(
+            token_rows, seq_count * per_turn
+        )
+        grad_cols = lax.dynamic_slice_in_dim(grad_view, first_row, per_turn, 2).reshape(
+            token_rows, seq_count * per_turn
+        )
+        term = jnp.concatenate(
+            [contract_first(input_cols, stacked), contract_first(grad_cols, hidden)], axis=1
+        )
+        share = lax.psum_scatter(term, "seq", scatter_dimension=0, tiled=True)
+        return lax.dynamic_update_slice_in_dim(collected, share, first_row, 0)
+
+    weight_grads = lax.fori_loop(
+        0, turns, grad_turn, jnp.zeros((local_rows, 3 * hidden_width), jnp.float32)
+    )
+    w_gate_grad = weight_grads[:, :hidden_width]
+    w_up_grad = weight_grads[:, hidden_width : 2 * hidden_width]
+    w_down_grad = weight_grads[:, 2 * hidden_width :]
+    return block_output, grad_xn_second, w_gate_grad, w_up_grad, w_down_grad
 
 
 def shards(
@@ -119,66 +679,20 @@
     residual = stream + state_full.astype(jnp.float32)
     second_scale, second_hat = norm_rows(residual)
     xn_second = (second_hat * mlp_gain).astype(jnp.bfloat16).reshape(token_rows, model_width)
-    hidden_width = w_gate.shape[1]
-    pieces = (
-        lax.all_gather(w_gate, "seq", axis=0, tiled=True),
-        lax.all_gather(w_up, "seq", axis=0, tiled=True),
-    )
-    columns = xn_second
-    gate = jnp.dot(columns, pieces[0], preferred_element_type=jnp.float32)
-    up_value = jnp.dot(columns, pieces[1], preferred_element_type=jnp.float32)
-    activated, gelu_back = jax.vjp(jax.nn.gelu, gate)
-    hidden = (activated * up_value).astype(jnp.bfloat16)
-    partial_mix = contract_last(hidden, lax.all_gather(w_down, "seq", axis=0, tiled=True))
-    mixed = lax.psum(partial_mix, "head")
-    block_output = (
-        (residual.reshape(token_rows, model_width) + mixed)
-        .astype(jnp.bfloat16)
-        .reshape(block_input.shape)
-    )
-    cotangent = out_grad.reshape(token_rows, model_width)
-    columns = cotangent
-    grad_hidden = jnp.dot(
-        columns,
-        lax.all_gather(w_down, "seq", axis=0, tiled=True),
-        preferred_element_type=jnp.float32,
-    )
-    grad_gate = gelu_back(grad_hidden * up_value)[0].astype(jnp.bfloat16)
-    grad_up = (grad_hidden * activated).astype(jnp.bfloat16)
-    pieces = (
-        lax.all_gather(w_gate, "seq", axis=0, tiled=True),
-        lax.all_gather(w_up, "seq", axis=0, tiled=True),
-    )
-    block_value = contract_last(grad_gate, pieces[0]) + contract_last(grad_up, pieces[1])
-    grad_xn_second = lax.psum(block_value, "head").reshape(block_input.shape)
-    stacked = jnp.concatenate([grad_gate, grad_up], axis=1)
-    local_rows = w_gate.shape[0]
     seq_count = lax.axis_size("seq")
-    turns = math.gcd(local_rows, 8)
-    per_turn = local_rows // turns
-    input_view = xn_second.reshape(token_rows, seq_count, local_rows)
-    grad_view = cotangent.reshape(token_rows, seq_count, local_rows)
-
-    def grad_turn(turn, collected):
-        first_row = turn * per_turn
-        input_cols = lax.dynamic_slice_in_dim(input_view, first_row, per_turn, 2).reshape(
-            token_rows, seq_count * per_turn
-        )
-        grad_cols = lax.dynamic_slice_in_dim(grad_view, first_row, per_turn, 2).reshape(
-            token_rows, seq_count * per_turn
-        )
-        term = jnp.concatenate(
-            [contract_first(input_cols, stacked), contract_first(grad_cols, hidden)], axis=1
-        )
-        share = lax.psum_scatter(term, "seq", scatter_dimension=0, tiled=True)
-        return lax.dynamic_update_slice_in_dim(collected, share, first_row, 0)
-
-    weight_grads = lax.fori_loop(
-        0, turns, grad_turn, jnp.zeros((local_rows, 3 * hidden_width), jnp.float32)
-    )
-    w_gate_grad = weight_grads[:, :hidden_width]
-    w_up_grad = weight_grads[:, hidden_width : 2 * hidden_width]
-    w_down_grad = weight_grads[:, 2 * hidden_width :]
+    if seq_count % 8 == 0 and w_gate.shape[0] % 32 == 0:
+        xn_half = lax.dynamic_slice_in_dim(xn_second, head_at * lru_width, lru_width, 1)
+        mixed_half, grad_half, weight_grads = feed_forward(
+            seq_count, xn_half, out_grad.reshape(token_rows, model_width), w_gate, w_up, w_down
+        )
+        mixed = lax.all_gather(mixed_half, "head", axis=1, tiled=True).reshape(block_input.shape)
+        grad_xn_second = lax.all_gather(grad_half, "head", axis=1, tiled=True).reshape(block_input.shape)
+        block_output = (residual + mixed).astype(jnp.bfloat16)
+        w_gate_grad, w_up_grad, w_down_grad = [weight_grads[w].astype(jnp.float32) for w in range(3)]
+    else:
+        block_output, grad_xn_second, w_gate_grad, w_up_grad, w_down_grad = gathered_feed_forward(
+            block_input, residual, xn_second, out_grad, w_gate, w_up, w_down
+        )
     weighted_second = grad_xn_second * mlp_gain
     mlp_gain_local = jnp.sum(grad_xn_second * second_hat, axis=(0, 1))
     grad_residual = out_grad.astype(jnp.float32) + second_scale * (

time: 5480 us -> 1570 us (0.29)
  blocking collectives: 3240 us -> 202 us
  waiting for transfers between devices: 920 us -> 75.7 us
  Pallas kernels: 0 us -> 654 us
  local copies, waits for them, and re-layouts: 730 us -> 416 us
  matrix products: 179 us -> 11.3 us
  starting transfers between devices: 128 us -> 6.34 us
  other arithmetic: 236 us -> 176 us
    while x8 -> x0, blocking collectives: 3020 us -> none
    pallas_call x0 -> x1, Pallas kernels: none -> 654 us  [feed_forward(): pl.pallas_call(functools.partial(ffn_kernel, seq_count), out_shape=[jax.S...]
    all_gather x3 -> x2, waiting for transfers between devices: 615 us -> 0.02 us  [the longest x1 0.02 us: shards(): lax.all_gather(grad_half, 'head', axis=1, tiled=True)]
    while x24 -> x0, waiting for transfers between devices: 242 us -> none
    while x48 -> x0, local copies, waits for them, and re-layouts: 210 us -> none
    dot_general x22 -> x0, matrix products: 165 us -> none  [the longest x3 52 us: contract_last(): lax.dot_general(left_side, right_side, (((1,), (1,)), ((), ())), preferre...]
    while x24 -> x0, starting transfers between devices: 122 us -> none
  transfers between devices with their start and end apart: 33 -> 7, of which waited for: 17 -> 4; matrix products, arithmetic and copies ran while one was open for 65% -> 4% of each run, Pallas kernels for 0% -> 0%
where the time goes in v1:
time: 1570 us; the launch traced here: 1560 us
  Pallas kernels  654 us (42%)
  local copies, waits for them, and re-layouts  416 us (26%)
  blocking collectives  202 us (13%)
  other arithmetic  176 us (11%)
  waiting for transfers between devices  75.7 us (5%)
  between operations  15.8 us (1%)
    pallas_call x1, Pallas kernels, feed_forward(): pl.pallas_call(functools.partial(ffn_kernel, seq_count), out_shape=[jax.S...  654 us
    slice x49, local copies, waits for them, and re-layouts, shards(): lax.associative_scan(link_forward, (jnp.flip(next_decay, 1), jnp.flip(gra...  128 us
    all_gather x3, blocking collectives, prefix(): gathered = jax.tree.map(lambda a: lax.all_gather(a, axis), part)  123 us
    slice x44, local copies, waits for them, and re-layouts, shards(): lax.associative_scan(link_forward, (decay, pushed), axis=1)  102 us
    psum x1, blocking collectives, shards(): lax.psum((norm_gain_local, conv_weight_local, conv_bias_local, recur_weig...  78.9 us
    psum x1, waiting for transfers between devices, shards(): lax.psum((norm_gain_local, conv_weight_local, conv_bias_local, recur_weig...  47.8 us
    pad x24, local copies, waits for them, and re-layouts, shards(): lax.associative_scan(link_forward, (jnp.flip(next_decay, 1), jnp.flip(gra...  36.7 us
    pad x24, local copies, waits for them, and re-layouts, shards(): lax.associative_scan(link_forward, (decay, pushed), axis=1)  36.2 us
  transfers between devices with their start and end apart: 7, of which 4 were waited for; matrix products, arithmetic and copies ran while one was open for 4% of the time, Pallas kernels for 0%

profile of v1, /device:TPU:0, one launch (start us, length us, event | category | flops | bytes accessed | tf_op | source)
XLA Modules:
  0.0 1557.1 jit_solution(4575791063175221253)
XLA Ops:
  54.7 7.1 convert_multiply_fusion.10
  61.9 7.7 slice.506
  73.8 7.5 slice.507
  81.3 7.5 slice.508
  171.0 7.6 slice.554
  224.1 45.8 %all-gather.1 = f32[64,1,1280]{2,1,0:T(1,128)} all-gather(f32[4,1,1280]{2,1,0:T(1,128)S(1)} %slice_add_fusion.2), channel_id=3, replica_groups=mesh['seq'=16,'head'=2] {'seq'}, dimensions={0}, use_global_device_ids=true | all-gather | bytes 348160 | tf_op jit(solution)/shard_map/all_gather | solution.py:27
  288.2 39.5 %all-gather = f32[64,1,1280]{2,1,0:T(1,128)} all-gather(f32[4,1,1280]{2,1,0:T(1,128)S(1)} %slice_add_fusion.3), channel_id=2, replica_groups=mesh['seq'=16,'head'=2] {'seq'}, dimensions={0}, use_global_device_ids=true | all-gather | bytes 348160 | tf_op jit(solution)/shard_map/all_gather | solution.py:27
  341.5 21.2 %all-gather.8.cloned.1.call-done = bf16[4,128,2560]{1,0,2:T(4,128)(2,1)} async-done(((bf16[4,128,1280]{1,0,2:T(4,128)(2,1)}), bf16[4,128,2560]{1,0,2:T(4,128)(2,1)}) %all-gather.8.cloned.1.call-update) | async-done | bytes 2621456 | tf_op jit(solution)/shard_map/all_gather | solution.py:678
  373.2 653.9 %feed_forward.1 = (f32[512,1280]{1,0:T(8,128)}, f32[512,1280]{1,0:T(8,128)}, bf16[3,160,3840]{2,1,0:T(8,128)(2,1)}, bf16[4,3,2560,256]{3,2,1,0:T(8,128)(2,1)}, b...) custom-call(bf16[512,1280]{1,0:T(8,128)(2,1)} %constant_dynamic-slic, ...), custom_call_target="tpu_custom_call" | custom-call | flops 96636764160 | bytes 104857600 | tf_op jit(solution)/shard_map/feed_forward/pallas_call | solution.py:537
  1048.5 6.7 slice.582
  1055.2 6.4 slice.573
  1061.6 7.4 multiply_reduce_fusion
  1069.0 7.8 multiply_add_fusion
  1087.8 6.4 slice.577
  1183.4 6.5 slice.627
  1239.5 37.5 %all-gather.2 = f32[64,1,1280]{2,1,0:T(1,128)S(1)} all-gather(f32[4,1,1280]{2,1,0:T(1,128)S(1)} %add_multiply_fusion.20), channel_id=4, replica_groups=mesh['seq'=16,'head'=2] {'seq'}, dimensions={0}, use_global_device_ids=true | all-gather | bytes 348160 | tf_op jit(solution)/shard_map/all_gather | solution.py:27
  1277.9 11.6 while.27
  1301.8 13.0 rev.10
  1314.9 21.0 %rev.9 = f32[4,128,1280]{2,1,0:T(8,128)} reverse(f32[4,128,1280]{2,1,0:T(8,128)} %add.501), dimensions={1} | reverse | bytes 5242880 | tf_op jit(solution)/shard_map/jit(_flip)/rev | solution.py:708
  1336.0 8.9 multiply_reduce_fusion.3
  1375.7 7.5 fusion.14
  1412.5 78.9 %all-reduce.58 = (f32[2560]{0:T(1024)}, f32[4,1280]{1,0:T(4,128)}, f32[1280]{0:T(1024)}, f32[1280]{0:T(1024)}, f32[1280]{0:T(1024)}, /*index=5*/f32[1280]{0:T(1024)}, f32[2560]{0:T(1024)}) all-reduce(f32[2560]{0:T(1024)S(1)} %get-tuple-element.218, f32[4,1280]{1,0:T(4,128)S(1)} %pad_maximum_fusion.23, ...), channel_id=1, replica_groups=mesh['seq'=16,'head'=2] {'seq'}, use_global_device_ids=true, to_apply=%region_9.10 | all-reduce | flops 15360 | bytes 122880 | tf_op jit(solution)/shard_map/psum | solution.py:764
  1491.4 7.3 fusion.5
  1498.7 47.8 %all-reduce.62.cloned.1.call-done = (f32[5,256,256]{2,1,0:T(8,128)}, f32[5,256,256]{2,1,0:T(8,128)}) async-done(((f32[5,256,256]{2,1,0:T(8,128)}, f32[5,256,256]{2,1,0:T(8,128)}), (f32[5,256,256]{2,1,0:T(8,128)}, f32[5,256,256]{2,1,0:T(8,128)})) %all-reduce.62.cloned.1.call-update) | async-done | bytes 2621456 | tf_op jit(solution)/shard_map/psum | solution.py:764
  (490 shorter events, 480.0 us)
Async XLA Ops:
  7.2 26.5 %copy-start = (bf16[5,256,256]{2,1,0:T(8,128)(2,1)S(1)}, bf16[5,256,256]{2,1,0:T(8,128)(2,1)}, u32[]{:S(2)}) copy-start(bf16[5,256,256]{2,1,0:T(8,128)(2,1)} %param.22) | copy-start | bytes 1966084
  7.2 355.4 %all-gather.8.cloned.1.call-start = ((), (), s32[]{:S(2)}) async-start(), calls=%async_computation | async-start | bytes 3932160 | tf_op jit(solution)/shard_map/all_gather | solution.py:678
  16.2 6.4 collective-permute-start
  21.1 33.6 %copy-start.48 = (f32[1280]{0:T(1024)}, f32[1280]{0:T(1024)S(1)}, u32[]{:S(2)}) copy-start(f32[1280]{0:T(1024)S(1)} %fusion.42) | copy-start | bytes 15364
  21.2 33.5 %copy-start.40 = (f32[1280]{0:T(1024)}, f32[1280]{0:T(1024)S(1)}, u32[]{:S(2)}) copy-start(f32[1280]{0:T(1024)S(1)} %get-tuple-element.225) | copy-start | bytes 15364
  21.2 33.5 %copy-start.42 = (f32[1280]{0:T(1024)}, f32[1280]{0:T(1024)S(1)}, u32[]{:S(2)}) copy-start(f32[1280]{0:T(1024)S(1)} %get-tuple-element.226) | copy-start | bytes 15364
  21.2 33.5 %copy-start.44 = (f32[1280]{0:T(1024)}, f32[1280]{0:T(1024)S(1)}, u32[]{:S(2)}) copy-start(f32[1280]{0:T(1024)S(1)} %get-tuple-element.227) | copy-start | bytes 15364
  21.2 33.5 %copy-start.46 = (f32[1280]{0:T(1024)}, f32[1280]{0:T(1024)S(1)}, u32[]{:S(2)}) copy-start(f32[1280]{0:T(1024)S(1)} %get-tuple-element.228) | copy-start | bytes 15364
  24.3 30.4 %copy-start.1 = (f32[4,131,1280]{2,1,0:T(8,128)}, f32[4,131,1280]{2,1,0:T(8,128)S(1)}, u32[]{:S(2)}) copy-start(f32[4,131,1280]{2,1,0:T(8,128)S(1)} %maximum_convert_fusion) | copy-start | bytes 8048644
  341.4 26.5 %copy-start.4 = (bf16[4,128,2560]{2,1,0:T(8,128)(2,1)S(1)}, bf16[4,128,2560]{2,1,0:T(8,128)(2,1)}, u32[]{:S(2)}) copy-start(bf16[4,128,2560]{2,1,0:T(8,128)(2,1)} %param.18) | copy-start | bytes 7864324
  341.4 720.2 %all-gather.12.cloned.1.call-start = ((), (), s32[]{:S(2)}) async-start(), calls=%async_computation.2 | async-start | bytes 7864320 | tf_op jit(solution)/shard_map/all_gather | solution.py:689
  1027.1 41.9 %all-gather.10.cloned.1.call-start = ((), (), s32[]{:S(2)}) async-start(), calls=%async_computation.1 | async-start | bytes 7864320 | tf_op jit(solution)/shard_map/all_gather | solution.py:688
  1027.9 375.3 %all-gather.14.cloned.1.call-start = ((), (), s32[]{:S(2)}) async-start(), calls=%async_computation.3 | async-start | bytes 3932160 | tf_op jit(solution)/shard_map/all_gather | solution.py:756
  1239.5 50.0 %copy-start.26 = (f32[4,63,1280]{2,1,0:T(8,128)S(1)}, f32[4,63,1280]{2,1,0:T(8,128)}, u32[]{:S(2)}) copy-start(f32[4,63,1280]{2,1,0:T(8,128)} %get-tuple-element.277) | copy-start | bytes 3870724
  1314.8 21.1 %copy-start.41 = (f32[1280]{0:T(1024)S(1)}, f32[1280]{0:T(1024)}, u32[]{:S(2)}) copy-start(f32[1280]{0:T(1024)} %copy-done.40) | copy-start | bytes 15364
  1314.8 21.1 %copy-start.43 = (f32[1280]{0:T(1024)S(1)}, f32[1280]{0:T(1024)}, u32[]{:S(2)}) copy-start(f32[1280]{0:T(1024)} %copy-done.42) | copy-start | bytes 15364
  1314.8 21.1 %copy-start.45 = (f32[1280]{0:T(1024)S(1)}, f32[1280]{0:T(1024)}, u32[]{:S(2)}) copy-start(f32[1280]{0:T(1024)} %copy-done.44) | copy-start | bytes 15364
  1314.8 21.1 %copy-start.47 = (f32[1280]{0:T(1024)S(1)}, f32[1280]{0:T(1024)}, u32[]{:S(2)}) copy-start(f32[1280]{0:T(1024)} %copy-done.46) | copy-start | bytes 15364
  1314.8 21.1 %copy-start.49 = (f32[1280]{0:T(1024)S(1)}, f32[1280]{0:T(1024)}, u32[]{:S(2)}) copy-start(f32[1280]{0:T(1024)} %copy-done.48) | copy-start | bytes 15364
  1314.9 21.1 %copy-start.53 = (f32[1280]{0:T(1024)S(1)}, f32[1280]{0:T(1024)}, u32[]{:S(2)}) copy-start(f32[1280]{0:T(1024)} %param.21) | copy-start | bytes 15364
  1314.9 21.1 %copy-start.55 = (f32[1280]{0:T(1024)S(1)}, f32[1280]{0:T(1024)}, u32[]{:S(2)}) copy-start(f32[1280]{0:T(1024)} %param.25) | copy-start | bytes 15364
  1314.9 21.1 %copy-start.57 = (f32[1280]{0:T(1024)S(1)}, f32[1280]{0:T(1024)}, u32[]{:S(2)}) copy-start(f32[1280]{0:T(1024)} %param.23) | copy-start | bytes 15364
  1383.2 5.8 collective-permute-start.1
  1392.6 153.9 %all-reduce.62.cloned.1.call-start = ((), (), s32[]{:S(2)}) async-start(), calls=%async_computation.4 | async-start | bytes 5242880 | tf_op jit(solution)/shard_map/psum | solution.py:764
  (72 other events, 321.6 us)
Sparse Core Ops, SparseCore 0:
  341.5 21.0 all-gather.7
  1027.2 12.8 all-gather.11
  1041.7 16.3 all-gather.9
  1392.7 9.1 all-gather.13
  1407.9 138.5 all-reduce.61

commit v2 on v1

--- a/solution.py
+++ b/solution.py
@@ -549,73 +549,456 @@
     return results[0], results[1], results[2]
 
 
-def gathered_feed_forward(block_input, residual, xn_second, out_grad, w_gate, w_up, w_down):
-    model_width = block_input.shape[2]
-    token_rows = xn_second.shape[0]
-    hidden_width = w_gate.shape[1]
-    pieces = (
-        lax.all_gather(w_gate, "seq", axis=0, tiled=True),
-        lax.all_gather(w_up, "seq", axis=0, tiled=True),
-    )
-    columns = xn_second
-    gate = jnp.dot(columns, pieces[0], preferred_element_type=jnp.float32)
-    up_value = jnp.dot(columns, pieces[1], preferred_element_type=jnp.float32)
-    activated, gelu_back = jax.vjp(jax.nn.gelu, gate)
-    hidden = (activated * up_value).astype(jnp.bfloat16)
-    partial_mix = contract_last(hidden, lax.all_gather(w_down, "seq", axis=0, tiled=True))
-    mixed = lax.psum(partial_mix, "head")
-    block_output = (
-        (residual.reshape(token_rows, model_width) + mixed)
-        .astype(jnp.bfloat16)
-        .reshape(block_input.shape)
-    )
-    cotangent = out_grad.reshape(token_rows, model_width)
-    columns = cotangent
-    grad_hidden = jnp.dot(
-        columns,
-        lax.all_gather(w_down, "seq", axis=0, tiled=True),
-        preferred_element_type=jnp.float32,
-    )
-    grad_gate = gelu_back(grad_hidden * up_value)[0].astype(jnp.bfloat16)
-    grad_up = (grad_hidden * activated).astype(jnp.bfloat16)
-    pieces = (
-        lax.all_gather(w_gate, "seq", axis=0, tiled=True),
-        lax.all_gather(w_up, "seq", axis=0, tiled=True),
-    )
-    block_value = contract_last(grad_gate, pieces[0]) + contract_last(grad_up, pieces[1])
-    grad_xn_second = lax.psum(block_value, "head").reshape(block_input.shape)
-    stacked = jnp.concatenate([grad_gate, grad_up], axis=1)
-    local_rows = w_gate.shape[0]
-    seq_count = lax.axis_size("seq")
-    turns = math.gcd(local_rows, 8)
-    per_turn = local_rows // turns
-    input_view = xn_second.reshape(token_rows, seq_count, local_rows)
-    grad_view = cotangent.reshape(token_rows, seq_count, local_rows)
-
-    def grad_turn(turn, collected):
-        first_row = turn * per_turn
-        input_cols = lax.dynamic_slice_in_dim(input_view, first_row, per_turn, 2).reshape(
-            token_rows, seq_count * per_turn
-        )
-        grad_cols = lax.dynamic_slice_in_dim(grad_view, first_row, per_turn, 2).reshape(
-            token_rows, seq_count * per_turn
-        )
-        term = jnp.concatenate(
-            [contract_first(input_cols, stacked), contract_first(grad_cols, hidden)], axis=1
-        )
-        share = lax.psum_scatter(term, "seq", scatter_dimension=0, tiled=True)
-        return lax.dynamic_update_slice_in_dim(collected, share, first_row, 0)
-
-    weight_grads = lax.fori_loop(
-        0, turns, grad_turn, jnp.zeros((local_rows, 3 * hidden_width), jnp.float32)
-    )
-    w_gate_grad = weight_grads[:, :hidden_width]
-    w_up_grad = weight_grads[:, hidden_width : 2 * hidden_width]
-    w_down_grad = weight_grads[:, 2 * hidden_width :]
-    return block_output, grad_xn_second, w_gate_grad, w_up_grad, w_down_grad
-
-
-def shards(
+def half_window(head, half):
+    return pl.ds(pl.multiple_of(head * half, LANES), half)
+
+
+def greet(partners):
+    barrier = pltpu.get_barrier_semaphore()
+    for seq, head in partners:
+        pl.semaphore_signal(barrier, inc=1, device_id={"seq": seq, "head": head}, device_id_type=MESH)
+    return barrier
+
+
+def greet_all(seq_count, s, h):
+    barrier = pltpu.get_barrier_semaphore()
+
+    @pl.loop(1, seq_count)
+    def _(q):
+        seq = (s + q) % seq_count
+        pl.semaphore_signal(barrier, inc=1, device_id={"seq": seq, "head": h}, device_id_type=MESH)
+
+    pl.semaphore_signal(barrier, inc=1, device_id={"seq": s, "head": 1 - h}, device_id_type=MESH)
+    pl.semaphore_wait(barrier, seq_count)
+
+
+def one_minus_square(log_decay):
+    twice = 2.0 * log_decay
+    series = 1.0 + twice * (1 / 2 + twice * (1 / 6 + twice * (1 / 24 + twice * (1 / 120 + twice * (1 / 720)))))
+    return jnp.where(twice > -0.25, -twice * series, 1.0 - jnp.exp(twice))
+
+
+def shifted(value, step, keep, fill):
+    return jnp.where(keep, pltpu.roll(value, step % 8, 0), fill)
+
+
+def recur_forward_kernel(
+    seq_count, sequences, x_ref, gain_ref, cw_ref, cb_ref, rw_ref, rb_ref, iw_ref, ib_ref, rate_ref, mgain_ref,
+    xn2_ref, res_ref, scale_ref, state_ref, rg_ref, ig_ref, conv_ref, ext_ref,
+    a_ref, b_ref, halo, ends, ent, part, part_in, halo_s, halo_r, end_s, end_r, part_s, part_r,
+):
+    s = lax.axis_index("seq")
+    h = lax.axis_index("head")
+    rows, width = x_ref.shape
+    half = width // 2
+    span = rows // sequences
+    groups = span // 8
+    mine = half_window(h, half)
+    greet_all(seq_count, s, h)
+
+    def normed(r, count):
+        full = x_ref[pl.ds(r, count), :].astype(jnp.float32)
+        scale = lax.rsqrt(jnp.sum(full * full, axis=1, keepdims=True) * (1.0 / width) + EPS)
+        own = x_ref[pl.ds(r, count), mine].astype(jnp.float32)
+        return ((own * scale) * gain_ref[:, mine]).astype(jnp.bfloat16).astype(jnp.float32)
+
+    for q in range(sequences):
+        halo[0, q] = normed(q * span + span - 16, 16)[8:]
+    halo_out = remote(halo.at[0], halo.at[1], halo_s, halo_r, jnp.minimum(s + 1, seq_count - 1), h)
+    pl.when(s + 1 < seq_count)(halo_out.start)
+    for q in range(sequences):
+        @pl.loop(0, span // 16)
+        def _(i, q=q):
+            r = pl.multiple_of(i * 16, 16)
+            ext_ref[q, pl.ds(8 + r, 16), :] = normed(pl.multiple_of(q * span + r, 16), 16)
+
+    @pl.when(s > 0)
+    def _():
+        halo_out.wait_recv()
+        for q in range(sequences):
+            ext_ref[q, pl.ds(0, 8), :] = halo[1, q]
+
+    @pl.when(s == 0)
+    def _():
+        for q in range(sequences):
+            ext_ref[q, pl.ds(0, 8), :] = jnp.zeros((8, half), jnp.float32)
+
+    block = rw_ref.shape[1]
+
+    @pl.loop(0, half // block)
+    def _(n):
+        lanes = pl.ds(pl.multiple_of(n * block, block), block)
+        for q in range(sequences):
+            total = cb_ref[:, lanes]
+            for k in range(4):
+                total = total + cw_ref[pl.ds(k, 1), lanes] * ext_ref[q, pl.ds(8 - k, span), lanes]
+            conv_ref[pl.ds(q * span, span), lanes] = total.astype(jnp.bfloat16)
+        low = conv_ref[:, lanes]
+        rg_ref[:, lanes] = jax.nn.sigmoid(dot_nn(low, rw_ref[n]) + rb_ref[:, lanes])
+        ig_ref[:, lanes] = jax.nn.sigmoid(dot_nn(low, iw_ref[n]) + ib_ref[:, lanes])
+
+        @pl.loop(0, rows // 64)
+        def _(i):
+            r = pl.ds(pl.multiple_of(i * 64, 64), 64)
+            log_decay = -8.0 * rate_ref[:, lanes] * rg_ref[r, lanes]
+            a_ref[r, lanes] = jnp.exp(log_decay)
+            mult = jnp.sqrt(one_minus_square(log_decay))
+            b_ref[r, lanes] = mult * ig_ref[r, lanes] * conv_ref[r, lanes].astype(jnp.float32)
+
+    row_ids = lax.broadcasted_iota(jnp.int32, (8, half), 0)
+
+    def scan_group(g, carry):
+        out = []
+        for q in range(sequences):
+            r = pl.ds(pl.multiple_of(q * span + g * 8, 8), 8)
+            a, b = a_ref[r, :], b_ref[r, :]
+            for k in (1, 2, 4):
+                keep = row_ids >= k
+                b = b + a * shifted(b, k, keep, 0.0)
+                a = a * shifted(a, k, keep, 1.0)
+            b = b + a * carry[2 * q]
+            a = a * carry[2 * q + 1]
+            a_ref[r, :] = a
+            b_ref[r, :] = b
+            out += [b[7:8], a[7:8]]
+        return tuple(out)
+
+    first = []
+    for q in range(sequences):
+        first += [jnp.zeros((1, half), jnp.float32), jnp.ones((1, half), jnp.float32)]
+    last = lax.fori_loop(0, groups, scan_group, tuple(first))
+    for q in range(sequences):
+        part_end = pl.ds(q, 1)
+        ends[s, part_end, :] = last[2 * q + 1]
+        ends[s, pl.ds(sequences + q, 1), :] = last[2 * q]
+
+    def end_copy(target, source):
+        return remote(ends.at[source], ends.at[source], end_s.at[target], end_r.at[source], target, h)
+
+    @pl.loop(1, seq_count)
+    def _(q):
+        pl.when(s + q < seq_count)(lambda: end_copy(s + q, s).start())
+
+    ent[...] = jnp.zeros_like(ent)
+
+    @pl.loop(0, seq_count)
+    def _(source):
+        @pl.when(source < s)
+        def _():
+            end_copy(s, source).wait_recv()
+            got = ends[source]
+            ent[...] = got[:sequences] * ent[...] + got[sequences:]
+
+    for q in range(sequences):
+        entering = ent[pl.ds(q, 1), :]
+        state_ref[q, pl.ds(0, 8), :] = jnp.broadcast_to(entering, (8, half))
+
+        @pl.loop(0, span // 16)
+        def _(i, q=q, entering=entering):
+            t = pl.multiple_of(i * 16, 16)
+            r = pl.ds(pl.multiple_of(q * span + t, 16), 16)
+            state = b_ref[r, :] + a_ref[r, :] * ent[pl.ds(q, 1), :]
+            state_ref[q, pl.ds(8 + t, 16), :] = state
+            residual = x_ref[r, mine].astype(jnp.float32) + state.astype(jnp.bfloat16).astype(jnp.float32)
+            res_ref[r, :] = residual
+            part[r, :] = jnp.broadcast_to(jnp.sum(residual * residual, axis=1, keepdims=True), (16, LANES))
+
+    other = remote(part, part_in, part_s, part_r, s, 1 - h)
+    other.start()
+    other.wait_recv()
+
+    @pl.loop(0, rows // 16)
+    def _(i):
+        r = pl.ds(pl.multiple_of(i * 16, 16), 16)
+        scale = lax.rsqrt((part[r, :] + part_in[r, :]) * (1.0 / width) + EPS)
+        scale_ref[r, :] = scale
+        xn2_ref[r, :] = ((res_ref[r, :] * scale[:, :1]) * mgain_ref[:, mine]).astype(jnp.bfloat16)
+
+    other.wait_send()
+    pl.when(s + 1 < seq_count)(halo_out.wait_send)
+
+    @pl.loop(1, seq_count)
+    def _(q):
+        pl.when(s + q < seq_count)(lambda: end_copy(s + q, s).wait_send())
+
+
+def recur_backward_kernel(
+    seq_count, sequences, gx_ref, g_ref, x_ref, res_ref, scale_ref, state_ref, rg_ref, ig_ref, conv_ref, ext_ref,
+    gain_ref, cw_ref, rw_ref, iw_ref, rate_ref, sig_ref, mgain_ref,
+    out_ref, vec_ref, rwg_ref, iwg_ref,
+    gres, dec, adj, gconv, halo, ends, arr, part, part_in, fin,
+    halo_s, halo_r, end_s, end_r, part_s, part_r, fin_s, fin_r, loc,
+):
+    s = lax.axis_index("seq")
+    h = lax.axis_index("head")
+    rows, half = gx_ref.shape
+    width = 2 * half
+    span = rows // sequences
+    groups = span // 8
+    mine = half_window(h, half)
+    greet_all(seq_count, s, h)
+    vec_ref[...] = jnp.zeros_like(vec_ref)
+    other = [remote(part.at[i], part_in.at[i], part_s.at[i], part_r.at[i], s, 1 - h) for i in range(2)]
+
+    @pl.loop(0, rows // 16)
+    def _(i):
+        r = pl.ds(pl.multiple_of(i * 16, 16), 16)
+        hat = res_ref[r, :] * scale_ref[r, :1]
+        product = gx_ref[r, :] * hat
+        vec_ref[pl.ds(9, 1), :] += jnp.sum(product, axis=0, keepdims=True)
+        part[0, r, :] = jnp.broadcast_to(jnp.sum(product * mgain_ref[:, mine], axis=1, keepdims=True), (16, LANES))
+
+    other[0].start()
+    for q in range(sequences):
+        @pl.loop(0, span // 16)
+        def _(i, q=q):
+            t = pl.multiple_of(i * 16, 16)
+            r = pl.ds(pl.multiple_of(q * span + t, 16), 16)
+            dec[q, pl.ds(t, 16), :] = jnp.exp(-8.0 * rate_ref[...] * rg_ref[r, :])
+    other[0].wait_recv()
+
+    @pl.loop(0, rows // 16)
+    def _(i):
+        r = pl.ds(pl.multiple_of(i * 16, 16), 16)
+        scale = scale_ref[r, :1]
+        hat = res_ref[r, :] * scale
+        mean = ((part[0, r, :] + part_in[0, r, :]) * (1.0 / width))[:, :1]
+        gres[r, :] = g_ref[r, mine].astype(jnp.float32) + scale * (gx_ref[r, :] * mgain_ref[:, mine] - hat * mean)
+
+    row_ids = lax.broadcasted_iota(jnp.int32, (8, half), 0)
+
+    def scan_group(i, carry):
+        g = groups - 1 - i
+        out = []
+        for q in range(sequences):
+            t = pl.multiple_of(g * 8, 8)
+            r = pl.ds(pl.multiple_of(q * span + t, 8), 8)
+            here = dec[q, pl.ds(t, 8), :]
+            a, b = shifted(here, -1, row_ids < 7, carry[3 * q + 2]), gres[r, :]
+            for k in (1, 2, 4):
+                keep = row_ids < 8 - k
+                b = b + a * shifted(b, -k, keep, 0.0)
+                a = a * shifted(a, -k, keep, 1.0)
+            b = b + a * carry[3 * q]
+            a = a * carry[3 * q + 1]
+            fin[r, :] = a
+            adj[r, :] = b
+            out += [b[:1], a[:1], here[:1]]
+        return tuple(out)
+
+    first = []
+    for q in range(sequences):
+        one = jnp.ones((1, half), jnp.float32)
+        first += [jnp.zeros((1, half), jnp.float32), one, one]
+    last = lax.fori_loop(0, groups, scan_group, tuple(first))
+    for q in range(sequences):
+        ends[s, pl.ds(q, 1), :] = last[3 * q + 1] * last[3 * q + 2]
+        ends[s, pl.ds(sequences + q, 1), :] = last[3 * q] * last[3 * q + 2]
+
+    def end_copy(target, source):
+        return remote(ends.at[source], ends.at[source], end_s.at[target], end_r.at[source], target, h)
+
+    @pl.loop(1, seq_count)
+    def _(q):
+        pl.when(s >= q)(lambda: end_copy(jnp.maximum(s - q, 0), s).start())
+
+    arr[...] = jnp.zeros_like(arr)
+
+    @pl.loop(1, seq_count)
+    def _(q):
+        source = seq_count - q
+
+        @pl.when(source > s)
+        def _():
+            end_copy(s, source).wait_recv()
+            got = ends[source]
+            arr[...] = got[:sequences] * arr[...] + got[sequences:]
+
+    for q in range(sequences):
+        @pl.loop(0, span // 16)
+        def _(i, q=q):
+            r = pl.ds(pl.multiple_of(q * span + i * 16, 16), 16)
+            adj[r, :] += fin[r, :] * arr[pl.ds(q, 1), :]
+
+    block = rw_ref.shape[1]
+
+    @pl.loop(0, half // block)
+    def _(n):
+        lanes = pl.ds(pl.multiple_of(n * block, block), block)
+        rate = rate_ref[:, lanes]
+        sums = [jnp.zeros((1, block), jnp.float32)] * 3
+        for q in range(sequences):
+            for i in range(2):
+                t = i * (span // 2)
+                count = span // 2
+                r = pl.ds(q * span + t, count)
+                rg, ig, conv = rg_ref[r, lanes], ig_ref[r, lanes], conv_ref[r, lanes].astype(jnp.float32)
+                a = adj[r, lanes]
+                decay = dec[q, pl.ds(t, count), lanes]
+                mult = jnp.sqrt(one_minus_square(-8.0 * rate * rg))
+                previous = state_ref[q, pl.ds(7 + t, count), lanes]
+                grad_mult = a * ig * conv
+                grad_log = a * previous * decay - grad_mult * decay * decay / mult
+                pre_r = (grad_log * (-8.0 * rate) * rg * (1.0 - rg)).astype(jnp.bfloat16)
+                pre_i = (a * mult * conv * ig * (1.0 - ig)).astype(jnp.bfloat16)
+                sums[0] = sums[0] + jnp.sum(grad_log * rg, axis=0, keepdims=True)
+                sums[1] = sums[1] + jnp.sum(pre_r.astype(jnp.float32), axis=0, keepdims=True)
+                sums[2] = sums[2] + jnp.sum(pre_i.astype(jnp.float32), axis=0, keepdims=True)
+                back = contract_last(pre_r, rw_ref[n]) + contract_last(pre_i, iw_ref[n])
+                gconv[q, pl.ds(t, count), lanes] = (
+                    (a * mult * ig + back).astype(jnp.bfloat16).astype(jnp.float32)
+                )
+                low = conv_ref[r, lanes]
+                if q == 0 and i == 0:
+                    rwg_ref[n] = contract_first(low, pre_r)
+                    iwg_ref[n] = contract_first(low, pre_i)
+                else:
+                    rwg_ref[n] += contract_first(low, pre_r)
+                    iwg_ref[n] += contract_first(low, pre_i)
+        vec_ref[pl.ds(8, 1), lanes] = sums[0] * 8.0 * sig_ref[:, lanes]
+        vec_ref[pl.ds(6, 1), lanes] = sums[1]
+        vec_ref[pl.ds(7, 1), lanes] = sums[2]
+
+    for q in range(sequences):
+        halo[0, q] = gconv[q, pl.ds(0, 8), :]
+    halo_out = remote(halo.at[0], halo.at[1], halo_s, halo_r, jnp.maximum(s - 1, 0), h)
+    pl.when(s > 0)(halo_out.start)
+
+    @pl.loop(0, half // block)
+    def _(n):
+        lanes = pl.ds(pl.multiple_of(n * block, block), block)
+        for k in range(5):
+            total = jnp.zeros((1, block), jnp.float32)
+            for q in range(sequences):
+                value = gconv[q, pl.ds(0, span), lanes]
+                if k < 4:
+                    value = value * ext_ref[q, pl.ds(8 - k, span), lanes]
+                total = total + jnp.sum(value, axis=0, keepdims=True)
+            vec_ref[pl.ds(1 + k, 1), lanes] = total
+
+    @pl.when(s + 1 < seq_count)
+    def _():
+        halo_out.wait_recv()
+        for q in range(sequences):
+            gconv[q, pl.ds(span, 8), :] = halo[1, q]
+
+    @pl.when(s + 1 == seq_count)
+    def _():
+        for q in range(sequences):
+            gconv[q, pl.ds(span, 8), :] = jnp.zeros((8, half), jnp.float32)
+
+    @pl.loop(0, half // block)
+    def _(n):
+        lanes = pl.ds(pl.multiple_of(n * block, block), block)
+        for q in range(sequences):
+            total = cw_ref[pl.ds(0, 1), lanes] * gconv[q, pl.ds(0, span), lanes]
+            for k in range(1, 4):
+                total = total + cw_ref[pl.ds(k, 1), lanes] * gconv[q, pl.ds(k, span), lanes]
+            adj[pl.ds(q * span, span), lanes] = total
+
+    def first_norm(r):
+        full = x_ref[r, :].astype(jnp.float32)
+        scale = lax.rsqrt(jnp.sum(full * full, axis=1, keepdims=True) * (1.0 / width) + EPS)
+        return scale, x_ref[r, mine].astype(jnp.float32) * scale
+
+    for q in range(sequences):
+        @pl.loop(0, span // 16)
+        def _(i, q=q):
+            t = pl.multiple_of(i * 16, 16)
+            r = pl.ds(pl.multiple_of(q * span + t, 16), 16)
+            product = adj[r, :] * first_norm(r)[1]
+            vec_ref[pl.ds(0, 1), :] += jnp.sum(product, axis=0, keepdims=True)
+            part[1, r, :] = jnp.broadcast_to(
+                jnp.sum(product * gain_ref[:, mine], axis=1, keepdims=True), (16, LANES)
+            )
+    other[1].start()
+    other[1].wait_recv()
+
+    @pl.loop(0, rows // 16)
+    def _(i):
+        r = pl.ds(pl.multiple_of(i * 16, 16), 16)
+        scale, hat = first_norm(r)
+        mean = ((part[1, r, :] + part_in[1, r, :]) * (1.0 / width))[:, :1]
+        fin[r, :] = gres[r, :] + scale * (adj[r, :] * gain_ref[:, mine] - hat * mean)
+
+    near = pltpu.make_async_copy(fin, out_ref.at[:, mine], loc)
+    near.start()
+    away = remote(fin, out_ref.at[:, mine], fin_s, fin_r, s, 1 - h)
+    away.start()
+    for i in range(2):
+        other[i].wait_send()
+    pl.when(s > 0)(halo_out.wait_send)
+
+    @pl.loop(1, seq_count)
+    def _(q):
+        pl.when(s >= q)(lambda: end_copy(jnp.maximum(s - q, 0), s).wait_send())
+
+    near.wait()
+    away.wait()
+
+
+def recur_forward(seq_count, sequences, x, norm_gain, conv_weight, conv_bias, recur_weight, recur_bias, input_weight,
+                  input_bias, rate, mlp_gain):
+    rows, width = x.shape
+    half = width // 2
+    span = rows // sequences
+    bf, f32 = jnp.bfloat16, jnp.float32
+    sem = pltpu.SemaphoreType.DMA
+    vmem = pl.BlockSpec(memory_space=pltpu.VMEM)
+    outs = [
+        ((rows, half), bf), ((rows, half), f32), ((rows, LANES), f32), ((sequences, span + 8, half), f32),
+        ((rows, half), f32), ((rows, half), f32), ((rows, half), bf), ((sequences, span + 8, half), f32),
+    ]
+    return pl.pallas_call(
+        functools.partial(recur_forward_kernel, seq_count, sequences),
+        out_shape=[jax.ShapeDtypeStruct(shape, kind) for shape, kind in outs],
+        in_specs=[vmem] * 10,
+        out_specs=[vmem] * len(outs),
+        scratch_shapes=[
+            pltpu.VMEM((rows, half), f32), pltpu.VMEM((rows, half), f32), pltpu.VMEM((2, sequences, 8, half), f32),
+            pltpu.VMEM((seq_count, 2 * sequences, half), f32), pltpu.VMEM((sequences, half), f32),
+            pltpu.VMEM((rows, LANES), f32), pltpu.VMEM((rows, LANES), f32),
+            sem, sem, sem((seq_count,)), sem((seq_count,)), sem, sem,
+        ],
+        compiler_params=pltpu.CompilerParams(
+            collective_id=1, has_side_effects=True, vmem_limit_bytes=60 * 2**20
+        ),
+        name="recur_forward",
+    )(x, norm_gain[None], conv_weight, conv_bias[None], recur_weight, recur_bias[None], input_weight, input_bias[None],
+      rate[None], mlp_gain[None])
+
+
+def recur_backward(seq_count, sequences, grad_half, cotangent, x, saved, norm_gain, conv_weight, recur_weight,
+                   input_weight, rate, slope, mlp_gain):
+    rows, width = x.shape
+    half = width // 2
+    span = rows // sequences
+    bf, f32 = jnp.bfloat16, jnp.float32
+    sem = pltpu.SemaphoreType.DMA
+    vmem = pl.BlockSpec(memory_space=pltpu.VMEM)
+    outs = [((rows, width), f32), ((16, half), f32), (recur_weight.shape, f32), (recur_weight.shape, f32)]
+    args = (grad_half, cotangent, x, *saved, norm_gain[None], conv_weight, recur_weight, input_weight, rate[None],
+            slope[None], mlp_gain[None])
+    return pl.pallas_call(
+        functools.partial(recur_backward_kernel, seq_count, sequences),
+        out_shape=[jax.ShapeDtypeStruct(shape, kind) for shape, kind in outs],
+        in_specs=[vmem] * len(args),
+        out_specs=[pl.BlockSpec(memory_space=pl.ANY)] + [vmem] * 3,
+        scratch_shapes=[
+            pltpu.VMEM((rows, half), f32), pltpu.VMEM((sequences, span, half), f32), pltpu.VMEM((rows, half), f32),
+            pltpu.VMEM((sequences, span + 8, half), f32), pltpu.VMEM((2, sequences, 8, half), f32),
+            pltpu.VMEM((seq_count, 2 * sequences, half), f32), pltpu.VMEM((sequences, half), f32),
+            pltpu.VMEM((2, rows, LANES), f32), pltpu.VMEM((2, rows, LANES), f32), pltpu.VMEM((rows, half), f32),
+            sem, sem, sem((seq_count,)), sem((seq_count,)), sem((2,)), sem((2,)), sem, sem, sem,
+        ],
+        compiler_params=pltpu.CompilerParams(
+            collective_id=2, has_side_effects=True, vmem_limit_bytes=60 * 2**20
+        ),
+        name="recur_backward",
+    )(*args)
+
+
+def gathered_shards(
     block_input,
     norm_gain,
     conv_weight,
@@ -679,20 +1062,66 @@
     residual = stream + state_full.astype(jnp.float32)
     second_scale, second_hat = norm_rows(residual)
     xn_second = (second_hat * mlp_gain).astype(jnp.bfloat16).reshape(token_rows, model_width)
+    hidden_width = w_gate.shape[1]
+    pieces = (
+        lax.all_gather(w_gate, "seq", axis=0, tiled=True),
+        lax.all_gather(w_up, "seq", axis=0, tiled=True),
+    )
+    columns = xn_second
+    gate = jnp.dot(columns, pieces[0], preferred_element_type=jnp.float32)
+    up_value = jnp.dot(columns, pieces[1], preferred_element_type=jnp.float32)
+    activated, gelu_back = jax.vjp(jax.nn.gelu, gate)
+    hidden = (activated * up_value).astype(jnp.bfloat16)
+    partial_mix = contract_last(hidden, lax.all_gather(w_down, "seq", axis=0, tiled=True))
+    mixed = lax.psum(partial_mix, "head")
+    block_output = (
+        (residual.reshape(token_rows, model_width) + mixed)
+        .astype(jnp.bfloat16)
+        .reshape(block_input.shape)
+    )
+    cotangent = out_grad.reshape(token_rows, model_width)
+    columns = cotangent
+    grad_hidden = jnp.dot(
+        columns,
+        lax.all_gather(w_down, "seq", axis=0, tiled=True),
+        preferred_element_type=jnp.float32,
+    )
+    grad_gate = gelu_back(grad_hidden * up_value)[0].astype(jnp.bfloat16)
+    grad_up = (grad_hidden * activated).astype(jnp.bfloat16)
+    pieces = (
+        lax.all_gather(w_gate, "seq", axis=0, tiled=True),
+        lax.all_gather(w_up, "seq", axis=0, tiled=True),
+    )
+    block_value = contract_last(grad_gate, pieces[0]) + contract_last(grad_up, pieces[1])
+    grad_xn_second = lax.psum(block_value, "head").reshape(block_input.shape)
+    stacked = jnp.concatenate([grad_gate, grad_up], axis=1)
+    local_rows = w_gate.shape[0]
     seq_count = lax.axis_size("seq")
-    if seq_count % 8 == 0 and w_gate.shape[0] % 32 == 0:
-        xn_half = lax.dynamic_slice_in_dim(xn_second, head_at * lru_width, lru_width, 1)
-        mixed_half, grad_half, weight_grads = feed_forward(
-            seq_count, xn_half, out_grad.reshape(token_rows, model_width), w_gate, w_up, w_down
-        )
-        mixed = lax.all_gather(mixed_half, "head", axis=1, tiled=True).reshape(block_input.shape)
-        grad_xn_second = lax.all_gather(grad_half, "head", axis=1, tiled=True).reshape(block_input.shape)
-        block_output = (residual + mixed).astype(jnp.bfloat16)
-        w_gate_grad, w_up_grad, w_down_grad = [weight_grads[w].astype(jnp.float32) for w in range(3)]
-    else:
-        block_output, grad_xn_second, w_gate_grad, w_up_grad, w_down_grad = gathered_feed_forward(
-            block_input, residual, xn_second, out_grad, w_gate, w_up, w_down
-        )
+    turns = math.gcd(local_rows, 8)
+    per_turn = local_rows // turns
+    input_view = xn_second.reshape(token_rows, seq_count, local_rows)
+    grad_view = cotangent.reshape(token_rows, seq_count, local_rows)
+
+    def grad_turn(turn, collected):
+        first_row = turn * per_turn
+        input_cols = lax.dynamic_slice_in_dim(input_view, first_row, per_turn, 2).reshape(
+            token_rows, seq_count * per_turn
+        )
+        grad_cols = lax.dynamic_slice_in_dim(grad_view, first_row, per_turn, 2).reshape(
+            token_rows, seq_count * per_turn
+        )
+        term = jnp.concatenate(
+            [contract_first(input_cols, stacked), contract_first(grad_cols, hidden)], axis=1
+        )
+        share = lax.psum_scatter(term, "seq", scatter_dimension=0, tiled=True)
+        return lax.dynamic_update_slice_in_dim(collected, share, first_row, 0)
+
+    weight_grads = lax.fori_loop(
+        0, turns, grad_turn, jnp.zeros((local_rows, 3 * hidden_width), jnp.float32)
+    )
+    w_gate_grad = weight_grads[:, :hidden_width]
+    w_up_grad = weight_grads[:, hidden_width : 2 * hidden_width]
+    w_down_grad = weight_grads[:, 2 * hidden_width :]
     weighted_second = grad_xn_second * mlp_gain
     mlp_gain_local = jnp.sum(grad_xn_second * second_hat, axis=(0, 1))
     grad_residual = out_grad.astype(jnp.float32) + second_scale * (
@@ -790,6 +1219,65 @@
         w_gate_grad,
         w_up_grad,
         w_down_grad,
+    )
+
+
+def shards(
+    block_input,
+    norm_gain,
+    conv_weight,
+    conv_bias,
+    recur_weight,
+    recur_bias,
+    input_weight,
+    input_bias,
+    decay_param,
+    mlp_gain,
+    w_gate,
+    w_up,
+    w_down,
+    out_grad,
+):
+    seq_count = lax.axis_size("seq")
+    sequences, span_len, width = block_input.shape
+    if seq_count % 8 or w_gate.shape[0] % 32:
+        return gathered_shards(
+            block_input, norm_gain, conv_weight, conv_bias, recur_weight, recur_bias, input_weight, input_bias,
+            decay_param, mlp_gain, w_gate, w_up, w_down, out_grad,
+        )
+    rows = sequences * span_len
+    stream = block_input.reshape(rows, width)
+    cotangent = out_grad.reshape(rows, width)
+    rate = jax.nn.softplus(-decay_param)
+    slope = jax.nn.sigmoid(-decay_param)
+    xn_half, *saved = recur_forward(
+        seq_count, sequences, stream, norm_gain, conv_weight, conv_bias, recur_weight, recur_bias, input_weight,
+        input_bias, rate, mlp_gain,
+    )
+    mixed_half, grad_half, weight_grads = feed_forward(seq_count, xn_half, cotangent, w_gate, w_up, w_down)
+    block_half = (saved[0] + mixed_half).astype(jnp.bfloat16)
+    block_output = lax.all_gather(block_half, "head", axis=1, tiled=True).reshape(block_input.shape)
+    input_grad, vectors, recur_local, input_local = recur_backward(
+        seq_count, sequences, grad_half, cotangent, stream, saved, norm_gain, conv_weight, recur_weight,
+        input_weight, rate, slope, mlp_gain,
+    )
+    vectors, recur_weight_grad, input_weight_grad = lax.psum((vectors, recur_local, input_local), "seq")
+    gains = lax.all_gather(jnp.stack([vectors[0], vectors[9]]), "head", axis=1, tiled=True)
+    return (
+        block_output,
+        input_grad.reshape(block_input.shape),
+        gains[0],
+        vectors[1:5],
+        vectors[5],
+        recur_weight_grad,
+        vectors[6],
+        input_weight_grad,
+        vectors[7],
+        vectors[8],
+        gains[1],
+        weight_grads[0].astype(jnp.float32),
+        weight_grads[1].astype(jnp.float32),
+        weight_grads[2].astype(jnp.float32),
     )
 
 

time: 1570 us -> 957 us (0.61)
  local copies, waits for them, and re-layouts: 416 us -> 20.5 us
  blocking collectives: 202 us -> 1.82 us
  other arithmetic: 176 us -> 9.79 us
  Pallas kernels: 654 us -> 777 us
  waiting for transfers between devices: 75.7 us -> 131 us
    slice x99 -> x3, local copies, waits for them, and re-layouts: 230 us -> 3.63 us  [the longest x1 1.6 us: shards(): vectors[8]]
    all_gather x3 -> x1, blocking collectives: 123 us -> 1.82 us  [shards(): lax.all_gather(jnp.stack([vectors[0], vectors[9]]), 'head', axis=1, tiled...]
    pallas_call x0 -> x2, Pallas kernels: none -> 114 us  [the longest x1 76.3 us: recur_backward(): pl.pallas_call(functools.partial(recur_backward_kernel, seq_count, sequen...]
    psum x1, waiting for transfers between devices: 47.8 us -> 131 us  [shards(): lax.psum((vectors, recur_local, input_local), 'seq')]
    psum x1 -> x0, blocking collectives: 78.9 us -> none  [shards(): lax.psum((norm_gain_local, conv_weight_local, conv_bias_local, recur_weig...]
    pad x48 -> x0, local copies, waits for them, and re-layouts: 72.9 us -> none  [the longest x24 36.7 us: shards(): lax.associative_scan(link_forward, (jnp.flip(next_decay, 1), jnp.flip(gra...]
    add x55 -> x0, other arithmetic: 66.3 us -> none  [the longest x11 17.5 us: link_forward(): return (earlier[0] * latter[0], latter[0] * earlier[1] + latter[1])]
    reduce_sum x7 -> x0, other arithmetic: 38.6 us -> none  [the longest x1 8.89 us: shards(): jnp.sum(grad_log * 8.0 * recur_gate, axis=(0, 1))]
  transfers between devices with their start and end apart: 7 -> 2, of which waited for: 4 -> 1; matrix products, arithmetic and copies ran while one was open for 4% -> 1% of each run, Pallas kernels for 0% -> 8%
where the time goes in v2:
time: 957 us; the launch traced here: 956 us
  Pallas kernels  777 us (81%)
  waiting for transfers between devices  131 us (14%)
  local copies, waits for them, and re-layouts  20.5 us (2%)
  between operations  15.5 us (2%)
  other arithmetic  9.79 us (1%)
    pallas_call x1, Pallas kernels, feed_forward(): pl.pallas_call(functools.partial(ffn_kernel, seq_count), out_shape=[jax.S...  662 us
    psum x1, waiting for transfers between devices, shards(): lax.psum((vectors, recur_local, input_local), 'seq')  131 us
    pallas_call x1, Pallas kernels, recur_backward(): pl.pallas_call(functools.partial(recur_backward_kernel, seq_count, sequen...  76.3 us
    pallas_call x1, Pallas kernels, recur_forward(): pl.pallas_call(functools.partial(recur_forward_kernel, seq_count, sequenc...  38 us
  transfers between devices with their start and end apart: 2, of which 1 were waited for; matrix products, arithmetic and copies ran while one was open for 1% of the time, Pallas kernels for 8%

profile of v2, /device:TPU:0, one launch (start us, length us, event | category | flops | bytes accessed | tf_op | source)
XLA Modules:
  0.0 955.5 jit_solution(3297934531887200967)
XLA Ops:
  8.1 1.3 broadcast_in_dim.25.cb_ref
  9.4 1.3 broadcast_in_dim.26.rb_ref
  10.6 1.3 broadcast_in_dim.27.ib_ref
  11.9 1.3 broadcast_in_dim.24.gain_ref
  13.2 1.3 broadcast_in_dim.29.mgain_ref
  14.6 0.7 add_divide_fusion
  15.3 0.6 broadcast_in_dim.28.rate_ref
  15.9 38.0 %recur_forward.1 = (bf16[512,1280]{1,0:T(8,128)(2,1)}, f32[512,1280]{1,0:T(8,128)}, f32[512,128]{1,0:T(8,128)}, f32[4,136,1280]{2,1,0:T(8,128)}, f32[512,1280]{1...) custom-call(bf16[512,2560]{1,0:T(8,128)(2,1)} %bitcast.13, ...), custom_call_target="tpu_custom_call" | custom-call | tf_op jit(solution)/shard_map/recur_forward/pallas_call | solution.py:952
  53.9 662.1 %feed_forward.1 = (f32[512,1280]{1,0:T(8,128)}, f32[512,1280]{1,0:T(8,128)}, bf16[3,160,3840]{2,1,0:T(8,128)(2,1)}, bf16[4,3,2560,256]{3,2,1,0:T(8,128)(2,1)}, b...) custom-call(bf16[512,1280]{1,0:T(8,128)(2,1)} %get-tuple-element.30., ...), custom_call_target="tpu_custom_call" | custom-call | flops 96636764160 | bytes 104857600 | tf_op jit(solution)/shard_map/feed_forward/pallas_call | solution.py:537
  716.1 3.8 add_convert_fusion
  720.2 0.6 broadcast_in_dim.30.sig_ref
  720.8 76.3 %recur_backward.1 = (f32[512,2560]{1,0:T(8,128)}, f32[16,1280]{1,0:T(8,128)}, f32[5,256,256]{2,1,0:T(8,128)}, f32[5,256,256]{2,1,0:T(8,128)}) custom-call(f32[512,1280]{1,0:T(8,128)} %get-tuple-element.32.gx_ref, bf16[512,2560]{1,0:T(8,128)(2,1)} %bitcast.18, bf16[512,2560]{1,0:T(8,128)(2,1)} %bitcast.14, f32[512,1280]{1,0:T(8,128)} %get-tuple-element.29.res_ref, ...), custom_call_target="tpu_custom_call" | custom-call | tf_op jit(solution)/shard_map/recur_backward/pallas_call | solution.py:982
  797.1 5.2 bitcast_convert_fusion
  802.4 131.1 %all-reduce.3.cloned.1.call-done = (f32[16,1280]{1,0:T(8,128)}, f32[5,256,256]{2,1,0:T(8,128)}, f32[5,256,256]{2,1,0:T(8,128)}) async-done(((f32[16,1280]{1,0:T(8,128)}, f32[5,256,256]{2,1,0:T(8,128)}, f32[5,256,256]{2,1,0:T(8,128)}), (f32[16,1280]{1,0:T(8,128)}, f32[5,256,256]{2,1,0:T(8,128)}, f32[5,256,256]{2,1,0:T(8,128)})) %all-reduce.3.cloned.1.call-update) | async-done | bytes 2703376 | tf_op jit(solution)/shard_map/psum | solution.py:1264
  933.5 1.4 slice.51
  934.8 1.6 slice_reduce_fusion.2
  936.5 1.8 all_gather.7
  938.3 0.7 slice_reduce_fusion
  938.9 3.6 copy.35
  942.5 0.4 copy-done
  942.9 2.4 copy.36
  945.2 1.1 copy.37
  946.3 0.7 copy-done.1
  947.0 1.1 copy.38
  (10 shorter events, 0.3 us)
Async XLA Ops:
  8.0 794.4 %all-gather.2.cloned.1.call-start = ((), (), s32[]{:S(2)}) async-start(), calls=%async_computation | async-start | bytes 3932160 | tf_op jit(solution)/shard_map/all_gather | solution.py:1259
  719.9 213.5 %all-reduce.3.cloned.1.call-start = ((), (), s32[]{:S(2)}) async-start(), calls=%async_computation.1 | async-start | bytes 5406720 | tf_op jit(solution)/shard_map/psum | solution.py:1264
  938.9 3.9 copy-start
  942.9 2.4 copy-start.2
  945.2 1.8 copy-start.1
Sparse Core Ops, SparseCore 0:
  720.0 11.5 all-gather.1
Sparse Core Ops, SparseCore 1:
  797.2 136.2 all-reduce.2

commit v3 on v0

--- a/solution.py
+++ b/solution.py
@@ -1,11 +1,17 @@
+import functools
 import math
 
 import jax
 import jax.numpy as jnp
 from jax import lax
+from jax.experimental import pallas as pl
+from jax.experimental.pallas import tpu as pltpu
 from jax.sharding import PartitionSpec as P
 
 EPS = 1e-06
+MESH = pl.DeviceIdType.MESH
+LANES = 128
+CHUNK = 256
 
 
 def from_behind(value, axis, steps):
@@ -55,7 +61,1147 @@
     )
 
 
-def shards(
+def dot_nn(left_side, right_side):
+    return jnp.dot(left_side, right_side, preferred_element_type=jnp.float32)
+
+
+def remote(src, dst, send, recv, seq, head):
+    return pltpu.make_async_remote_copy(
+        src_ref=src, dst_ref=dst, send_sem=send, recv_sem=recv,
+        device_id={"seq": seq, "head": head}, device_id_type=MESH,
+    )
+
+
+def half_window(head, half):
+    return pl.ds(pl.multiple_of(head * half, LANES), half)
+
+
+def greet_all(seq_count, s, h):
+    barrier = pltpu.get_barrier_semaphore()
+
+    @pl.loop(1, seq_count)
+    def _(q):
+        seq = (s + q) % seq_count
+        pl.semaphore_signal(barrier, inc=1, device_id={"seq": seq, "head": h}, device_id_type=MESH)
+
+    pl.semaphore_signal(barrier, inc=1, device_id={"seq": s, "head": 1 - h}, device_id_type=MESH)
+    pl.semaphore_wait(barrier, seq_count)
+
+
+def one_minus_square(log_decay):
+    twice = 2.0 * log_decay
+    series = 1.0 + twice * (1 / 2 + twice * (1 / 6 + twice * (1 / 24 + twice * (1 / 120 + twice * (1 / 720)))))
+    return jnp.where(twice > -0.25, -twice * series, 1.0 - jnp.exp(twice))
+
+
+def shifted(value, step, keep, fill):
+    return jnp.where(keep, pltpu.roll(value, step % 8, 0), fill)
+
+
+def block_kernel(
+    seq_count, sequences, x_ref, g_ref, wg_ref, wu_ref, wd_ref,
+    gain_ref, cw_ref, cb_ref, rw_ref, rb_ref, iw_ref, ib_ref, rate_ref, sig_ref, mgain_ref,
+    out_ref, ingrad_ref, dw_ref, vec_ref, mat_ref,
+    dh_ref, r1_ref, e_ref, r2_ref, f_ref, sib_ref, peer_ref, xn_half, rg_keep, ig_keep, conv_keep, ext_keep, state_keep,
+    res_keep, ma_ref, mb_ref,
+    x_all, g_all, w_all, ld, halos, ends_all, ent, arr, part, part_in, scales, vec_in,
+    tok_s, tok_r, fwd_s, fwd_r, s1_s, s1_r, z_s, z_r, y_s, y_r, c1_s, c1_r, c2_s, c2_r, c3_s, c3_r,
+    sib_s, sib_r, peer_s, peer_r, halo_s, halo_r, end_s, end_r, part_s, part_r, fin_s, fin_r, ma_s, ma_r, mb_s, mb_r, mc_s, mc_r, md_s, md_r, va_s, va_r, vb_s, vb_r, keep, loc,
+):
+    far = seq_count // 8
+    rows = wg_ref.shape[0]
+    pair = 2 * rows
+    tokens, half = x_ref.shape[0], x_ref.shape[1] // 2
+    span = w_all.shape[2]
+    chunks = span // CHUNK
+    tiles = wg_ref.shape[1] // LANES
+    base, extra = tiles // 4, tiles % 4
+    s = lax.axis_index("seq")
+    h = lax.axis_index("head")
+    x = s % 2
+    y = (s // 2) % 2
+    zl = (s // 4) % 2
+    zh = s // 8
+    a = zl * 2 + x
+    weights = (wg_ref, wu_ref, wd_ref)
+
+    def seq_of(zh_, zl_, y_, x_):
+        return ((zh_ * 2 + zl_) * 2 + y_) * 2 + x_
+
+    def peer(d):
+        zl_, x_ = (zl + d // 2) % 2, (x + d % 2) % 2
+        return zl_ * 2 + x_, seq_of(zh, zl_, y, x_), zl_, x_
+
+    def first_tile(a_):
+        low = base * a_ + jnp.minimum(a_, extra)
+        high = base * a_ + jnp.maximum(a_ - (4 - extra), 0)
+        return jnp.where(h == 0, low, high)
+
+    def wide(zl_):
+        return zl_ == h
+
+    def block_rows(zh_, zl_, y_):
+        return pl.ds(pl.multiple_of(((zh_ * 2 + zl_) * 2 + y_) * pair, 32), pair)
+
+    def cols(c, width=CHUNK):
+        return pl.ds(pl.multiple_of(c * CHUNK, CHUNK), width)
+
+    def by_width(c, is_wide, run):
+        narrow = (c == chunks - 1) & jnp.logical_not(is_wide)
+        pl.when(narrow)(lambda: run(LANES))
+        pl.when(jnp.logical_not(narrow))(lambda: run(CHUNK))
+
+    y_seq = seq_of(zh, zl, 1 - y, x)
+
+    def z_seq(q):
+        return seq_of((zh + q) % far, zl, y, x)
+
+    model = 2 * half
+    length = tokens // sequences
+    groups = length // 8
+    mine = half_window(h, half)
+    block = rw_ref.shape[1]
+    heads = half // block
+    f32, bf = jnp.float32, jnp.bfloat16
+    greet_all(seq_count, s, h)
+
+    def s1_send(c, d, w, width):
+        a_, seq, zl_, _ = peer(d)
+        col = pl.multiple_of((first_tile(a_) + 2 * c) * LANES, LANES)
+        return remote(
+            weights[w].at[:, pl.ds(col, width)],
+            w_all.at[w, pl.ds(pl.multiple_of(s * rows, 32), rows), cols(c, width)],
+            s1_s.at[c, d - 1, w], s1_r.at[c, d - 1, w], seq, h,
+        )
+
+    def s1_recv(c, d, w, width):
+        _, seq, _, _ = peer(d)
+        return remote(
+            weights[w].at[:, pl.ds(0, width)],
+            w_all.at[w, pl.ds(pl.multiple_of(seq * rows, 32), rows), cols(c, width)],
+            s1_s.at[c, d - 1, w], s1_r.at[c, d - 1, w], seq, h,
+        )
+
+    def s1_own(c, w, width):
+        col = pl.multiple_of((first_tile(a) + 2 * c) * LANES, LANES)
+        return pltpu.make_async_copy(
+            weights[w].at[:, pl.ds(col, width)],
+            w_all.at[w, pl.ds(pl.multiple_of(s * rows, 32), rows), cols(c, width)],
+            loc.at[c, w],
+        )
+
+    def s1_start(c):
+        for d in (1, 2, 3):
+            def go(width, d=d):
+                for w in range(3):
+                    s1_send(c, d, w, width).start()
+            by_width(c, wide(peer(d)[2]), go)
+
+        def own(width):
+            for w in range(3):
+                s1_own(c, w, width).start()
+        by_width(c, wide(zl), own)
+
+    def s1_wait(c):
+        def got(width):
+            for w in range(3):
+                s1_own(c, w, width).wait()
+                for d in (1, 2, 3):
+                    s1_recv(c, d, w, width).wait_recv()
+        by_width(c, wide(zl), got)
+
+    def s1_drain(c):
+        for d in (1, 2, 3):
+            def go(width, d=d):
+                for w in range(3):
+                    s1_send(c, d, w, width).wait_send()
+            by_width(c, wide(peer(d)[2]), go)
+
+    def z_copy(c, q, zl_, width, incoming):
+        zh_ = (zh - q + far) % far if incoming else zh
+        part = w_all.at[:, block_rows(zh_, zl_, y), cols(c, width)]
+        return remote(part, part, z_s.at[c, q - 1, zl_], z_r.at[c, q - 1, zl_], z_seq(q), h)
+
+    def y_copy(c, q, zl_, width, incoming):
+        part = w_all.at[:, block_rows((zh - q + far) % far, zl_, 1 - y if incoming else y), cols(c, width)]
+        return remote(part, part, y_s.at[c, q, zl_], y_r.at[c, q, zl_], y_seq, h)
+
+    def z_start(c):
+        def go(width):
+            for q in range(1, far):
+                for zl_ in range(2):
+                    z_copy(c, q, zl_, width, False).start()
+            for zl_ in range(2):
+                y_copy(c, 0, zl_, width, False).start()
+        by_width(c, wide(zl), go)
+
+    def z_forward(c):
+        def go(width):
+            for q in range(1, far):
+                for zl_ in range(2):
+                    z_copy(c, q, zl_, width, True).wait_recv()
+                    y_copy(c, q, zl_, width, False).start()
+        by_width(c, wide(zl), go)
+
+    def y_wait(c):
+        def go(width):
+            for q in range(far):
+                for zl_ in range(2):
+                    y_copy(c, q, zl_, width, True).wait_recv()
+        by_width(c, wide(zl), go)
+
+    def zy_drain(c):
+        def go(width):
+            for zl_ in range(2):
+                for q in range(1, far):
+                    z_copy(c, q, zl_, width, False).wait_send()
+                for q in range(far):
+                    y_copy(c, q, zl_, width, False).wait_send()
+        by_width(c, wide(zl), go)
+
+    half_cols = pl.ds(pl.multiple_of(h * half, LANES), half)
+
+    def tok_rows(a_):
+        return pl.ds(pl.multiple_of(a_ * tokens, 32), tokens)
+
+    def tok_copy(k, d, incoming):
+        src = xn_half if k == 0 else g_ref.at[:, half_cols]
+        dst = (x_all, g_all)[k]
+        here = a
+        if d == 3:
+            here = peer(2)[0]
+            src = dst.at[tok_rows(here), half_cols]
+        return remote(
+            src, dst.at[tok_rows(peer(d)[0] if incoming else here), half_cols],
+            tok_s.at[k, d - 1], tok_r.at[k, d - 1], peer(1 if d == 3 else d)[1], h,
+        )
+
+    def fwd_copy(k, d, incoming):
+        dst = (x_all, g_all)[k]
+        side = pl.ds(pl.multiple_of((1 - h if incoming else h) * half, LANES), half)
+        part = dst.at[tok_rows(peer(d)[0]), side]
+        return remote(part, part, fwd_s.at[k, d], fwd_r.at[k, d], s, 1 - h)
+
+    own_x = pltpu.make_async_copy(xn_half, x_all.at[tok_rows(a), half_cols], loc.at[chunks, 0])
+    own_g = pltpu.make_async_copy(g_ref, g_all.at[tok_rows(a), :], loc.at[chunks, 1])
+
+    def tok_start(k):
+        tok_copy(k, 2, False).start()
+        tok_copy(k, 1, False).start()
+
+    def tok_turn(k):
+        tok_copy(k, 2, True).wait_recv()
+        tok_copy(k, 3, False).start()
+        fwd_copy(k, 2, False).start()
+
+    def tok_last(k):
+        for d in (1, 3):
+            tok_copy(k, d, True).wait_recv()
+            fwd_copy(k, d, False).start()
+
+    def tok_wait(k):
+        for d in ((1, 2, 3) if k else (0, 1, 2, 3)):
+            fwd_copy(k, d, True).wait_recv()
+
+    def r1_copy(c, zh_, zl_, incoming):
+        return remote(
+            dh_ref.at[c, :, block_rows(zh_, zl_, 1 - y), :], r1_ref.at[c, :, pl.ds((zh_ * 2 + zl_) * pair, pair)],
+            c1_s.at[c, zh_, zl_], c1_r.at[c, zh_, zl_], y_seq, h,
+        )
+
+    def r1_start(c, steps_away):
+        for q in steps_away:
+            for zl_ in range(2):
+                r1_copy(c, (zh + q) % far, zl_, False).start()
+
+    def r2_copy(c, q, zl_):
+        return remote(
+            e_ref.at[c, :, pl.ds(pl.multiple_of((((zh + q) % far) * 2 + zl_) * pair, 32), pair)], r2_ref.at[c, q - 1, :, pl.ds(zl_ * pair, pair)],
+            c2_s.at[c, q - 1, zl_], c2_r.at[c, q - 1, zl_], z_seq(q), h,
+        )
+
+    def add_into(first, second, blocks):
+        @pl.loop(0, 3)
+        def _(w):
+            @pl.loop(0, blocks)
+            def _(b):
+                r = pl.ds(pl.multiple_of(b * pair, 32), pair)
+                total = first[w, r, :].astype(jnp.float32) + second[w, r, :].astype(jnp.float32)
+                first[w, r, :] = total.astype(jnp.bfloat16)
+
+    def plane_rows(zh_):
+        return pl.ds(pl.multiple_of(zh_ * 2 * pair, 32), 2 * pair)
+
+    def sum_near(c, q, va, vb):
+        zh_ = (zh + q) % far
+        loads = []
+        for zl_ in range(2):
+            loads.append(pltpu.make_async_copy(
+                dh_ref.at[c, :, block_rows(zh_, zl_, y), :], va.at[:, pl.ds(zl_ * pair, pair)], loc.at[chunks + 1, zl_]
+            ))
+            loads[-1].start()
+        for zl_ in range(2):
+            r1_copy(c, zh_, zl_, True).wait_recv()
+        loads.append(pltpu.make_async_copy(r1_ref.at[c, :, plane_rows(zh_)], vb, loc.at[chunks, 2]))
+        loads[-1].start()
+        for load in loads:
+            load.wait()
+        add_into(va, vb, 2)
+        back = pltpu.make_async_copy(va, e_ref.at[c, :, plane_rows(zh_)], loc.at[chunks, 2])
+        back.start()
+        back.wait()
+        if q:
+            for zl_ in range(2):
+                r2_copy(c, q, zl_).start()
+
+    def near_all(c, va, vb):
+        for q in list(range(1, far)) + [0]:
+            sum_near(c, q, va, vb)
+
+    def c3_copy(c, d, width, incoming):
+        a_, seq, zl_, x_ = peer(d)
+        col = pl.multiple_of((first_tile(a_ if incoming else a) + 2 * c) * LANES, LANES)
+        return remote(
+            f_ref.at[c, :, pl.ds(pl.multiple_of((zl_ * 2 + x_) * rows, 32), rows), pl.ds(0, width)],
+            dw_ref.at[:, :, pl.ds(col, width)],
+            c3_s.at[c, d - 1], c3_r.at[c, d - 1], seq, h,
+        )
+
+    def c3_own(c, width):
+        col = pl.multiple_of((first_tile(a) + 2 * c) * LANES, LANES)
+        return pltpu.make_async_copy(
+            f_ref.at[c, :, pl.ds(pl.multiple_of(a * rows, 32), rows), pl.ds(0, width)],
+            dw_ref.at[:, :, pl.ds(col, width)], loc.at[c, 0],
+        )
+
+    def sum_far(c, va, vb):
+        first, second = va, vb
+        kept = pltpu.make_async_copy(
+            e_ref.at[c, :, pl.ds(pl.multiple_of(zh * 2 * pair, 32), 2 * pair)], first, loc.at[chunks, 0]
+        )
+        kept.start()
+        kept.wait()
+        for q in range(1, far):
+            for zl_ in range(2):
+                r2_copy(c, q, zl_).wait_recv()
+            other = pltpu.make_async_copy(r2_ref.at[c, q - 1], second, loc.at[chunks, 0])
+            other.start()
+            other.wait()
+            add_into(va, vb, 2)
+        back = pltpu.make_async_copy(first, f_ref.at[c], loc.at[chunks, 0])
+        back.start()
+        back.wait()
+
+        def go(width):
+            for d in (1, 2, 3):
+                c3_copy(c, d, width, False).start()
+            c3_own(c, width).start()
+        by_width(c, wide(zl), go)
+
+    def forward_chunk(c, hid, gg, gu):
+        @pl.loop(0, 4)
+        def _(i):
+            r = tok_rows(i)
+            xb = x_all[r, :]
+            gate = dot_nn(xb, w_all[0, :, cols(c)])
+            up = dot_nn(xb, w_all[1, :, cols(c)])
+            gh = dot_nn(g_all[r, :], w_all[2, :, cols(c)])
+            k0, k1 = 0.7978845608028654, 0.044715
+            th = jnp.tanh(k0 * (gate + k1 * gate * gate * gate))
+            cdf = 0.5 * (1.0 + th)
+            act = gate * cdf
+            slope = cdf + 0.5 * gate * (1.0 - th * th) * k0 * (1.0 + 3.0 * k1 * gate * gate)
+            hid[r, cols(c)] = (act * up).astype(jnp.bfloat16)
+            gu[r, cols(c)] = (gh * act).astype(jnp.bfloat16)
+            gg[r, cols(c)] = (gh * up * slope).astype(jnp.bfloat16)
+
+    def weight_chunk(c, hid, gg, gu, dv):
+        for w, (left, right) in enumerate(((x_all, gg), (x_all, gu), (g_all, hid))):
+            @pl.loop(0, x_all.shape[1] // 512)
+            def _(j):
+                r = pl.ds(pl.multiple_of(j * 512, 512), 512)
+                dv[w, r, :] = contract_first(left[:, r], right[:, cols(c)]).astype(jnp.bfloat16)
+            pltpu.make_async_copy(dv.at[w], dh_ref.at[c, w], loc.at[chunks, w]).start()
+        for w in range(3):
+            pltpu.make_async_copy(dv.at[w], dh_ref.at[c, w], loc.at[chunks, w]).wait()
+
+    def product(which, r, d_rows, hid, gg, gu):
+        if which == 0:
+            return contract_last(gg[r, :], w_all[0, d_rows, :]) + contract_last(gu[r, :], w_all[1, d_rows, :])
+        return contract_last(hid[r, :], w_all[2, d_rows, :])
+
+    def pairs(i):
+        return pl.ds(pl.multiple_of(i * 16, 16), 16)
+
+    def head_lanes(n):
+        return pl.ds(pl.multiple_of(n * block, block), block)
+
+    def end_copy(side, target, source):
+        part_ends = ends_all.at[side, source]
+        return remote(part_ends, part_ends, end_s.at[side, target], end_r.at[side, source], target, h)
+
+    def part_copy(i):
+        return remote(part.at[i], part_in.at[i], part_s.at[i], part_r.at[i], s, 1 - h)
+
+    def halo_copy(side):
+        target = jnp.minimum(s + 1, seq_count - 1) if side == 0 else jnp.maximum(s - 1, 0)
+        return remote(halos.at[side, 0], halos.at[side, 1], halo_s.at[side], halo_r.at[side], target, h)
+
+    row_ids = lax.broadcasted_iota(jnp.int32, (8, half), 0)
+
+    place, plane, planes = s % 4, s // 4, seq_count // 4
+    quarter = 2 * heads * block // 4
+    piece = quarter // planes
+    mat = w_all.at[0, pl.ds(0, 4 * quarter), pl.ds(2 * CHUNK, block)]
+    got_a = w_all.at[1, pl.ds(0, 3 * quarter), pl.ds(2 * CHUNK, block)]
+    got_b = w_all.at[2, pl.ds(quarter, (planes - 1) * piece), pl.ds(2 * CHUNK, block)]
+    own_sum = w_all.at[2, pl.ds(0, quarter), pl.ds(2 * CHUNK, block)]
+
+    def mate(i):
+        return plane * 4 + (place + i) % 4
+
+    def layer(j):
+        return (plane + j) % planes * 4 + place
+
+    def rows_at(start, count):
+        return pl.ds(pl.multiple_of(start, 32), count)
+
+    def mat_a(i):
+        return remote(
+            mat.at[rows_at((place + i) % 4 * quarter, quarter)], ma_ref.at[pl.ds((i - 1) * quarter, quarter)],
+            ma_s.at[i - 1], ma_r.at[i - 1], mate(i), h,
+        )
+
+    def mat_b(j):
+        return remote(
+            own_sum.at[rows_at((plane + j) % planes * piece, piece)], mb_ref.at[pl.ds((j - 1) * piece, piece)],
+            mb_s.at[j - 1], mb_r.at[j - 1], layer(j), h,
+        )
+
+    def mat_c(j, incoming):
+        source = (plane - j + planes) % planes if incoming else plane
+        part_rows = mat_ref.at[rows_at(place * quarter + source * piece, piece)]
+        return remote(part_rows, part_rows, mc_s.at[j - 1], mc_r.at[j - 1], layer(j), h)
+
+    def mat_d(i, incoming):
+        source = (place - i + 4) % 4 if incoming else place
+        part_rows = mat_ref.at[rows_at(source * quarter, quarter)]
+        return remote(part_rows, part_rows, md_s.at[i - 1], md_r.at[i - 1], mate(i), h)
+
+    def take(src, dst, i):
+        load = pltpu.make_async_copy(src, dst, keep.at[i])
+        load.start()
+        load.wait()
+
+    def matrices_start():
+        for i in (1, 2, 3):
+            mat_a(i).start()
+
+    def matrices_plane():
+        for i in (1, 2, 3):
+            mat_a(i).wait_recv()
+        take(ma_ref, got_a, 8)
+
+        @pl.loop(0, quarter // 32)
+        def _(i):
+            total = mat[rows_at(place * quarter + i * 32, 32), :].astype(f32)
+            for k in range(3):
+                total = total + got_a[rows_at(k * quarter + i * 32, 32), :].astype(f32)
+            own_sum[rows_at(i * 32, 32), :] = total.astype(bf)
+        for j in range(1, planes):
+            mat_b(j).start()
+
+    def matrices_across():
+        for j in range(1, planes):
+            mat_b(j).wait_recv()
+        take(mb_ref, got_b, 8)
+
+        @pl.loop(0, piece // 32)
+        def _(i):
+            r = rows_at(plane * piece + i * 32, 32)
+            total = own_sum[r, :].astype(f32)
+            for k in range(planes - 1):
+                total = total + got_b[rows_at(k * piece + i * 32, 32), :].astype(f32)
+            own_sum[r, :] = total.astype(bf)
+        take(own_sum.at[rows_at(plane * piece, piece)], mat_ref.at[rows_at(place * quarter + plane * piece, piece)], 8)
+        for j in range(1, planes):
+            mat_c(j, False).start()
+
+    def matrices_spread():
+        for j in range(1, planes):
+            mat_c(j, True).wait_recv()
+        for i in (1, 2, 3):
+            mat_d(i, False).start()
+
+    def matrices_end():
+        for i in (1, 2, 3):
+            mat_d(i, True).wait_recv()
+            mat_d(i, False).wait_send()
+            mat_a(i).wait_send()
+        for j in range(1, planes):
+            mat_b(j).wait_send()
+            mat_c(j, False).wait_send()
+
+    def vec_copy(level, k):
+        if level == 0:
+            return remote(vec_ref, vec_in.at[k - 1], va_s.at[k - 1], va_r.at[k - 1], mate(k), h)
+        return remote(vec_ref, vec_in.at[2 + k], vb_s.at[k - 1], vb_r.at[k - 1], layer(k), h)
+
+    def vectors_start(level):
+        for k in range(1, (4, planes)[level]):
+            vec_copy(level, k).start()
+
+    def vectors_sum(level):
+        count = (4, planes)[level]
+        for k in range(1, count):
+            vec_copy(level, k).wait()
+        total = vec_ref[...]
+        for k in range(1, count):
+            total = total + vec_in[(0, 3)[level] + k - 1]
+        vec_ref[...] = total
+
+    s1_start(0)
+    s1_start(1)
+    own_g.start()
+    tok_start(1)
+
+    @pl.when(jnp.logical_not(wide(zl)))
+    def _():
+        w_all[:, :, pl.ds(span - LANES, LANES)] = jnp.zeros((3, w_all.shape[1], LANES), bf)
+
+    def recur_forward(xin, rg, ig, conv, ext, prod, run):
+        load = pltpu.make_async_copy(x_ref, xin, loc.at[chunks, 0])
+        load.start()
+        load.wait()
+
+        def normed(r, count):
+            full = xin[pl.ds(r, count), :].astype(f32)
+            scale = lax.rsqrt(jnp.sum(full * full, axis=1, keepdims=True) * (1.0 / model) + EPS)
+            scales[0, pl.ds(r, count), :] = jnp.broadcast_to(scale, (count, LANES))
+            own = xin[pl.ds(r, count), mine].astype(f32)
+            return ((own * scale) * gain_ref[:, mine]).astype(bf).astype(f32)
+
+        for q in range(sequences):
+            halos[0, 0, q] = normed(q * length + length - 16, 16)[8:]
+        pl.when(s + 1 < seq_count)(halo_copy(0).start)
+        for q in range(sequences):
+            @pl.loop(0, length // 16)
+            def _(i, q=q):
+                r = pl.multiple_of(i * 16, 16)
+                ext[q, pl.ds(8 + r, 16), :] = normed(pl.multiple_of(q * length + r, 16), 16)
+
+        @pl.when(s > 0)
+        def _():
+            halo_copy(0).wait_recv()
+            for q in range(sequences):
+                ext[q, pl.ds(0, 8), :] = halos[0, 1, q]
+
+        @pl.when(s == 0)
+        def _():
+            for q in range(sequences):
+                ext[q, pl.ds(0, 8), :] = jnp.zeros((8, half), f32)
+
+        saves = [pltpu.make_async_copy(ext, ext_keep, keep.at[0])]
+        saves[0].start()
+        s1_wait(0)
+        z_start(0)
+        s1_start(2)
+
+        @pl.loop(0, heads)
+        def _(n):
+            lanes = head_lanes(n)
+            for q in range(sequences):
+                total = cb_ref[:, lanes]
+                for k in range(4):
+                    total = total + cw_ref[pl.ds(k, 1), lanes] * ext[q, pl.ds(8 - k, length), lanes]
+                conv[pl.ds(q * length, length), lanes] = total.astype(bf)
+            low = conv[:, lanes]
+            rg[:, lanes] = jax.nn.sigmoid(dot_nn(low, rw_ref[n]) + rb_ref[:, lanes])
+            ig[:, lanes] = jax.nn.sigmoid(dot_nn(low, iw_ref[n]) + ib_ref[:, lanes])
+
+            @pl.loop(0, tokens // 64)
+            def _(i):
+                r = pl.ds(pl.multiple_of(i * 64, 64), 64)
+                log_decay = -8.0 * rate_ref[:, lanes] * rg[r, lanes]
+                prod[r, lanes] = jnp.exp(log_decay)
+                mult = jnp.sqrt(one_minus_square(log_decay))
+                run[r, lanes] = mult * ig[r, lanes] * conv[r, lanes].astype(f32)
+
+        for i, (src, dst) in enumerate(((rg, rg_keep), (ig, ig_keep), (conv, conv_keep))):
+            saves.append(pltpu.make_async_copy(src, dst, keep.at[1 + i]))
+            saves[-1].start()
+        s1_wait(1)
+        z_start(1)
+        s1_start(3)
+
+        def scan_group(g, carry):
+            out = []
+            for q in range(sequences):
+                r = pl.ds(pl.multiple_of(q * length + g * 8, 8), 8)
+                a_, b_ = prod[r, :], run[r, :]
+                for k in (1, 2, 4):
+                    inside = row_ids >= k
+                    b_ = b_ + a_ * shifted(b_, k, inside, 0.0)
+                    a_ = a_ * shifted(a_, k, inside, 1.0)
+                b_ = b_ + a_ * carry[2 * q]
+                a_ = a_ * carry[2 * q + 1]
+                prod[r, :] = a_
+                run[r, :] = b_
+                out += [b_[7:8], a_[7:8]]
+            return tuple(out)
+
+        first = []
+        for q in range(sequences):
+            first += [jnp.zeros((1, half), f32), jnp.ones((1, half), f32)]
+        last = lax.fori_loop(0, groups, scan_group, tuple(first))
+        for q in range(sequences):
+            ends_all[0, s, pl.ds(q, 1), :] = last[2 * q + 1]
+            ends_all[0, s, pl.ds(sequences + q, 1), :] = last[2 * q]
+
+        @pl.loop(1, seq_count)
+        def _(q):
+            pl.when(s + q < seq_count)(lambda: end_copy(0, s + q, s).start())
+
+        tok_turn(1)
+        ent[...] = jnp.zeros_like(ent)
+
+        @pl.loop(0, seq_count)
+        def _(source):
+            @pl.when(source < s)
+            def _():
+                end_copy(0, s, source).wait_recv()
+                got = ends_all[0, source]
+                ent[...] = got[:sequences] * ent[...] + got[sequences:]
+
+        for q in range(sequences):
+            @pl.loop(0, length // 16)
+            def _(i, q=q):
+                r = pl.ds(pl.multiple_of(q * length + i * 16, 16), 16)
+                state = run[r, :] + prod[r, :] * ent[pl.ds(q, 1), :]
+                run[r, :] = state
+                residual = xin[r, mine].astype(f32) + state.astype(bf).astype(f32)
+                prod[r, :] = residual
+                part[0, r, :] = jnp.broadcast_to(jnp.sum(residual * residual, axis=1, keepdims=True), (16, LANES))
+
+        part_copy(0).start()
+        for i, (src, dst) in enumerate(((run, state_keep), (prod, res_keep))):
+            saves.append(pltpu.make_async_copy(src, dst, keep.at[4 + i]))
+            saves[-1].start()
+        part_copy(0).wait_recv()
+
+        @pl.loop(0, tokens // 16)
+        def _(i):
+            r = pairs(i)
+            scale = lax.rsqrt((part[0, r, :] + part_in[0, r, :]) * (1.0 / model) + EPS)
+            scales[1, r, :] = scale
+            ld[r, :] = ((prod[r, :] * scale[:, :1]) * mgain_ref[:, mine]).astype(bf)
+
+        saves.append(pltpu.make_async_copy(ld, xn_half, keep.at[6]))
+        saves[-1].start()
+        for save in saves:
+            save.wait()
+
+    pl.run_scoped(
+        recur_forward,
+        pltpu.VMEM((tokens, model), bf), pltpu.VMEM((tokens, half), f32), pltpu.VMEM((tokens, half), f32),
+        pltpu.VMEM((tokens, half), bf), pltpu.VMEM((sequences, length + 8, half), f32),
+        pltpu.VMEM((tokens, half), f32), pltpu.VMEM((tokens, half), f32),
+    )
+    tok_start(0)
+    own_x.start()
+    s1_wait(2)
+    z_start(2)
+    s1_wait(3)
+    z_start(3)
+    own_x.wait()
+    fwd_copy(0, 0, False).start()
+    z_forward(0)
+    own_g.wait()
+    tok_turn(0)
+    tok_last(1)
+    z_forward(1)
+    z_forward(2)
+    tok_last(0)
+    tok_wait(1)
+    tok_wait(0)
+
+    stage = (x_all, g_all)
+    steps = half // 256
+
+    def slot(k):
+        return pl.ds(pl.multiple_of(k * tokens, 32), tokens)
+
+    def sib_copy(which, k):
+        return remote(
+            stage[which].at[slot(k), pl.ds(0, half)], sib_ref.at[which, k], sib_s.at[which, k], sib_r.at[which, k],
+            s, 1 - h,
+        )
+
+    def peer_copy(which, k):
+        zl_step, x_step = k // 2, 1 - k // 2
+        seq = seq_of(zh, (zl + zl_step) % 2, y, (x + x_step) % 2)
+        return remote(
+            stage[which].at[slot(k), pl.ds(half, half)], peer_ref.at[which, k], peer_s.at[which, k], peer_r.at[which, k],
+            seq, h,
+        )
+
+    def fetch(src):
+        load = pltpu.make_async_copy(src, ld, loc.at[chunks, 0])
+        load.start()
+        load.wait()
+
+    def add_slot(which, k, src):
+        fetch(src)
+
+        @pl.loop(0, tokens // 64)
+        def _(i):
+            r = pl.ds(pl.multiple_of(k * tokens + i * 64, 64), 64)
+            lanes = pl.ds(half, half)
+            total = stage[which][r, lanes].astype(f32) + ld[pl.ds(pl.multiple_of(i * 64, 64), 64), :].astype(f32)
+            stage[which][r, lanes] = total.astype(bf)
+
+    def combine(which, k):
+        sib_copy(which, k).wait_recv()
+        add_slot(which, k, sib_ref.at[which, k])
+        if k == 2:
+            peer_copy(which, 0).wait_recv()
+            add_slot(which, k, peer_ref.at[which, 0])
+        peer_copy(which, k).start()
+
+    def compute_sums(which, k, hid, gg, gu):
+        zl_step, x_step = 1 - k % 2, 1 - k // 2
+        r = tok_rows(((zl + zl_step) % 2) * 2 + (x + x_step) % 2)
+
+        def one(side, base_col):
+            @pl.loop(0, steps)
+            def _(j):
+                dr = pl.ds(pl.multiple_of(side * half + j * 256, 256), 256)
+                value = product(which, r, dr, hid, gg, gu)
+                stage[which][slot(k), pl.ds(pl.multiple_of(base_col + j * 256, 256), 256)] = value.astype(bf)
+
+        one(1 - h, 0)
+        sib_copy(which, k).start()
+        one(h, half)
+
+    def feed_forward(hid, gg, gu, dv, va, vb):
+        @pl.loop(0, chunks)
+        def _(c):
+            y_wait(c)
+            forward_chunk(c, hid, gg, gu)
+            weight_chunk(c, hid, gg, gu, dv)
+            away, near = range(1, far), (0,)
+            pl.when(c == 0)(lambda: r1_start(0, away))
+
+            @pl.when(c == 1)
+            def _():
+                z_forward(3)
+                r1_start(0, near)
+
+            pl.when(c >= 1)(lambda: r1_start(c, (*away, *near)))
+
+        for k in (0, 1, 2, 3):
+            for d in (1, 2, 3) if k == 0 else ():
+                for i in (0, 1):
+                    tok_copy(i, d, False).wait_send()
+                    fwd_copy(i, d, False).wait_send()
+            if k == 0:
+                fwd_copy(0, 0, False).wait_send()
+            compute_sums(0, k, hid, gg, gu)
+            if k in (1, 2):
+                combine(0, k - 1)
+            if k == 1:
+                near_all(0, va, vb)
+
+        @pl.loop(0, 4)
+        def _(k):
+            compute_sums(1, k, hid, gg, gu)
+        combine(0, 2)
+        near_all(1, va, vb)
+        sum_far(0, va, vb)
+
+    wide_buf = pltpu.VMEM((4 * tokens, span), bf)
+    pl.run_scoped(
+        feed_forward, wide_buf, wide_buf, wide_buf, pltpu.VMEM((3, model, CHUNK), bf),
+        pltpu.VMEM((3, 2 * pair, CHUNK), bf), pltpu.VMEM((3, 2 * pair, CHUNK), bf),
+    )
+    pl.loop(0, chunks)(zy_drain)
+    held = 2 * pair
+    va, vb = w_all.at[:, pl.ds(0, held), pl.ds(0, CHUNK)], w_all.at[:, pl.ds(held, held), pl.ds(0, CHUNK)]
+
+    def recur_backward(fin, adj, gres, rg, ig, gconv, ext, wsum):
+        spare = [x_all.at[slot(k), pl.ds(0, half)] for k in range(4)]
+        for k in range(4):
+            sib_copy(0, k).wait_send()
+        conv, own_x_half, own_g_half = spare[0], spare[1], spare[2]
+        loads = [
+            pltpu.make_async_copy(conv_keep, conv, keep.at[0]),
+            pltpu.make_async_copy(x_ref.at[:, mine], own_x_half, keep.at[1]),
+            pltpu.make_async_copy(g_ref.at[:, mine], own_g_half, keep.at[2]),
+            pltpu.make_async_copy(rg_keep, rg, keep.at[3]),
+            pltpu.make_async_copy(ig_keep, ig, keep.at[4]),
+            pltpu.make_async_copy(res_keep, adj, keep.at[5]),
+        ]
+        for q in range(sequences):
+            loads.append(pltpu.make_async_copy(
+                state_keep.at[pl.ds(q * length, length)], ext.at[q, pl.ds(8, length)], keep.at[6 + q]
+            ))
+        for load in loads:
+            load.start()
+
+        def widen(first):
+            @pl.loop(0, tokens // 64)
+            def _(i):
+                r = pl.ds(pl.multiple_of(i * 64, 64), 64)
+                if first:
+                    own = x_all[pl.ds(pl.multiple_of(3 * tokens + i * 64, 64), 64), pl.ds(half, half)]
+                    fin[r, :] = own.astype(f32) + ld[r, :].astype(f32)
+                else:
+                    fin[r, :] += ld[r, :].astype(f32)
+
+        sib_copy(0, 3).wait_recv()
+        fetch(sib_ref.at[0, 3])
+        widen(True)
+        peer_copy(0, 1).wait_recv()
+        fetch(peer_ref.at[0, 1])
+        widen(False)
+        combine(1, 0)
+        combine(1, 1)
+        vec_ref[...] = jnp.zeros_like(vec_ref)
+        for load in loads:
+            load.wait()
+        for q in range(sequences):
+            ext[q, pl.ds(0, 8), :] = jnp.broadcast_to(ent[pl.ds(q, 1), :], (8, half))
+
+            @pl.loop(0, length // 16)
+            def _(i, q=q):
+                r = pl.ds(pl.multiple_of(q * length + i * 16, 16), 16)
+                gconv[q, pairs(i), :] = jnp.exp(-8.0 * rate_ref[...] * rg[r, :])
+        peer_copy(0, 2).wait_recv()
+        fetch(peer_ref.at[0, 2])
+        widen(False)
+
+        @pl.loop(0, tokens // 16)
+        def _(i):
+            r = pairs(i)
+            hat = adj[r, :] * scales[1, r, :1]
+            product_ = fin[r, :] * hat
+            vec_ref[pl.ds(9, 1), :] += jnp.sum(product_, axis=0, keepdims=True)
+            part[1, r, :] = jnp.broadcast_to(jnp.sum(product_ * mgain_ref[:, mine], axis=1, keepdims=True), (16, LANES))
+
+        part_copy(1).start()
+        part_copy(1).wait_recv()
+
+        @pl.loop(0, tokens // 16)
+        def _(i):
+            r = pairs(i)
+            scale = scales[1, r, :1]
+            hat = adj[r, :] * scale
+            mean = ((part[1, r, :] + part_in[1, r, :]) * (1.0 / model))[:, :1]
+            own = x_all[pl.ds(pl.multiple_of(2 * tokens + i * 16, 16), 16), pl.ds(0, half)].astype(f32)
+            gres[r, :] = own + scale * (fin[r, :] * mgain_ref[:, mine] - hat * mean)
+
+        def scan_group(i, carry):
+            g = groups - 1 - i
+            out = []
+            for q in range(sequences):
+                t = pl.multiple_of(g * 8, 8)
+                r = pl.ds(pl.multiple_of(q * length + t, 8), 8)
+                here = gconv[q, pl.ds(t, 8), :]
+                a_, b_ = shifted(here, -1, row_ids < 7, carry[3 * q + 2]), gres[r, :]
+                for k in (1, 2, 4):
+                    inside = row_ids < 8 - k
+                    b_ = b_ + a_ * shifted(b_, -k, inside, 0.0)
+                    a_ = a_ * shifted(a_, -k, inside, 1.0)
+                b_ = b_ + a_ * carry[3 * q]
+                a_ = a_ * carry[3 * q + 1]
+                fin[r, :] = a_
+                adj[r, :] = b_
+                out += [b_[:1], a_[:1], here[:1]]
+            return tuple(out)
+
+        first = []
+        for q in range(sequences):
+            one = jnp.ones((1, half), f32)
+            first += [jnp.zeros((1, half), f32), one, one]
+        last = lax.fori_loop(0, groups, scan_group, tuple(first))
+        for q in range(sequences):
+            ends_all[1, s, pl.ds(q, 1), :] = last[3 * q + 1] * last[3 * q + 2]
+            ends_all[1, s, pl.ds(sequences + q, 1), :] = last[3 * q] * last[3 * q + 2]
+
+        @pl.loop(1, seq_count)
+        def _(q):
+            pl.when(s >= q)(lambda: end_copy(1, jnp.maximum(s - q, 0), s).start())
+
+        arr[...] = jnp.zeros_like(arr)
+
+        @pl.loop(1, seq_count)
+        def _(q):
+            source = seq_count - q
+
+            @pl.when(source > s)
+            def _():
+                end_copy(1, s, source).wait_recv()
+                got = ends_all[1, source]
+                arr[...] = got[:sequences] * arr[...] + got[sequences:]
+
+        for q in range(sequences):
+            @pl.loop(0, length // 16)
+            def _(i, q=q):
+                r = pl.ds(pl.multiple_of(q * length + i * 16, 16), 16)
+                adj[r, :] += fin[r, :] * arr[pl.ds(q, 1), :]
+
+        near_all(2, va, vb)
+        combine(1, 2)
+        sum_far(1, va, vb)
+
+        @pl.loop(0, heads)
+        def _(n):
+            lanes = head_lanes(n)
+            rate = rate_ref[:, lanes]
+            sums = [jnp.zeros((1, block), f32)] * 3
+            for q in range(sequences):
+                for i in range(2):
+                    count = length // 2
+                    t = i * count
+                    r = pl.ds(q * length + t, count)
+                    rg_, ig_ = rg[r, lanes], ig[r, lanes]
+                    low = x_all[r, lanes]
+                    conv_ = low.astype(f32)
+                    a_ = adj[r, lanes]
+                    log_decay = -8.0 * rate * rg_
+                    decay = jnp.exp(log_decay)
+                    mult = jnp.sqrt(one_minus_square(log_decay))
+                    previous = ext[q, pl.ds(7 + t, count), lanes]
+                    grad_mult = a_ * ig_ * conv_
+                    grad_log = a_ * previous * decay - grad_mult * decay * decay / mult
+                    pre_r = (grad_log * (-8.0 * rate) * rg_ * (1.0 - rg_)).astype(bf)
+                    pre_i = (a_ * mult * conv_ * ig_ * (1.0 - ig_)).astype(bf)
+                    sums[0] = sums[0] + jnp.sum(grad_log * rg_, axis=0, keepdims=True)
+                    sums[1] = sums[1] + jnp.sum(pre_r.astype(f32), axis=0, keepdims=True)
+                    sums[2] = sums[2] + jnp.sum(pre_i.astype(f32), axis=0, keepdims=True)
+                    back = contract_last(pre_r, rw_ref[n]) + contract_last(pre_i, iw_ref[n])
+                    gconv[q, pl.ds(t, count), lanes] = (a_ * mult * ig_ + back).astype(bf).astype(f32)
+                    if q == 0 and i == 0:
+                        wsum[0] = contract_first(low, pre_r)
+                        wsum[1] = contract_first(low, pre_i)
+                    else:
+                        wsum[0] += contract_first(low, pre_r)
+                        wsum[1] += contract_first(low, pre_i)
+            for k in range(2):
+                mat[rows_at((k * heads + n) * block, block), :] = wsum[k].astype(bf)
+            vec_ref[pl.ds(8, 1), lanes] = sums[0] * 8.0 * sig_ref[:, lanes]
+            vec_ref[pl.ds(6, 1), lanes] = sums[1]
+            vec_ref[pl.ds(7, 1), lanes] = sums[2]
+
+        for q in range(sequences):
+            halos[1, 0, q] = gconv[q, pl.ds(0, 8), :]
+        pl.when(s > 0)(halo_copy(1).start)
+        matrices_start()
+        again = pltpu.make_async_copy(ext_keep, ext, keep.at[2])
+        again.start()
+        again.wait()
+
+        @pl.loop(0, heads)
+        def _(n):
+            lanes = head_lanes(n)
+            for k in range(5):
+                total = jnp.zeros((1, block), f32)
+                for q in range(sequences):
+                    value = gconv[q, pl.ds(0, length), lanes]
+                    if k < 4:
+                        value = value * ext[q, pl.ds(8 - k, length), lanes]
+                    total = total + jnp.sum(value, axis=0, keepdims=True)
+                vec_ref[pl.ds(1 + k, 1), lanes] = total
+
+        matrices_plane()
+
+        @pl.when(s + 1 < seq_count)
+        def _():
+            halo_copy(1).wait_recv()
+            for q in range(sequences):
+                gconv[q, pl.ds(length, 8), :] = halos[1, 1, q]
+
+        @pl.when(s + 1 == seq_count)
+        def _():
+            for q in range(sequences):
+                gconv[q, pl.ds(length, 8), :] = jnp.zeros((8, half), f32)
+
+        @pl.loop(0, heads)
+        def _(n):
+            lanes = head_lanes(n)
+            for q in range(sequences):
+                total = cw_ref[pl.ds(0, 1), lanes] * gconv[q, pl.ds(0, length), lanes]
+                for k in range(1, 4):
+                    total = total + cw_ref[pl.ds(k, 1), lanes] * gconv[q, pl.ds(k, length), lanes]
+                adj[pl.ds(q * length, length), lanes] = total
+
+        def own_rows(i):
+            return x_all[pl.ds(pl.multiple_of(tokens + i * 16, 16), 16), pl.ds(0, half)].astype(f32)
+
+        @pl.loop(0, tokens // 16)
+        def _(i):
+            r = pairs(i)
+            product_ = adj[r, :] * (own_rows(i) * scales[0, r, :1])
+            vec_ref[pl.ds(0, 1), :] += jnp.sum(product_, axis=0, keepdims=True)
+            part[2, r, :] = jnp.broadcast_to(jnp.sum(product_ * gain_ref[:, mine], axis=1, keepdims=True), (16, LANES))
+
+        part_copy(2).start()
+        vectors_start(0)
+        matrices_across()
+        part_copy(2).wait_recv()
+
+        @pl.loop(0, tokens // 16)
+        def _(i):
+            r = pairs(i)
+            scale = scales[0, r, :1]
+            hat = own_rows(i) * scale
+            mean = ((part[2, r, :] + part_in[2, r, :]) * (1.0 / model))[:, :1]
+            fin[r, :] = gres[r, :] + scale * (adj[r, :] * gain_ref[:, mine] - hat * mean)
+
+        near = pltpu.make_async_copy(fin, ingrad_ref.at[:, mine], keep.at[3])
+        near.start()
+        away = remote(fin, ingrad_ref.at[:, mine], fin_s.at[0], fin_r.at[0], s, 1 - h)
+        away.start()
+        vectors_sum(0)
+        vectors_start(1)
+        matrices_spread()
+        near_all(3, va, vb)
+        sum_far(2, va, vb)
+
+        res = pltpu.make_async_copy(res_keep, rg, keep.at[4])
+        res.start()
+        res.wait()
+
+        def absorb(src):
+            fetch(src)
+
+            @pl.loop(0, tokens // 64)
+            def _(i):
+                r = pl.ds(pl.multiple_of(i * 64, 64), 64)
+                rg[r, :] += ld[r, :].astype(f32)
+
+        sib_copy(1, 3).wait_recv()
+        absorb(sib_ref.at[1, 3])
+        for k in (1, 2):
+            peer_copy(1, k).wait_recv()
+            absorb(peer_ref.at[1, k])
+
+        @pl.loop(0, tokens // 64)
+        def _(i):
+            r = pl.ds(pl.multiple_of(i * 64, 64), 64)
+            own = g_all[pl.ds(pl.multiple_of(3 * tokens + i * 64, 64), 64), pl.ds(half, half)]
+            ld[r, :] = (rg[r, :] + own.astype(f32)).astype(bf)
+
+        near_out = pltpu.make_async_copy(ld, out_ref.at[:, mine], keep.at[4])
+        near_out.start()
+        away_out = remote(ld, out_ref.at[:, mine], fin_s.at[1], fin_r.at[1], s, 1 - h)
+        away_out.start()
+        sum_far(3, va, vb)
+        vectors_sum(1)
+        matrices_end()
+        near.wait()
+        near_out.wait()
+        away.wait()
+        away_out.wait()
+
+    act = pltpu.VMEM((tokens, half), f32)
+    padded = pltpu.VMEM((sequences, length + 8, half), f32)
+    pl.run_scoped(
+        recur_backward, act, act, act, act, act, padded, padded, pltpu.VMEM((2, block, block), f32),
+    )
+
+    @pl.loop(0, chunks)
+    def _(c):
+        s1_drain(c)
+        for zh_ in range(far):
+            for zl_ in range(2):
+                r1_copy(c, zh_, zl_, False).wait_send()
+        for q in range(1, far):
+            for zl_ in range(2):
+                r2_copy(c, q, zl_).wait_send()
+
+        def sent(width):
+            for d in (1, 2, 3):
+                c3_copy(c, d, width, False).wait_send()
+            c3_own(c, width).wait()
+        by_width(c, wide(zl), sent)
+        for d in (1, 2, 3):
+            by_width(c, wide(peer(d)[2]), lambda width, d=d: c3_copy(c, d, width, True).wait_recv())
+    for k in range(4):
+        sib_copy(1, k).wait_send()
+    for which in range(2):
+        for k in range(3):
+            peer_copy(which, k).wait_send()
+    for i in range(3):
+        part_copy(i).wait_send()
+    pl.when(s + 1 < seq_count)(halo_copy(0).wait_send)
+    pl.when(s > 0)(halo_copy(1).wait_send)
+
+    @pl.loop(1, seq_count)
+    def _(q):
+        pl.when(s + q < seq_count)(lambda: end_copy(0, s + q, s).wait_send())
+        pl.when(s >= q)(lambda: end_copy(1, jnp.maximum(s - q, 0), s).wait_send())
+
+
+def block_pass(seq_count, sequences, x, cotangent, norm_gain, conv_weight, conv_bias, recur_weight, recur_bias,
+               input_weight, input_bias, decay_param, mlp_gain, w_gate, w_up, w_down):
+    tokens, width = x.shape
+    half = width // 2
+    length = tokens // sequences
+    rows, units = w_gate.shape
+    pair, far = 2 * rows, seq_count // 8
+    chunks = -(-units // (4 * CHUNK))
+    span = chunks * CHUNK
+    matrix = (2 * recur_weight.shape[0] * recur_weight.shape[1], recur_weight.shape[2])
+    planes = seq_count // 4
+    bf, f32 = jnp.bfloat16, jnp.float32
+    any_space = pl.BlockSpec(memory_space=pl.ANY)
+    vmem = pl.BlockSpec(memory_space=pltpu.VMEM)
+    outs = [
+        ((tokens, width), bf), ((tokens, width), f32), ((3, rows, units), bf), ((16, half), f32), (matrix, bf),
+        ((chunks, 3, width, CHUNK), bf), ((chunks, 3, 2 * far * pair, CHUNK), bf), ((chunks, 3, 2 * far * pair, CHUNK), bf),
+        ((chunks, far - 1, 3, 2 * pair, CHUNK), bf), ((chunks, 3, 2 * pair, CHUNK), bf),
+        ((2, 4, tokens, half), bf), ((2, 3, tokens, half), bf),
+        ((tokens, half), bf), ((tokens, half), f32), ((tokens, half), f32), ((tokens, half), bf),
+        ((sequences, length + 8, half), f32), ((tokens, half), f32), ((tokens, half), f32),
+        ((3 * matrix[0] // 4, matrix[1]), bf), ((matrix[0] // 4 // planes * (planes - 1), matrix[1]), bf),
+    ]
+    sem = pltpu.SemaphoreType.DMA
+    scratch = [
+        pltpu.VMEM((4 * tokens, width), bf), pltpu.VMEM((4 * tokens, width), bf), pltpu.VMEM((3, width, span), bf),
+        pltpu.VMEM((tokens, half), bf), pltpu.VMEM((2, 2, sequences, 8, half), f32),
+        pltpu.VMEM((2, seq_count, 2 * sequences, half), f32), pltpu.VMEM((sequences, half), f32),
+        pltpu.VMEM((sequences, half), f32), pltpu.VMEM((3, tokens, LANES), f32), pltpu.VMEM((3, tokens, LANES), f32),
+        pltpu.VMEM((2, tokens, LANES), f32), pltpu.VMEM((2 + planes, 16, half), f32),
+    ]
+    for shape in (
+        (2, 3), (2, 4), (chunks, 3, 3), (chunks, far - 1, 2), (chunks, far, 2), (chunks, far, 2),
+        (chunks, far - 1, 2), (chunks, 3), (2, 4), (2, 3), (2,), (2, seq_count), (3,), (2,),
+        (3,), (planes - 1,), (planes - 1,), (3,), (3,), (planes - 1,),
+    ):
+        scratch += [sem(shape), sem(shape)]
+    scratch += [sem((6 + sequences,)), sem((chunks + 1 + far, 3))]
+    rate = jax.nn.softplus(-decay_param)[None]
+    slope = jax.nn.sigmoid(-decay_param)[None]
+    results = pl.pallas_call(
+        functools.partial(block_kernel, seq_count, sequences),
+        out_shape=[jax.ShapeDtypeStruct(shape, kind) for shape, kind in outs],
+        in_specs=[any_space] * 5 + [vmem] * 10,
+        out_specs=[any_space] * 3 + [vmem] + [any_space] * (len(outs) - 4),
+        scratch_shapes=scratch,
+        compiler_params=pltpu.CompilerParams(
+            collective_id=0, has_side_effects=True, vmem_limit_bytes=64 * 2**20 - 2**18
+        ),
+        cost_estimate=pl.CostEstimate(
+            flops=18 * 4 * tokens * width * span, bytes_accessed=150 * 2**20, transcendentals=4 * tokens * span
+        ),
+        name="block_pass",
+    )(x, cotangent, w_gate, w_up, w_down, norm_gain[None], conv_weight, conv_bias[None], recur_weight,
+      recur_bias[None], input_weight, input_bias[None], rate, slope, mlp_gain[None])
+    return results[:5]
+
+
+def gathered_shards(
     block_input,
     norm_gain,
     conv_weight,
@@ -279,6 +1425,56 @@
     )
 
 
+def shards(
+    block_input,
+    norm_gain,
+    conv_weight,
+    conv_bias,
+    recur_weight,
+    recur_bias,
+    input_weight,
+    input_bias,
+    decay_param,
+    mlp_gain,
+    w_gate,
+    w_up,
+    w_down,
+    out_grad,
+):
+    seq_count = lax.axis_size("seq")
+    sequences, span_len, width = block_input.shape
+    if seq_count % 8 or w_gate.shape[0] % 32:
+        return gathered_shards(
+            block_input, norm_gain, conv_weight, conv_bias, recur_weight, recur_bias, input_weight, input_bias,
+            decay_param, mlp_gain, w_gate, w_up, w_down, out_grad,
+        )
+    rows = sequences * span_len
+    stream = block_input.reshape(rows, width)
+    cotangent = out_grad.reshape(rows, width)
+    block_output, input_grad, weight_grads, vectors, matrices = block_pass(
+        seq_count, sequences, stream, cotangent, norm_gain, conv_weight, conv_bias, recur_weight, recur_bias,
+        input_weight, input_bias, decay_param, mlp_gain, w_gate, w_up, w_down,
+    )
+    matrices = matrices.astype(jnp.float32).reshape(2, *recur_weight.shape)
+    gains = lax.all_gather(jnp.stack([vectors[0], vectors[9]]), "head", axis=1, tiled=True)
+    return (
+        block_output.reshape(block_input.shape),
+        input_grad.reshape(block_input.shape),
+        gains[0],
+        vectors[1:5],
+        vectors[5],
+        matrices[0],
+        vectors[6],
+        matrices[1],
+        vectors[7],
+        vectors[8],
+        gains[1],
+        weight_grads[0].astype(jnp.float32),
+        weight_grads[1].astype(jnp.float32),
+        weight_grads[2].astype(jnp.float32),
+    )
+
+
 def solution(mesh):
     placed = (
         P(None, "seq", None),

time: 5480 us -> 652 us (0.12)
  blocking collectives: 3240 us -> 1.95 us
  waiting for transfers between devices: 920 us -> 0 us
  local copies, waits for them, and re-layouts: 730 us -> 18.4 us
  Pallas kernels: 0 us -> 625 us
  other arithmetic: 236 us -> 4.39 us
  matrix products: 179 us -> 0 us
  starting transfers between devices: 128 us -> 0 us
    while x8 -> x0, blocking collectives: 3020 us -> none
    all_gather x5 -> x0, waiting for transfers between devices: 634 us -> none  [the longest x1 211 us: shards(): lax.all_gather(w_gate, 'seq', axis=0, tiled=True)]
    pallas_call x0 -> x1, Pallas kernels: none -> 625 us  [block_pass(): pl.pallas_call(functools.partial(block_kernel, seq_count, sequences), out...]
    while x24 -> x0, waiting for transfers between devices: 242 us -> none
    slice x100 -> x4, local copies, waits for them, and re-layouts: 235 us -> 6.8 us  [the longest x1 3.13 us: shards(): matrices[1]]
    while x48 -> x0, local copies, waits for them, and re-layouts: 210 us -> none
    dot_general x28 -> x0, matrix products: 179 us -> none  [the longest x3 52 us: contract_last(): lax.dot_general(left_side, right_side, (((1,), (1,)), ((), ())), preferre...]
    all_gather x3 -> x1, blocking collectives: 127 us -> 1.95 us  [shards(): lax.all_gather(jnp.stack([vectors[0], vectors[9]]), 'head', axis=1, tiled...]
  transfers between devices with their start and end apart: 33 -> 0, of which waited for: 17 -> 0; matrix products, arithmetic and copies ran while one was open for 65% -> 0% of each run, Pallas kernels for 0% -> 0%
where the time goes in v3:
time: 652 us; the launch traced here: 651 us
  Pallas kernels  625 us (96%)
  local copies, waits for them, and re-layouts  18.4 us (3%)
    pallas_call x1, Pallas kernels, block_pass(): pl.pallas_call(functools.partial(block_kernel, seq_count, sequences), out...  625 us

profile of v3, /device:TPU:0, one launch (start us, length us, event | category | flops | bytes accessed | tf_op | source)
XLA Modules:
  0.0 650.7 jit_solution(18329202563698524967)
XLA Ops:
  0.6 1.3 broadcast_in_dim.22.cb_ref
  1.9 1.3 broadcast_in_dim.23.rb_ref
  3.2 1.3 broadcast_in_dim.24.ib_ref
  4.5 1.3 broadcast_in_dim.21.gain_ref
  5.8 1.3 broadcast_in_dim.27.mgain_ref
  7.2 0.7 add_divide_fusion
  7.9 0.6 broadcast_in_dim.26.sig_ref
  8.5 0.6 broadcast_in_dim.25.rate_ref
  9.1 625.3 %block_pass.1 = (bf16[512,2560]{1,0:T(8,128)(2,1)}, f32[512,2560]{1,0:T(8,128)}, bf16[3,160,3840]{2,1,0:T(8,128)(2,1)}, f32[16,1280]{1,0:T(8,128)}, bf16[2560,25...) custom-call(bf16[512,2560]{1,0:T(8,128)(2,1)} %bitcast.21, ...), custom_call_target="tpu_custom_call" | custom-call | flops 96636764160 | bytes 157286400 | tf_op jit(solution)/shard_map/block_pass/pallas_call | solution.py:1186
  634.4 1.4 slice.47
  635.8 1.6 slice_reduce_fusion.2
  637.4 0.0 copy-start
  637.4 2.0 all_gather.3
  639.4 0.7 slice_reduce_fusion
  640.0 0.0 slice-start
  640.0 3.1 fusion
  643.2 0.0 copy-done
  643.2 0.0 copy-start.1
  643.2 3.7 bitcast_convert_fusion
  646.8 0.0 copy-done.1
  646.8 1.5 copy.30
  648.3 0.0 slice-done
  648.3 0.0 slice-done.1
  648.3 2.4 copy.31
  (3 shorter events, 0.0 us)
Async XLA Ops:
  637.4 5.7 copy-start
  640.0 8.3 %slice-start = ((s8[5242880]{0:T(1024)(128)(4,1)}), s8[4194304]{0:T(1024)(128)(4,1)S(1)}, s32[]{:S(2)}) async-start(s8[5242880]{0:T(1024)(128)(4,1)} %bitcast.15), calls=%async_computation | async-start | bytes 8388608
  643.2 3.7 copy-start.1
  643.2 5.2 slice-start.1

commit v4 on v3

--- a/solution.py
+++ b/solution.py
@@ -100,13 +100,13 @@
 
 def block_kernel(
     seq_count, sequences, x_ref, g_ref, wg_ref, wu_ref, wd_ref,
-    gain_ref, cw_ref, cb_ref, rw_ref, rb_ref, iw_ref, ib_ref, rate_ref, sig_ref, mgain_ref,
+    prm_ref, rw_ref, iw_ref,
     out_ref, ingrad_ref, dw_ref, vec_ref, mat_ref,
-    dh_ref, r1_ref, e_ref, r2_ref, f_ref, sib_ref, peer_ref, xn_half, rg_keep, ig_keep, conv_keep, ext_keep, state_keep,
+    dh_ref, r1_ref, e_ref, r2_ref, sib_ref, peer_ref, xn_half, rg_keep, ig_keep, conv_keep, ext_keep, state_keep,
     res_keep, ma_ref, mb_ref,
     x_all, g_all, w_all, ld, halos, ends_all, ent, arr, part, part_in, scales, vec_in,
     tok_s, tok_r, fwd_s, fwd_r, s1_s, s1_r, z_s, z_r, y_s, y_r, c1_s, c1_r, c2_s, c2_r, c3_s, c3_r,
-    sib_s, sib_r, peer_s, peer_r, halo_s, halo_r, end_s, end_r, part_s, part_r, fin_s, fin_r, ma_s, ma_r, mb_s, mb_r, mc_s, mc_r, md_s, md_r, va_s, va_r, vb_s, vb_r, keep, loc,
+    sib_s, sib_r, peer_s, peer_r, halo_s, halo_r, end_s, end_r, part_s, part_r, fin_s, fin_r, ma_s, ma_r, mb_s, mb_r, mc_s, mc_r, md_s, md_r, va_s, va_r, vb_s, vb_r, sums, keep, loc,
 ):
     far = seq_count // 8
     rows = wg_ref.shape[0]
@@ -163,6 +163,8 @@
     block = rw_ref.shape[1]
     heads = half // block
     f32, bf = jnp.float32, jnp.bfloat16
+    gain_ref, mgain_ref, cb_ref, rb_ref, ib_ref, rate_ref, sig_ref = [prm_ref.at[pl.ds(i, 1)] for i in range(7)]
+    cw_ref = prm_ref.at[pl.ds(8, 4)]
     greet_all(seq_count, s, h)
 
     def s1_send(c, d, w, width):
@@ -226,12 +228,11 @@
         part = w_all.at[:, block_rows((zh - q + far) % far, zl_, 1 - y if incoming else y), cols(c, width)]
         return remote(part, part, y_s.at[c, q, zl_], y_r.at[c, q, zl_], y_seq, h)
 
-    def z_start(c):
+    def z_start(c, halves=(0, 1)):
         def go(width):
-            for q in range(1, far):
-                for zl_ in range(2):
+            for zl_ in halves:
+                for q in range(1, far):
                     z_copy(c, q, zl_, width, False).start()
-            for zl_ in range(2):
                 y_copy(c, 0, zl_, width, False).start()
         by_width(c, wide(zl), go)
 
@@ -303,100 +304,115 @@
         for d in ((1, 2, 3) if k else (0, 1, 2, 3)):
             fwd_copy(k, d, True).wait_recv()
 
-    def r1_copy(c, zh_, zl_, incoming):
+    def r1_copy(c, zh_, zl_, width):
+        lanes = pl.ds(0, width)
         return remote(
-            dh_ref.at[c, :, block_rows(zh_, zl_, 1 - y), :], r1_ref.at[c, :, pl.ds((zh_ * 2 + zl_) * pair, pair)],
+            dh_ref.at[c, :, block_rows(zh_, zl_, 1 - y), lanes],
+            r1_ref.at[c, :, pl.ds(pl.multiple_of((zh_ * 2 + zl_) * pair, 32), pair), lanes],
             c1_s.at[c, zh_, zl_], c1_r.at[c, zh_, zl_], y_seq, h,
         )
 
     def r1_start(c, steps_away):
-        for q in steps_away:
-            for zl_ in range(2):
-                r1_copy(c, (zh + q) % far, zl_, False).start()
-
-    def r2_copy(c, q, zl_):
-        return remote(
-            e_ref.at[c, :, pl.ds(pl.multiple_of((((zh + q) % far) * 2 + zl_) * pair, 32), pair)], r2_ref.at[c, q - 1, :, pl.ds(zl_ * pair, pair)],
-            c2_s.at[c, q - 1, zl_], c2_r.at[c, q - 1, zl_], z_seq(q), h,
-        )
-
-    def add_into(first, second, blocks):
+        def go(width):
+            for q in steps_away:
+                for zl_ in range(2):
+                    r1_copy(c, (zh + q) % far, zl_, width).start()
+        by_width(c, wide(zl), go)
+
+    def plane_rows(zh_):
+        return pl.ds(pl.multiple_of(zh_ * 2 * pair, 32), 2 * pair)
+
+    def r2_copy(c, q, width, src=None):
+        lanes = pl.ds(0, width)
+        if src is None:
+            src = e_ref.at[c, :, plane_rows((zh + q) % far), lanes]
+        else:
+            src = src.at[:, :, lanes]
+        return remote(src, r2_ref.at[c, q - 1, :, :, lanes], c2_s.at[c, q - 1], c2_r.at[c, q - 1], z_seq(q), h)
+
+    def r2_start(c, q, src=None):
+        by_width(c, wide(zl), lambda width: r2_copy(c, q, width, src).start())
+
+    def add_into(first, second):
         @pl.loop(0, 3)
         def _(w):
-            @pl.loop(0, blocks)
+            @pl.loop(0, 2)
             def _(b):
                 r = pl.ds(pl.multiple_of(b * pair, 32), pair)
-                total = first[w, r, :].astype(jnp.float32) + second[w, r, :].astype(jnp.float32)
-                first[w, r, :] = total.astype(jnp.bfloat16)
-
-    def plane_rows(zh_):
-        return pl.ds(pl.multiple_of(zh_ * 2 * pair, 32), 2 * pair)
-
-    def sum_near(c, q, va, vb):
+                first[w, r, :] = first[w, r, :] + second[w, r, :]
+
+    def near_loads(c, q, first, second):
         zh_ = (zh + q) % far
-        loads = []
-        for zl_ in range(2):
-            loads.append(pltpu.make_async_copy(
-                dh_ref.at[c, :, block_rows(zh_, zl_, y), :], va.at[:, pl.ds(zl_ * pair, pair)], loc.at[chunks + 1, zl_]
-            ))
-            loads[-1].start()
-        for zl_ in range(2):
-            r1_copy(c, zh_, zl_, True).wait_recv()
-        loads.append(pltpu.make_async_copy(r1_ref.at[c, :, plane_rows(zh_)], vb, loc.at[chunks, 2]))
-        loads[-1].start()
-        for load in loads:
+        loads = [
+            pltpu.make_async_copy(
+                dh_ref.at[c, :, block_rows(zh_, zl_, y), :], first.at[:, pl.ds(zl_ * pair, pair)], sums.at[c, q, zl_]
+            )
+            for zl_ in range(2)
+        ]
+        return loads + [pltpu.make_async_copy(r1_ref.at[c, :, plane_rows(zh_)], second, sums.at[c, q, 2])]
+
+    def near_store(c, q, first):
+        return pltpu.make_async_copy(first, e_ref.at[c, :, plane_rows((zh + q) % far)], sums.at[c, q, 3])
+
+    def near_issue(c, q, first, second):
+        def got(width):
+            for zl_ in range(2):
+                r1_copy(c, (zh + q) % far, zl_, width).wait_recv()
+        by_width(c, wide(zl), got)
+        for load in near_loads(c, q, first, second):
+            load.start()
+
+    def near_finish(c, q, first, second, direct):
+        for load in near_loads(c, q, first, second):
             load.wait()
-        add_into(va, vb, 2)
-        back = pltpu.make_async_copy(va, e_ref.at[c, :, plane_rows(zh_)], loc.at[chunks, 2])
-        back.start()
-        back.wait()
+        add_into(first, second)
+        if direct and q:
+            r2_start(c, q, first)
+        else:
+            near_store(c, q, first).start()
+
+    def near_send(c, q, first):
+        near_store(c, q, first).wait()
         if q:
-            for zl_ in range(2):
-                r2_copy(c, q, zl_).start()
-
-    def near_all(c, va, vb):
-        for q in list(range(1, far)) + [0]:
-            sum_near(c, q, va, vb)
-
-    def c3_copy(c, d, width, incoming):
+            r2_start(c, q)
+
+    def far_loads(c, first, second):
+        return [
+            pltpu.make_async_copy(e_ref.at[c, :, plane_rows(zh)], first, sums.at[c, 0, 0]),
+            pltpu.make_async_copy(r2_ref.at[c, 0], second, sums.at[c, 0, 1]),
+        ]
+
+    def far_issue(c, first, second):
+        by_width(c, wide(zl), lambda width: r2_copy(c, 1, width).wait_recv())
+        for load in far_loads(c, first, second):
+            load.start()
+
+    def far_finish(c, first, second):
+        for load in far_loads(c, first, second):
+            load.wait()
+        add_into(first, second)
+
+        def go(width):
+            for d in (1, 2, 3):
+                c3_copy(c, d, width, False, first).start()
+            c3_own(c, width, first).start()
+        by_width(c, wide(zl), go)
+
+    def c3_copy(c, d, width, incoming, src):
         a_, seq, zl_, x_ = peer(d)
         col = pl.multiple_of((first_tile(a_ if incoming else a) + 2 * c) * LANES, LANES)
         return remote(
-            f_ref.at[c, :, pl.ds(pl.multiple_of((zl_ * 2 + x_) * rows, 32), rows), pl.ds(0, width)],
+            src.at[:, pl.ds(pl.multiple_of((zl_ * 2 + x_) * rows, 32), rows), pl.ds(0, width)],
             dw_ref.at[:, :, pl.ds(col, width)],
             c3_s.at[c, d - 1], c3_r.at[c, d - 1], seq, h,
         )
 
-    def c3_own(c, width):
+    def c3_own(c, width, src):
         col = pl.multiple_of((first_tile(a) + 2 * c) * LANES, LANES)
         return pltpu.make_async_copy(
-            f_ref.at[c, :, pl.ds(pl.multiple_of(a * rows, 32), rows), pl.ds(0, width)],
+            src.at[:, pl.ds(pl.multiple_of(a * rows, 32), rows), pl.ds(0, width)],
             dw_ref.at[:, :, pl.ds(col, width)], loc.at[c, 0],
         )
-
-    def sum_far(c, va, vb):
-        first, second = va, vb
-        kept = pltpu.make_async_copy(
-            e_ref.at[c, :, pl.ds(pl.multiple_of(zh * 2 * pair, 32), 2 * pair)], first, loc.at[chunks, 0]
-        )
-        kept.start()
-        kept.wait()
-        for q in range(1, far):
-            for zl_ in range(2):
-                r2_copy(c, q, zl_).wait_recv()
-            other = pltpu.make_async_copy(r2_ref.at[c, q - 1], second, loc.at[chunks, 0])
-            other.start()
-            other.wait()
-            add_into(va, vb, 2)
-        back = pltpu.make_async_copy(first, f_ref.at[c], loc.at[chunks, 0])
-        back.start()
-        back.wait()
-
-        def go(width):
-            for d in (1, 2, 3):
-                c3_copy(c, d, width, False).start()
-            c3_own(c, width).start()
-        by_width(c, wide(zl), go)
 
     def forward_chunk(c, hid, gg, gu):
         @pl.loop(0, 4)
@@ -436,9 +452,64 @@
     def head_lanes(n):
         return pl.ds(pl.multiple_of(n * block, block), block)
 
-    def end_copy(side, target, source):
+    def near_copy(side, k, incoming):
+        source = (place - k + 4) % 4 if incoming else place
         part_ends = ends_all.at[side, source]
-        return remote(part_ends, part_ends, end_s.at[side, target], end_r.at[side, source], target, h)
+        return remote(part_ends, part_ends, end_s.at[side, k - 1], end_r.at[side, k - 1], mate(k), h)
+
+    def far_copy(side, j, incoming):
+        step = -j if (side == 0) == incoming else j
+        source = plane + step if incoming else plane
+        target = plane if incoming else plane + step
+        bound = jnp.clip(source, 0, planes - 1), jnp.clip(target, 0, planes - 1)
+        part_ends = ends_all.at[side, 4 + bound[0]]
+        return remote(
+            part_ends, part_ends, end_s.at[side, 2 + j], end_r.at[side, 2 + j], bound[1] * 4 + place, h
+        )
+
+    def far_exists(side, incoming, j):
+        if (side == 0) == incoming:
+            return plane >= j
+        return plane + j < planes
+
+    def ends_near(side):
+        for k in (1, 2, 3):
+            near_copy(side, k, False).start()
+
+    def follow(total, got):
+        return total[0] * got[:sequences], got[:sequences] * total[1] + got[sequences:]
+
+    def ends_far(side):
+        for k in (1, 2, 3):
+            near_copy(side, k, True).wait_recv()
+        order = range(4) if side == 0 else range(3, -1, -1)
+        total = jnp.ones((sequences, half), f32), jnp.zeros((sequences, half), f32)
+        for p in order:
+            total = follow(total, ends_all[side, p])
+        ends_all[side, 4 + plane, pl.ds(0, sequences), :] = total[0]
+        ends_all[side, 4 + plane, pl.ds(sequences, sequences), :] = total[1]
+        for j in range(1, planes):
+            pl.when(far_exists(side, False, j))(far_copy(side, j, False).start)
+
+    def ends_fold(side, out):
+        out[...] = jnp.zeros_like(out)
+        for j in range(planes - 1, 0, -1):
+            @pl.when(far_exists(side, True, j))
+            def _(j=j):
+                far_copy(side, j, True).wait_recv()
+                got = ends_all[side, 4 + (jnp.maximum(plane - j, 0) if side == 0 else jnp.minimum(plane + j, planes - 1))]
+                out[...] = got[:sequences] * out[...] + got[sequences:]
+        for p in range(4) if side == 0 else range(3, -1, -1):
+            @pl.when(p < place if side == 0 else p > place)
+            def _(p=p):
+                got = ends_all[side, p]
+                out[...] = got[:sequences] * out[...] + got[sequences:]
+
+    def ends_drain(side):
+        for k in (1, 2, 3):
+            near_copy(side, k, False).wait_send()
+        for j in range(1, planes):
+            pl.when(far_exists(side, False, j))(far_copy(side, j, False).wait_send)
 
     def part_copy(i):
         return remote(part.at[i], part_in.at[i], part_s.at[i], part_r.at[i], s, 1 - h)
@@ -560,10 +631,7 @@
             total = total + vec_in[(0, 3)[level] + k - 1]
         vec_ref[...] = total
 
-    s1_start(0)
-    s1_start(1)
     own_g.start()
-    tok_start(1)
 
     @pl.when(jnp.logical_not(wide(zl)))
     def _():
@@ -579,11 +647,13 @@
             scale = lax.rsqrt(jnp.sum(full * full, axis=1, keepdims=True) * (1.0 / model) + EPS)
             scales[0, pl.ds(r, count), :] = jnp.broadcast_to(scale, (count, LANES))
             own = xin[pl.ds(r, count), mine].astype(f32)
-            return ((own * scale) * gain_ref[:, mine]).astype(bf).astype(f32)
+            return ((own * scale) * gain_ref[...]).astype(bf).astype(f32)
 
         for q in range(sequences):
             halos[0, 0, q] = normed(q * length + length - 16, 16)[8:]
         pl.when(s + 1 < seq_count)(halo_copy(0).start)
+        s1_start(0)
+        s1_start(1)
         for q in range(sequences):
             @pl.loop(0, length // 16)
             def _(i, q=q):
@@ -603,10 +673,6 @@
 
         saves = [pltpu.make_async_copy(ext, ext_keep, keep.at[0])]
         saves[0].start()
-        s1_wait(0)
-        z_start(0)
-        s1_start(2)
-
         @pl.loop(0, heads)
         def _(n):
             lanes = head_lanes(n)
@@ -630,9 +696,6 @@
         for i, (src, dst) in enumerate(((rg, rg_keep), (ig, ig_keep), (conv, conv_keep))):
             saves.append(pltpu.make_async_copy(src, dst, keep.at[1 + i]))
             saves[-1].start()
-        s1_wait(1)
-        z_start(1)
-        s1_start(3)
 
         def scan_group(g, carry):
             out = []
@@ -655,23 +718,15 @@
             first += [jnp.zeros((1, half), f32), jnp.ones((1, half), f32)]
         last = lax.fori_loop(0, groups, scan_group, tuple(first))
         for q in range(sequences):
-            ends_all[0, s, pl.ds(q, 1), :] = last[2 * q + 1]
-            ends_all[0, s, pl.ds(sequences + q, 1), :] = last[2 * q]
-
-        @pl.loop(1, seq_count)
-        def _(q):
-            pl.when(s + q < seq_count)(lambda: end_copy(0, s + q, s).start())
-
-        tok_turn(1)
-        ent[...] = jnp.zeros_like(ent)
-
-        @pl.loop(0, seq_count)
-        def _(source):
-            @pl.when(source < s)
-            def _():
-                end_copy(0, s, source).wait_recv()
-                got = ends_all[0, source]
-                ent[...] = got[:sequences] * ent[...] + got[sequences:]
+            ends_all[0, place, pl.ds(q, 1), :] = last[2 * q + 1]
+            ends_all[0, place, pl.ds(sequences + q, 1), :] = last[2 * q]
+        ends_near(0)
+        ends_far(0)
+        s1_wait(0)
+        z_start(0)
+        tok_start(1)
+        own_g.wait()
+        ends_fold(0, ent)
 
         for q in range(sequences):
             @pl.loop(0, length // 16)
@@ -694,7 +749,7 @@
             r = pairs(i)
             scale = lax.rsqrt((part[0, r, :] + part_in[0, r, :]) * (1.0 / model) + EPS)
             scales[1, r, :] = scale
-            ld[r, :] = ((prod[r, :] * scale[:, :1]) * mgain_ref[:, mine]).astype(bf)
+            ld[r, :] = ((prod[r, :] * scale[:, :1]) * mgain_ref[...]).astype(bf)
 
         saves.append(pltpu.make_async_copy(ld, xn_half, keep.at[6]))
         saves[-1].start()
@@ -709,18 +764,21 @@
     )
     tok_start(0)
     own_x.start()
+    s1_start(2)
+    s1_wait(1)
+    z_start(1)
+    own_x.wait()
+    fwd_copy(0, 0, False).start()
+    tok_turn(1)
+    s1_start(3)
+    z_forward(0)
     s1_wait(2)
     z_start(2)
+    tok_last(1)
+    tok_turn(0)
+    z_forward(1)
     s1_wait(3)
     z_start(3)
-    own_x.wait()
-    fwd_copy(0, 0, False).start()
-    z_forward(0)
-    own_g.wait()
-    tok_turn(0)
-    tok_last(1)
-    z_forward(1)
-    z_forward(2)
     tok_last(0)
     tok_wait(1)
     tok_wait(0)
@@ -757,8 +815,7 @@
         def _(i):
             r = pl.ds(pl.multiple_of(k * tokens + i * 64, 64), 64)
             lanes = pl.ds(half, half)
-            total = stage[which][r, lanes].astype(f32) + ld[pl.ds(pl.multiple_of(i * 64, 64), 64), :].astype(f32)
-            stage[which][r, lanes] = total.astype(bf)
+            stage[which][r, lanes] = stage[which][r, lanes] + ld[pl.ds(pl.multiple_of(i * 64, 64), 64), :]
 
     def combine(which, k):
         sib_copy(which, k).wait_recv()
@@ -783,21 +840,29 @@
         sib_copy(which, k).start()
         one(h, half)
 
-    def feed_forward(hid, gg, gu, dv, va, vb):
+    def feed_forward(hid, gg, gu, dv, sum_bufs):
+        bufs = [(sum_bufs.at[0], sum_bufs.at[1]), (sum_bufs.at[2], sum_bufs.at[3])]
+
         @pl.loop(0, chunks)
         def _(c):
             y_wait(c)
             forward_chunk(c, hid, gg, gu)
             weight_chunk(c, hid, gg, gu, dv)
             away, near = range(1, far), (0,)
-            pl.when(c == 0)(lambda: r1_start(0, away))
+
+
+            @pl.when(c == 0)
+            def _():
+                z_forward(2)
+                r1_start(0, away)
 
             @pl.when(c == 1)
             def _():
                 z_forward(3)
                 r1_start(0, near)
 
-            pl.when(c >= 1)(lambda: r1_start(c, (*away, *near)))
+            pl.when((c >= 1) & (c < chunks - 1))(lambda: r1_start(c, (*away, *near)))
+            pl.when(c == chunks - 1)(lambda: r1_start(c, away))
 
         for k in (0, 1, 2, 3):
             for d in (1, 2, 3) if k == 0 else ():
@@ -806,27 +871,50 @@
                     fwd_copy(i, d, False).wait_send()
             if k == 0:
                 fwd_copy(0, 0, False).wait_send()
+            if k == 2:
+                near_issue(0, 1, *bufs[0])
+            if k == 3:
+                near_finish(0, 1, *bufs[0], False)
             compute_sums(0, k, hid, gg, gu)
             if k in (1, 2):
                 combine(0, k - 1)
-            if k == 1:
-                near_all(0, va, vb)
-
-        @pl.loop(0, 4)
-        def _(k):
-            compute_sums(1, k, hid, gg, gu)
+        near_send(0, 1, bufs[0][0])
+        near_issue(0, 0, *bufs[1])
+        compute_sums(1, 0, hid, gg, gu)
+        near_finish(0, 0, *bufs[1], False)
+        compute_sums(1, 1, hid, gg, gu)
         combine(0, 2)
-        near_all(1, va, vb)
-        sum_far(0, va, vb)
+        near_issue(1, 1, *bufs[0])
+        compute_sums(1, 2, hid, gg, gu)
+        near_finish(1, 1, *bufs[0], False)
+        near_send(0, 0, bufs[1][0])
+        compute_sums(1, 3, hid, gg, gu)
+        near_send(1, 1, bufs[0][0])
 
     wide_buf = pltpu.VMEM((4 * tokens, span), bf)
     pl.run_scoped(
         feed_forward, wide_buf, wide_buf, wide_buf, pltpu.VMEM((3, model, CHUNK), bf),
-        pltpu.VMEM((3, 2 * pair, CHUNK), bf), pltpu.VMEM((3, 2 * pair, CHUNK), bf),
+        pltpu.VMEM((4, 3, 2 * pair, CHUNK), bf),
     )
     pl.loop(0, chunks)(zy_drain)
     held = 2 * pair
-    va, vb = w_all.at[:, pl.ds(0, held), pl.ds(0, CHUNK)], w_all.at[:, pl.ds(held, held), pl.ds(0, CHUNK)]
+
+    def hold(row, col):
+        return w_all.at[:, pl.ds(row * held, held), pl.ds(col * CHUNK, CHUNK)]
+
+    near_slots = {
+        (1, 0): (hold(0, 3), hold(1, 3)), (2, 1): (hold(0, 0), hold(1, 0)), (2, 0): (hold(2, 0), hold(3, 0)),
+        (3, 1): (hold(0, 1), hold(1, 1)), (3, 0): (hold(2, 1), hold(3, 1)),
+    }
+    far_slots = [
+        (hold(2, 3), hold(3, 3)), (hold(1, 3), hold(1, 0)), (hold(3, 0), hold(1, 1)), (hold(3, 1), hold(3, 3)),
+    ]
+
+    def near_first(c, q):
+        near_issue(c, q, *near_slots[c, q])
+
+    def near_last(c, q):
+        near_finish(c, q, *near_slots[c, q], True)
 
     def recur_backward(fin, adj, gres, rg, ig, gconv, ext, wsum):
         spare = [x_all.at[slot(k), pl.ds(0, half)] for k in range(4)]
@@ -864,8 +952,6 @@
         peer_copy(0, 1).wait_recv()
         fetch(peer_ref.at[0, 1])
         widen(False)
-        combine(1, 0)
-        combine(1, 1)
         vec_ref[...] = jnp.zeros_like(vec_ref)
         for load in loads:
             load.wait()
@@ -876,9 +962,12 @@
             def _(i, q=q):
                 r = pl.ds(pl.multiple_of(q * length + i * 16, 16), 16)
                 gconv[q, pairs(i), :] = jnp.exp(-8.0 * rate_ref[...] * rg[r, :])
+        near_first(1, 0)
         peer_copy(0, 2).wait_recv()
         fetch(peer_ref.at[0, 2])
         widen(False)
+        near_last(1, 0)
+        combine(1, 0)
 
         @pl.loop(0, tokens // 16)
         def _(i):
@@ -886,9 +975,11 @@
             hat = adj[r, :] * scales[1, r, :1]
             product_ = fin[r, :] * hat
             vec_ref[pl.ds(9, 1), :] += jnp.sum(product_, axis=0, keepdims=True)
-            part[1, r, :] = jnp.broadcast_to(jnp.sum(product_ * mgain_ref[:, mine], axis=1, keepdims=True), (16, LANES))
+            part[1, r, :] = jnp.broadcast_to(jnp.sum(product_ * mgain_ref[...], axis=1, keepdims=True), (16, LANES))
 
         part_copy(1).start()
+        near_send(1, 0, near_slots[1, 0][0])
+        far_issue(0, *far_slots[0])
         part_copy(1).wait_recv()
 
         @pl.loop(0, tokens // 16)
@@ -898,7 +989,9 @@
             hat = adj[r, :] * scale
             mean = ((part[1, r, :] + part_in[1, r, :]) * (1.0 / model))[:, :1]
             own = x_all[pl.ds(pl.multiple_of(2 * tokens + i * 16, 16), 16), pl.ds(0, half)].astype(f32)
-            gres[r, :] = own + scale * (fin[r, :] * mgain_ref[:, mine] - hat * mean)
+            gres[r, :] = own + scale * (fin[r, :] * mgain_ref[...] - hat * mean)
+
+        far_finish(0, *far_slots[0])
 
         def scan_group(i, carry):
             g = groups - 1 - i
@@ -925,24 +1018,14 @@
             first += [jnp.zeros((1, half), f32), one, one]
         last = lax.fori_loop(0, groups, scan_group, tuple(first))
         for q in range(sequences):
-            ends_all[1, s, pl.ds(q, 1), :] = last[3 * q + 1] * last[3 * q + 2]
-            ends_all[1, s, pl.ds(sequences + q, 1), :] = last[3 * q] * last[3 * q + 2]
-
-        @pl.loop(1, seq_count)
-        def _(q):
-            pl.when(s >= q)(lambda: end_copy(1, jnp.maximum(s - q, 0), s).start())
-
-        arr[...] = jnp.zeros_like(arr)
-
-        @pl.loop(1, seq_count)
-        def _(q):
-            source = seq_count - q
-
-            @pl.when(source > s)
-            def _():
-                end_copy(1, s, source).wait_recv()
-                got = ends_all[1, source]
-                arr[...] = got[:sequences] * arr[...] + got[sequences:]
+            ends_all[1, place, pl.ds(q, 1), :] = last[3 * q + 1] * last[3 * q + 2]
+            ends_all[1, place, pl.ds(sequences + q, 1), :] = last[3 * q] * last[3 * q + 2]
+        ends_near(1)
+        ends_far(1)
+        r1_start(chunks - 1, (0,))
+        near_first(2, 1)
+        combine(1, 1)
+        ends_fold(1, arr)
 
         for q in range(sequences):
             @pl.loop(0, length // 16)
@@ -950,9 +1033,9 @@
                 r = pl.ds(pl.multiple_of(q * length + i * 16, 16), 16)
                 adj[r, :] += fin[r, :] * arr[pl.ds(q, 1), :]
 
-        near_all(2, va, vb)
+        near_last(2, 1)
+        near_first(2, 0)
         combine(1, 2)
-        sum_far(1, va, vb)
 
         @pl.loop(0, heads)
         def _(n):
@@ -993,10 +1076,13 @@
             vec_ref[pl.ds(6, 1), lanes] = sums[1]
             vec_ref[pl.ds(7, 1), lanes] = sums[2]
 
+        near_last(2, 0)
         for q in range(sequences):
             halos[1, 0, q] = gconv[q, pl.ds(0, 8), :]
         pl.when(s > 0)(halo_copy(1).start)
         matrices_start()
+        far_issue(1, *far_slots[1])
+        near_send(2, 0, near_slots[2, 0][0])
         again = pltpu.make_async_copy(ext_keep, ext, keep.at[2])
         again.start()
         again.wait()
@@ -1013,7 +1099,7 @@
                     total = total + jnp.sum(value, axis=0, keepdims=True)
                 vec_ref[pl.ds(1 + k, 1), lanes] = total
 
-        matrices_plane()
+        far_finish(1, *far_slots[1])
 
         @pl.when(s + 1 < seq_count)
         def _():
@@ -1035,6 +1121,9 @@
                     total = total + cw_ref[pl.ds(k, 1), lanes] * gconv[q, pl.ds(k, length), lanes]
                 adj[pl.ds(q * length, length), lanes] = total
 
+        near_first(3, 1)
+        near_last(3, 1)
+
         def own_rows(i):
             return x_all[pl.ds(pl.multiple_of(tokens + i * 16, 16), 16), pl.ds(0, half)].astype(f32)
 
@@ -1043,11 +1132,11 @@
             r = pairs(i)
             product_ = adj[r, :] * (own_rows(i) * scales[0, r, :1])
             vec_ref[pl.ds(0, 1), :] += jnp.sum(product_, axis=0, keepdims=True)
-            part[2, r, :] = jnp.broadcast_to(jnp.sum(product_ * gain_ref[:, mine], axis=1, keepdims=True), (16, LANES))
+            part[2, r, :] = jnp.broadcast_to(jnp.sum(product_ * gain_ref[...], axis=1, keepdims=True), (16, LANES))
 
         part_copy(2).start()
         vectors_start(0)
-        matrices_across()
+        matrices_plane()
         part_copy(2).wait_recv()
 
         @pl.loop(0, tokens // 16)
@@ -1056,17 +1145,21 @@
             scale = scales[0, r, :1]
             hat = own_rows(i) * scale
             mean = ((part[2, r, :] + part_in[2, r, :]) * (1.0 / model))[:, :1]
-            fin[r, :] = gres[r, :] + scale * (adj[r, :] * gain_ref[:, mine] - hat * mean)
+            fin[r, :] = gres[r, :] + scale * (adj[r, :] * gain_ref[...] - hat * mean)
 
         near = pltpu.make_async_copy(fin, ingrad_ref.at[:, mine], keep.at[3])
         near.start()
         away = remote(fin, ingrad_ref.at[:, mine], fin_s.at[0], fin_r.at[0], s, 1 - h)
         away.start()
+        near_first(3, 0)
+        matrices_across()
+        near_last(3, 0)
         vectors_sum(0)
         vectors_start(1)
+        far_issue(2, *far_slots[2])
+        near_send(3, 0, near_slots[3, 0][0])
+        far_finish(2, *far_slots[2])
         matrices_spread()
-        near_all(3, va, vb)
-        sum_far(2, va, vb)
 
         res = pltpu.make_async_copy(res_keep, rg, keep.at[4])
         res.start()
@@ -1096,8 +1189,9 @@
         near_out.start()
         away_out = remote(ld, out_ref.at[:, mine], fin_s.at[1], fin_r.at[1], s, 1 - h)
         away_out.start()
-        sum_far(3, va, vb)
         vectors_sum(1)
+        far_issue(3, *far_slots[3])
+        far_finish(3, *far_slots[3])
         matrices_end()
         near.wait()
         near_out.wait()
@@ -1110,23 +1204,20 @@
         recur_backward, act, act, act, act, act, padded, padded, pltpu.VMEM((2, block, block), f32),
     )
 
-    @pl.loop(0, chunks)
-    def _(c):
+    for c in range(chunks):
         s1_drain(c)
-        for zh_ in range(far):
-            for zl_ in range(2):
-                r1_copy(c, zh_, zl_, False).wait_send()
-        for q in range(1, far):
-            for zl_ in range(2):
-                r2_copy(c, q, zl_).wait_send()
-
-        def sent(width):
+
+        def sent(width, c=c):
+            for zh_ in range(far):
+                for zl_ in range(2):
+                    r1_copy(c, zh_, zl_, width).wait_send()
+            r2_copy(c, 1, width).wait_send()
             for d in (1, 2, 3):
-                c3_copy(c, d, width, False).wait_send()
-            c3_own(c, width).wait()
+                c3_copy(c, d, width, False, far_slots[c][0]).wait_send()
+            c3_own(c, width, far_slots[c][0]).wait()
         by_width(c, wide(zl), sent)
         for d in (1, 2, 3):
-            by_width(c, wide(peer(d)[2]), lambda width, d=d: c3_copy(c, d, width, True).wait_recv())
+            by_width(c, wide(peer(d)[2]), lambda width, d=d, c=c: c3_copy(c, d, width, True, far_slots[c][0]).wait_recv())
     for k in range(4):
         sib_copy(1, k).wait_send()
     for which in range(2):
@@ -1137,10 +1228,8 @@
     pl.when(s + 1 < seq_count)(halo_copy(0).wait_send)
     pl.when(s > 0)(halo_copy(1).wait_send)
 
-    @pl.loop(1, seq_count)
-    def _(q):
-        pl.when(s + q < seq_count)(lambda: end_copy(0, s + q, s).wait_send())
-        pl.when(s >= q)(lambda: end_copy(1, jnp.maximum(s - q, 0), s).wait_send())
+    ends_drain(0)
+    ends_drain(1)
 
 
 def block_pass(seq_count, sequences, x, cotangent, norm_gain, conv_weight, conv_bias, recur_weight, recur_bias,
@@ -1160,7 +1249,7 @@
     outs = [
         ((tokens, width), bf), ((tokens, width), f32), ((3, rows, units), bf), ((16, half), f32), (matrix, bf),
         ((chunks, 3, width, CHUNK), bf), ((chunks, 3, 2 * far * pair, CHUNK), bf), ((chunks, 3, 2 * far * pair, CHUNK), bf),
-        ((chunks, far - 1, 3, 2 * pair, CHUNK), bf), ((chunks, 3, 2 * pair, CHUNK), bf),
+        ((chunks, far - 1, 3, 2 * pair, CHUNK), bf),
         ((2, 4, tokens, half), bf), ((2, 3, tokens, half), bf),
         ((tokens, half), bf), ((tokens, half), f32), ((tokens, half), f32), ((tokens, half), bf),
         ((sequences, length + 8, half), f32), ((tokens, half), f32), ((tokens, half), f32),
@@ -1170,23 +1259,28 @@
     scratch = [
         pltpu.VMEM((4 * tokens, width), bf), pltpu.VMEM((4 * tokens, width), bf), pltpu.VMEM((3, width, span), bf),
         pltpu.VMEM((tokens, half), bf), pltpu.VMEM((2, 2, sequences, 8, half), f32),
-        pltpu.VMEM((2, seq_count, 2 * sequences, half), f32), pltpu.VMEM((sequences, half), f32),
+        pltpu.VMEM((2, 4 + planes, 2 * sequences, half), f32), pltpu.VMEM((sequences, half), f32),
         pltpu.VMEM((sequences, half), f32), pltpu.VMEM((3, tokens, LANES), f32), pltpu.VMEM((3, tokens, LANES), f32),
         pltpu.VMEM((2, tokens, LANES), f32), pltpu.VMEM((2 + planes, 16, half), f32),
     ]
     for shape in (
         (2, 3), (2, 4), (chunks, 3, 3), (chunks, far - 1, 2), (chunks, far, 2), (chunks, far, 2),
-        (chunks, far - 1, 2), (chunks, 3), (2, 4), (2, 3), (2,), (2, seq_count), (3,), (2,),
+        (chunks, far - 1), (chunks, 3), (2, 4), (2, 3), (2,), (2, 2 + planes), (3,), (2,),
         (3,), (planes - 1,), (planes - 1,), (3,), (3,), (planes - 1,),
     ):
         scratch += [sem(shape), sem(shape)]
-    scratch += [sem((6 + sequences,)), sem((chunks + 1 + far, 3))]
-    rate = jax.nn.softplus(-decay_param)[None]
-    slope = jax.nn.sigmoid(-decay_param)[None]
+    scratch += [sem((chunks, far, 4)), sem((6 + sequences,)), sem((chunks + 1 + far, 3))]
+    first = lax.axis_index("head") * half
+    norm_half = lax.dynamic_slice_in_dim(norm_gain, first, half, 0)
+    mlp_half = lax.dynamic_slice_in_dim(mlp_gain, first, half, 0)
+    rate = jax.nn.softplus(-decay_param)
+    slope = jax.nn.sigmoid(-decay_param)
+    vectors = [norm_half, mlp_half, conv_bias, recur_bias, input_bias, rate, slope, slope]
+    params = jnp.concatenate([jnp.stack(vectors), conv_weight, jnp.zeros_like(conv_weight)])
     results = pl.pallas_call(
         functools.partial(block_kernel, seq_count, sequences),
         out_shape=[jax.ShapeDtypeStruct(shape, kind) for shape, kind in outs],
-        in_specs=[any_space] * 5 + [vmem] * 10,
+        in_specs=[any_space] * 5 + [vmem] * 3,
         out_specs=[any_space] * 3 + [vmem] + [any_space] * (len(outs) - 4),
         scratch_shapes=scratch,
         compiler_params=pltpu.CompilerParams(
@@ -1196,8 +1290,7 @@
             flops=18 * 4 * tokens * width * span, bytes_accessed=150 * 2**20, transcendentals=4 * tokens * span
         ),
         name="block_pass",
-    )(x, cotangent, w_gate, w_up, w_down, norm_gain[None], conv_weight, conv_bias[None], recur_weight,
-      recur_bias[None], input_weight, input_bias[None], rate, slope, mlp_gain[None])
+    )(x, cotangent, w_gate, w_up, w_down, params, recur_weight, input_weight)
     return results[:5]
 
 
@@ -1443,7 +1536,7 @@
 ):
     seq_count = lax.axis_size("seq")
     sequences, span_len, width = block_input.shape
-    if seq_count % 8 or w_gate.shape[0] % 32:
+    if seq_count != 16 or w_gate.shape[0] % 32:
         return gathered_shards(
             block_input, norm_gain, conv_weight, conv_bias, recur_weight, recur_bias, input_weight, input_bias,
             decay_param, mlp_gain, w_gate, w_up, w_down, out_grad,

time: 652 us -> 581 us (0.89)
  Pallas kernels: 625 us -> 555 us
    pallas_call x1, Pallas kernels: 625 us -> 555 us  [block_pass(): pl.pallas_call(functools.partial(block_kernel, seq_count, sequences), out...]
    broadcast_in_dim x7 -> x1, local copies, waits for them, and re-layouts: 7.7 us -> 0.01 us  [block_pass(): jnp.zeros_like(conv_weight)]
where the time goes in v4:
time: 581 us; the launch traced here: 579 us
  Pallas kernels  555 us (96%)
  local copies, waits for them, and re-layouts  17.4 us (3%)
    pallas_call x1, Pallas kernels, block_pass(): pl.pallas_call(functools.partial(block_kernel, seq_count, sequences), out...  555 us

profile of v4, /device:TPU:0, one launch (start us, length us, event | category | flops | bytes accessed | tf_op | source)
XLA Modules:
  0.0 579.3 jit_solution(1395800426117527386)
XLA Ops:
  0.6 0.7 stack.27
  1.4 0.7 stack.28
  2.1 0.7 stack.29
  2.8 0.8 dynamic_slice.6
  3.5 0.8 dynamic_slice.7
  4.3 0.7 add_divide_fusion
  5.1 2.0 concatenate.3.prm_ref
  7.1 554.8 %block_pass.1 = (bf16[512,2560]{1,0:T(8,128)(2,1)}, f32[512,2560]{1,0:T(8,128)}, bf16[3,160,3840]{2,1,0:T(8,128)(2,1)}, f32[16,1280]{1,0:T(8,128)}, bf16[2560,25...) custom-call(bf16[512,2560]{1,0:T(8,128)(2,1)} %bitcast.21, ...), custom_call_target="tpu_custom_call" | custom-call | flops 96636764160 | bytes 157286400 | tf_op jit(solution)/shard_map/block_pass/pallas_call | solution.py:1280
  562.0 1.4 slice.47
  563.4 1.6 slice_reduce_fusion.2
  565.0 1.8 all_gather.3
  566.8 0.7 slice_reduce_fusion
  567.4 0.0 copy-start
  567.4 0.0 slice-start
  567.4 3.1 fusion
  570.6 0.0 copy-done
  570.6 0.0 copy-start.1
  570.6 0.0 slice-start.1
  570.6 3.8 bitcast_convert_fusion
  574.4 1.0 copy-done.1
  575.4 1.5 copy.30
  576.9 0.0 slice-done
  576.9 0.0 slice-done.1
  576.9 2.4 copy.31
  (7 shorter events, 0.0 us)
Async XLA Ops:
  567.4 3.1 copy-start
  567.4 9.5 %slice-start = ((s8[5242880]{0:T(1024)(128)(4,1)}), s8[4194304]{0:T(1024)(128)(4,1)S(1)}, s32[]{:S(2)}) async-start(s8[5242880]{0:T(1024)(128)(4,1)} %bitcast.15), calls=%async_computation | async-start | bytes 8388608
  570.6 4.8 copy-start.1
  570.6 6.3 %slice-start.1 = ((s8[5242880]{0:T(1024)(128)(4,1)}), s8[1048576]{0:T(1024)(128)(4,1)S(1)}, s32[]{:S(2)}) async-start(s8[5242880]{0:T(1024)(128)(4,1)} %bitcast.15), calls=%async_computation.1 | async-start | bytes 2097152

commit v5 on v4

--- a/solution.py
+++ b/solution.py
@@ -1100,6 +1100,7 @@
                 vec_ref[pl.ds(1 + k, 1), lanes] = total
 
         far_finish(1, *far_slots[1])
+        near_first(3, 1)
 
         @pl.when(s + 1 < seq_count)
         def _():
@@ -1121,7 +1122,6 @@
                     total = total + cw_ref[pl.ds(k, 1), lanes] * gconv[q, pl.ds(k, length), lanes]
                 adj[pl.ds(q * length, length), lanes] = total
 
-        near_first(3, 1)
         near_last(3, 1)
 
         def own_rows(i):
@@ -1152,13 +1152,13 @@
         away = remote(fin, ingrad_ref.at[:, mine], fin_s.at[0], fin_r.at[0], s, 1 - h)
         away.start()
         near_first(3, 0)
+        near_last(3, 0)
+        far_issue(2, *far_slots[2])
         matrices_across()
-        near_last(3, 0)
+        far_finish(2, *far_slots[2])
         vectors_sum(0)
         vectors_start(1)
-        far_issue(2, *far_slots[2])
         near_send(3, 0, near_slots[3, 0][0])
-        far_finish(2, *far_slots[2])
         matrices_spread()
 
         res = pltpu.make_async_copy(res_keep, rg, keep.at[4])

time: 581 us -> 579 us (level)
  no operation moved by 1% of the time
where the time goes in v5:
time: 579 us; the launch traced here: 577 us
  Pallas kernels  553 us (96%)
  local copies, waits for them, and re-layouts  17.4 us (3%)
    pallas_call x1, Pallas kernels, block_pass(): pl.pallas_call(functools.partial(block_kernel, seq_count, sequences), out...  553 us

profile of v5, /device:TPU:0, one launch (start us, length us, event | category | flops | bytes accessed | tf_op | source)
XLA Modules:
  0.0 577.4 jit_solution(16295277916379480695)
XLA Ops:
  0.6 0.7 stack.27
  1.4 0.7 stack.28
  2.1 0.7 stack.29
  2.8 0.8 dynamic_slice.6
  3.5 0.8 dynamic_slice.7
  4.3 0.7 add_divide_fusion
  5.1 2.0 concatenate.3.prm_ref
  7.1 553.0 %block_pass.1 = (bf16[512,2560]{1,0:T(8,128)(2,1)}, f32[512,2560]{1,0:T(8,128)}, bf16[3,160,3840]{2,1,0:T(8,128)(2,1)}, f32[16,1280]{1,0:T(8,128)}, bf16[2560,25...) custom-call(bf16[512,2560]{1,0:T(8,128)(2,1)} %bitcast.21, ...), custom_call_target="tpu_custom_call" | custom-call | flops 96636764160 | bytes 157286400 | tf_op jit(solution)/shard_map/block_pass/pallas_call | solution.py:1280
  560.1 1.4 slice.47
  561.5 1.6 slice_reduce_fusion.2
  563.1 1.8 all_gather.3
  564.9 0.7 slice_reduce_fusion
  565.6 0.0 copy-start
  565.6 0.0 slice-start
  565.6 3.1 fusion
  568.7 0.0 copy-done
  568.7 0.0 copy-start.1
  568.7 0.0 slice-start.1
  568.7 3.8 bitcast_convert_fusion
  572.5 1.0 copy-done.1
  573.5 1.5 copy.30
  575.0 0.0 slice-done
  575.0 0.0 slice-done.1
  575.0 2.4 copy.31
  (7 shorter events, 0.0 us)
Async XLA Ops:
  565.6 3.1 copy-start
  565.6 9.5 %slice-start = ((s8[5242880]{0:T(1024)(128)(4,1)}), s8[4194304]{0:T(1024)(128)(4,1)S(1)}, s32[]{:S(2)}) async-start(s8[5242880]{0:T(1024)(128)(4,1)} %bitcast.15), calls=%async_computation | async-start | bytes 8388608
  568.7 4.8 copy-start.1
  568.7 6.3 %slice-start.1 = ((s8[5242880]{0:T(1024)(128)(4,1)}), s8[1048576]{0:T(1024)(128)(4,1)S(1)}, s32[]{:S(2)}) async-start(s8[5242880]{0:T(1024)(128)(4,1)} %bitcast.15), calls=%async_computation.1 | async-start | bytes 2097152
